TPU v7x, 128 devices: a whole 4x4x4 slice. The times are simulated.
128 devices in a mesh: blk: 64 (over z, x, y), col: 2 (over core).
Axes of the slice: x: 4, y: 4, z: 4, core: 2. Of those that a mesh axis runs over, the one named last changes fastest.
Arguments:
- basis_rows: bfloat16 [65536, 4096], P('blk', 'col'), may hold values from -2 to 2
- screen: int32 [64, 4], P('blk'), may hold values from 0 to 1, as said below
Outputs:
- exchange_blocks: float32 [64, 5, 1024, 1024], P('blk', None, 'col')
Inputs may be any that keep to these rules, and one draw needn't show every extreme that they name: `screen`: entries are zero where a + k + 1 >= 64; block 0 keeps all its 4 partners.
All inputs are finite; a program needn't handle non-finite values.
Results may differ from a plain program's by a relative error of at most 0.0003.
Values may be sent and summed in bfloat16 or wider, within the bound.
No kernel may reach another device: no remote copies, remote signals or barrier semaphores. Data moves between devices by JAX's collectives and lax.ppermute only.
A program may use at most 128 MiB of HBM per device.

v0:
```python
import jax
import jax.numpy as jnp
from jax import lax
from jax.experimental import pallas as pl
from jax.experimental.pallas import tpu as pltpu
from jax.sharding import PartitionSpec as P

RING = 4
PARTS = 4
STRIP = 512
MIB = 1 << 20
SMALL = pl.CostEstimate(flops=1, bytes_accessed=1, transcendentals=0)
VMEM = pl.BlockSpec(memory_space=pltpu.VMEM)
SMEM = pl.BlockSpec(memory_space=pltpu.SMEM)
ANY = pl.BlockSpec(memory_space=pl.ANY)
HBM = pl.BlockSpec(memory_space=pltpu.HBM)
LIMIT = pltpu.CompilerParams(vmem_limit_bytes=12 * MIB)


def product(rows, partner):
    return lax.dot_general(
        rows, partner, (((1,), (1,)), ((), ())), preferred_element_type=jnp.float32
    )


def strips(height, run):
    @pl.loop(0, height // STRIP)
    def _(strip):
        run(pl.ds(pl.multiple_of(strip * STRIP, STRIP), STRIP))


def take_rows(after, own, first, count):
    def kernel(_, own_ref, taken_ref, sem):
        copy = pltpu.make_async_copy(own_ref.at[pl.ds(first, count), :], taken_ref, sem)
        copy.start()
        copy.wait()

    return pl.pallas_call(
        kernel,
        out_shape=jax.ShapeDtypeStruct((count, own.shape[1]), own.dtype),
        in_specs=[SMEM, HBM],
        out_specs=VMEM,
        scratch_shapes=[pltpu.SemaphoreType.DMA],
        compiler_params=LIMIT,
        cost_estimate=SMALL,
    )(after, own)


def columns(group, half):
    e, first = half // PARTS, 0
    for k, part in group:
        count = 2 * half if part is None else 2 * e
        yield k, count, first, [0] if part is None else [part * e, half + part * e]
        first += count


def width(group, half):
    return sum(count for _, count, _, _ in columns(group, half))


def spans(refs, count, e, run):
    if len(refs) > 1 or count == 2 * e:
        run(0, count, lambda: whole(refs))
        return

    @pl.loop(0, count // (2 * e))
    def _(index):
        at = pl.multiple_of(index * 2 * e, 2 * e)
        run(at, 2 * e, lambda: refs[0][pl.ds(at, 2 * e), :])


def whole(refs):
    return refs[0][...] if len(refs) == 1 else jnp.concatenate([ref[...] for ref in refs], axis=0)


def deal(refs, partners):
    refs = iter(refs)
    return [[next(refs) for _ in arrays] for arrays in partners]


def handed_products(handed, partners, group, before=None, total=None):
    half, many = handed.shape[0], sum(map(len, partners))
    size = width(group, half)
    room = total or size
    offset = 0 if before is None else room - size

    def kernel(handed_ref, *refs):
        made_ref = refs[-1]
        for (_, count, first, _), tile_refs in zip(columns(group, half), deal(refs, partners)):
            def span(column, columns, partner):
                def strip(at):
                    across = pl.ds(offset + first + column, columns)
                    made_ref[at, across] = product(handed_ref[at, :], partner())
                strips(half, strip)

            spans(tile_refs, count, half // PARTS, span)

    return pl.pallas_call(
        kernel,
        out_shape=jax.ShapeDtypeStruct((half, room), jnp.float32),
        in_specs=[VMEM] * (1 + many) + [VMEM] * (before is not None),
        out_specs=VMEM,
        input_output_aliases={} if before is None else {1 + many: 0},
        compiler_params=LIMIT,
        cost_estimate=SMALL,
    )(handed, *sum(partners, []), *([] if before is None else [before]))


def kept_products(out, weights, kept, theirs, partners, groups):
    half, first_call = kept.shape[0], out is None
    many = sum(map(len, partners))

    def kernel(weights_ref, kept_ref, *refs):
        theirs_refs, refs = refs[:len(groups)], refs[len(groups):]
        partner_refs, refs = iter(deal(refs, partners)), refs[many:]
        out_ref, *made_refs, sems = refs if first_call else refs[1:]
        copies = []
        for group, theirs_ref, made_ref in zip(groups, theirs_refs, made_refs):
            for (k, count, first, runs), tile_refs in zip(columns(group, half), partner_refs):
                def span(column, columns, partner):
                    def strip(at):
                        across = pl.ds(first + column, columns)
                        total = product(kept_ref[at, :], partner()) + theirs_ref[at, across]
                        made_ref[at, across] = total * weights_ref[k]
                    strips(half, strip)

                spans(tile_refs, count, half // PARTS, span)
                for n, column in enumerate(runs):
                    run = count // len(runs)
                    copies.append(pltpu.make_async_copy(
                        made_ref.at[:, pl.ds(first + n * run, run)],
                        out_ref.at[k, :, pl.ds(column, run)],
                        sems.at[len(copies)],
                    ))
                    copies[-1].start()
        for copy in copies:
            copy.wait()

    inputs = len(groups) + many
    return pl.pallas_call(
        kernel,
        out_shape=jax.ShapeDtypeStruct((5, half, 2 * half), jnp.float32),
        in_specs=[SMEM] + [VMEM] * (1 + inputs) + [ANY] * (not first_call),
        out_specs=ANY,
        scratch_shapes=[pltpu.VMEM((half, width(group, half)), jnp.float32) for group in groups]
        + [pltpu.SemaphoreType.DMA((2 * sum(map(len, groups)),))],
        input_output_aliases={} if first_call else {2 + inputs: 0},
        compiler_params=LIMIT,
        cost_estimate=SMALL,
    )(weights, kept, *theirs, *sum(partners, []), *([] if first_call else [out]))


def relayed_products(where, rows, partners, blocks, theirs=()):
    e, sums = rows[0][0].shape[0], len(theirs) > 0
    used = sorted({j for parts, *_ in blocks for j in parts})
    sizes = {}
    for parts, _, *places in blocks:
        array, first, *starts = places[sums]
        height, size = sizes.get(array, (0, 0))
        sizes[array] = max(height, first + len(parts) * e), max(size, *(c + e for c in starts))

    def kernel(where_ref, *refs):
        row_refs, refs = deal(refs, rows), refs[2 * len(rows):]
        partner_refs, refs = deal(refs, partners), refs[2 * len(partners):]
        theirs_refs, (*made_refs, taken_ref) = refs[:len(theirs)], refs[len(theirs):]

        def take(kept):
            for n, j in enumerate(used):
                taken_ref[pl.ds(n * e, e), :] = row_refs[j][kept][...]

        for core in range(2):
            pl.when(where_ref[0] == core)(lambda core=core: take(core if sums else 1 - core))

        for parts, partner, *places in blocks:
            taken = taken_ref[pl.ds(used.index(parts[0]) * e, len(parts) * e), :]
            made = product(taken, whole(partner_refs[partner]))
            for n in range(2):
                piece = made[:, n * e:(n + 1) * e]
                if sums:
                    array, first, *starts = places[0]
                    piece += theirs_refs[array][pl.ds(first, len(parts) * e), pl.ds(starts[n], e)]
                array, first, *starts = places[sums]
                made_refs[array][pl.ds(first, len(parts) * e), pl.ds(starts[n], e)] = piece

    operands = sum([*rows, *partners], []) + list(theirs)
    return pl.pallas_call(
        kernel,
        out_shape=[jax.ShapeDtypeStruct(sizes[n], jnp.float32) for n in sorted(sizes)],
        in_specs=[SMEM] + [VMEM] * len(operands),
        out_specs=[VMEM] * len(sizes),
        scratch_shapes=[pltpu.VMEM((len(used) * e, rows[0][0].shape[1]), rows[0][0].dtype)],
        compiler_params=LIMIT,
        cost_estimate=SMALL,
    )(where, *operands)


def scaled_write(out, weights, made, k, regions):
    def kernel(weights_ref, summed_ref, _, out_ref, made_ref, sems):
        made_ref[...] = summed_ref[...] * weights_ref[k]
        copies = [
            pltpu.make_async_copy(
                made_ref.at[pl.ds(row, height), pl.ds(column, size)],
                out_ref.at[k, pl.ds(to_row, height), pl.ds(to_column, size)],
                sems.at[n],
            )
            for n, (row, column, height, size, to_row, to_column) in enumerate(regions)
        ]
        for copy in copies:
            copy.start()
        for copy in copies:
            copy.wait()

    return pl.pallas_call(
        kernel,
        out_shape=jax.ShapeDtypeStruct(out.shape, jnp.float32),
        in_specs=[SMEM, VMEM, ANY],
        out_specs=ANY,
        scratch_shapes=[
            pltpu.VMEM(made.shape, jnp.float32), pltpu.SemaphoreType.DMA((len(regions),))
        ],
        input_output_aliases={2: 0},
        compiler_params=LIMIT,
        cost_estimate=SMALL,
    )(weights, made, out)


def body(basis_rows, screen):
    blocks = lax.axis_size("blk")
    half = basis_rows.shape[0] // 2
    e = half // PARTS
    column = lax.axis_index("blk") % RING
    core = lax.axis_index("col")
    weights = jnp.concatenate([jnp.ones((1,), jnp.float32), screen[0].astype(jnp.float32)])

    def below(distance):
        return [(i, (i - distance) % blocks) for i in range(blocks)]

    def around(distance):
        return [(i, i - i % RING + (i + distance) % RING) for i in range(blocks)]

    def swap(array):
        return lax.ppermute(array, "col", [(0, 1), (1, 0)])

    s = dict(where=core.astype(jnp.int32)[None], held={}, made={}, out=None)

    def fence(*arrived):
        s["held"].update(arrived)
        s.update(lax.optimization_barrier(s))

    def mine(p):
        first = p % 2 * half + p // 2 * e
        s["held"][0, p] = take_rows(s["where"], basis_rows, first, e)

    def fetch4(p):
        return (4, p), lax.ppermute(s["held"][0, p], "blk", below(4))

    def fetch1(p):
        send = jnp.where(column == 0, s["held"][4, p], s["held"][0, p])
        return (1, p), lax.ppermute(send, "blk", around(-1))

    def fetch3(p):
        send = jnp.where(column == RING - 1, s["held"][0, p], s["held"][4, p])
        return (3, p), lax.ppermute(send, "blk", around(1))

    def part(k, j):
        if j is None:
            return [basis_rows]
        return [s["relayed"]] if k == 2 else [s["held"][k, 2 * j], s["held"][k, 2 * j + 1]]

    def partners(*groups):
        return [part(k, j) for group in groups for k, j in group]

    def make(group, new=(), total=None):
        s["made"][group] = handed_products(
            s["handed"], partners(new or group), new or group, s["made"].get(group), total
        )

    def finish(*groups):
        theirs = [swap(s["made"].pop(group)) for group in groups]
        s["out"] = kept_products(s["out"], weights, s["kept"], theirs, partners(*groups), groups)

    own, ones = ((0, None),), ((4, 0), (4, 1), (1, 0), (3, 0))
    twos, threes = ((4, 2), (1, 1), (3, 1)), ((4, 3), (1, 2), (3, 2))
    first, second = own + ones, twos + threes

    mine(0)
    fence()
    mine(1)
    s["kept"] = lax.dynamic_slice_in_dim(basis_rows, core * half, half, 0)
    s["handed"] = lax.dynamic_slice_in_dim(basis_rows, (1 - core) * half, half, 0)
    pieces = 2 * PARTS
    x = [fetch4(0), fetch4(1)]
    fence(x[0])
    d, u = [fetch1(0)], [fetch3(0)]
    for p in range(pieces - 1):
        if p + 2 < pieces:
            mine(p + 2)
            x.append(fetch4(p + 2))
        if p == 1:
            make(first, own, width(first, half))
        if p == 3:
            make(first, ones, width(first, half))
        if p == 5:
            make(second, twos, width(second, half))
        fence(x[p + 1])
        d.append(fetch1(p + 1))
        u.append(fetch3(p + 1))
        fence(d[p], u[p])

    make(second, threes, width(second, half))
    some = (0, 1, 2)
    early = [(some, n, (n, 0, 0, e), (0, 0, n * e, (2 + n) * e)) for n in range(2)]
    late = [((3,), n) + 2 * ((0, 0, n * e, (3 + n) * e),) for n in range(3)]
    late += [((j,), 2) + 2 * ((0, e, 2 * j * e, (2 * j + 1) * e),) for j in some]

    def ahead(blocks):
        rows = [part(1, j) for j in range(1 + max(max(parts) for parts, *_ in blocks))]
        others = [part(3, j) for j in range(1 + max(n for _, n, *_ in blocks))]
        theirs = [swap(array) for array in relayed_products(s["where"], rows, others, blocks)]
        return relayed_products(s["where"], rows, others, blocks, theirs)[0]

    s["ahead"] = ahead(early)
    fence(d[-1], u[-1])

    first_sums = lax.ppermute(s["ahead"], "blk", below(-1))
    relayed = lax.ppermute(jnp.concatenate(part(1, 3)), "blk", below(1))
    last_sums = lax.ppermute(ahead(late), "blk", below(-1))
    third, fourth, fifth = ((1, 3),), ((3, 3),), ((2, 3),)
    make(third)
    make(fourth)
    finish(first)
    finish(second)
    s["sums"], s["relayed"] = first_sums, relayed
    fence()

    make(fifth)
    finish(third, fourth, fifth)
    regions = [(0, n * 2 * e, 3 * e, 2 * e, 0, n * half) for n in range(2)]
    out = scaled_write(s["out"], weights, s["sums"], 2, regions)
    regions = [(0, n * 3 * e, e, 3 * e, 3 * e, n * half) for n in range(2)]
    regions += [(e, (2 * j + n) * e, e, e, j * e, n * half + 2 * e) for j in some for n in range(2)]
    out = scaled_write(out, weights, last_sums, 2, regions)
    return out[None]


def solution(mesh):
    return jax.shard_map(
        body,
        mesh=mesh,
        in_specs=(P("blk", "col"), P("blk", None)),
        out_specs=P("blk", None, "col", None),
        check_vma=False,
    )
```

profile of v0, /device:TPU:1, one launch (start us, length us, event | category | flops | bytes accessed | tf_op | source)
XLA Modules:
  0.0 170.0 jit_solution(6125709465891636751)
XLA Ops:
  3.0 6.8 %collective-permute-start = (bf16[128,2048]{1,0:T(8,128)(2,1)}, bf16[128,2048]{1,0:T(8,128)(2,1)S(1)}, u32[]{:S(2)}, u32[]{:S(2)}) collective-permute-start(bf16[128,2048]{1,0:T(8,128)(2,1)} %shard_map.28), channel_id=1, source_target_pairs={{0,120},{2,122},{4,124},{6,126},{8,0},{10,2},{12,4},{14,6},{16,8},... | collective-permute-start | bytes 1572872 | tf_op jit(solution)/shard_map/ppermute | solution.py:255
  11.4 4.0 %constant_dynamic-slice_fusion = (bf16[512,2048]{1,0:T(8,128)(2,1)}, bf16[512,2048]{1,0:T(8,128)(2,1)S(1)}) fusion(bf16[1024,2048]{1,0:T(8,128)(2,1)} %refs_1_.1, s32[]{:T(128)S(6)} %select_n.84, s32[]{:T(128)S(6)} %select_n.83), kind=kLoop, calls=%fused_computation.18 | loop fusion | bytes 8388616 | tf_op jit(solution)/shard_map/dynamic_slice | solution.py:289
  15.4 5.4 %collective-permute-done.refs_0_.refs_2_ = bf16[128,2048]{1,0:T(8,128)(2,1)S(1)} collective-permute-done((bf16[128,2048]{1,0:T(8,128)(2,1)}, bf16[128,2048]{1,0:T(8,128)(2,1)S(1)}, u32[]{:S(2)}, u32[]{:S(2)}) %collective-permute-start) | collective-permute-done | bytes 524320 | tf_op jit(solution)/shard_map/ppermute | solution.py:255
  21.9 2.8 %collective-permute-start.2 = (bf16[128,2048]{1,0:T(8,128)(2,1)S(1)}, bf16[128,2048]{1,0:T(8,128)(2,1)S(1)}, u32[]{:S(2)}, u32[]{:S(2)}) collective-permute-start(bf16[128,2048]{1,0:T(8,128)(2,1)S(1)} %get-tuple-element.616), channel_id=1, source_target_pairs={{0,6},{2,0},{4,2},{6,4},{8,14},{10,8},{12,10},{14,12},{16,22},{18,... | collective-permute-start | bytes 1572872 | tf_op jit(solution)/shard_map/ppermute | solution.py:259
  27.0 5.5 %collective-permute-start.4 = (bf16[128,2048]{1,0:T(8,128)(2,1)S(1)}, bf16[128,2048]{1,0:T(8,128)(2,1)S(1)}, u32[]{:S(2)}, u32[]{:S(2)}) collective-permute-start(bf16[128,2048]{1,0:T(8,128)(2,1)S(1)} %shard_map.30), channel_id=1, source_target_pairs={{0,120},{2,122},{4,124},{6,126},{8,0},{10,2},{12,4},{14,6},{16,8},... | collective-permute-start | bytes 1572872 | tf_op jit(solution)/shard_map/ppermute | solution.py:255
  33.6 2.7 %collective-permute-start.5 = (bf16[128,2048]{1,0:T(8,128)(2,1)S(1)}, bf16[128,2048]{1,0:T(8,128)(2,1)S(1)}, u32[]{:S(2)}, u32[]{:S(2)}) collective-permute-start(bf16[128,2048]{1,0:T(8,128)(2,1)S(1)} %get-tuple-element.614), channel_id=1, source_target_pairs={{0,6},{2,0},{4,2},{6,4},{8,14},{10,8},{12,10},{14,12},{16,22},{18,... | collective-permute-start | bytes 1572872 | tf_op jit(solution)/shard_map/ppermute | solution.py:259
  36.4 5.5 %collective-permute-start.7 = (bf16[128,2048]{1,0:T(8,128)(2,1)S(1)}, bf16[128,2048]{1,0:T(8,128)(2,1)S(1)}, u32[]{:S(2)}, u32[]{:S(2)}) collective-permute-start(bf16[128,2048]{1,0:T(8,128)(2,1)S(1)} %shard_map.31), channel_id=1, source_target_pairs={{0,120},{2,122},{4,124},{6,126},{8,0},{10,2},{12,4},{14,6},{16,8},... | collective-permute-start | bytes 1572872 | tf_op jit(solution)/shard_map/ppermute | solution.py:255
  41.9 3.0 %shard_map.32.refs_8_ = f32[512,2048]{1,0:T(8,128)S(1)} custom-call(bf16[512,2048]{1,0:T(8,128)(2,1)S(1)} %get-tuple-element.592.handed_ref, bf16[1024,2048]{1,0:T(8,128)(2,1)S(1)} %copy-done.2), custom_call_target="tpu_custom_call" | custom-call | flops 1 | bytes 1 | tf_op jit(solution)/shard_map/pallas_call | solution.py:98
  47.4 6.8 %collective-permute-start.10 = (bf16[128,2048]{1,0:T(8,128)(2,1)S(1)}, bf16[128,2048]{1,0:T(8,128)(2,1)S(1)}, u32[]{:S(2)}, u32[]{:S(2)}) collective-permute-start(bf16[128,2048]{1,0:T(8,128)(2,1)S(1)} %shard_map.33), channel_id=1, source_target_pairs={{0,120},{2,122},{4,124},{6,126},{8,0},{10,2},{12,4},{14,6},{16,8},... | collective-permute-start | bytes 1572872 | tf_op jit(solution)/shard_map/ppermute | solution.py:255
  56.4 3.1 %collective-permute-done.9.refs_4_.refs_8_.refs_10_.refs_5_ = bf16[128,2048]{1,0:T(8,128)(2,1)S(1)} collective-permute-done((bf16[128,2048]{1,0:T(8,128)(2,1)S(1)}, bf16[128,2048]{1,0:T(8,128)(2,1)S(1)}, u32[]{:S(2)}, u32[]{:S(2)}) %collective-permute-start.9) | collective-permute-done | bytes 524320 | tf_op jit(solution)/shard_map/ppermute | solution.py:263
  59.6 4.7 %collective-permute-start.13 = (bf16[128,2048]{1,0:T(8,128)(2,1)S(1)}, bf16[128,2048]{1,0:T(8,128)(2,1)S(1)}, u32[]{:S(2)}, u32[]{:S(2)}) collective-permute-start(bf16[128,2048]{1,0:T(8,128)(2,1)S(1)} %shard_map.34), channel_id=1, source_target_pairs={{0,120},{2,122},{4,124},{6,126},{8,0},{10,2},{12,4},{14,6},{16,8},... | collective-permute-start | bytes 1572872 | tf_op jit(solution)/shard_map/ppermute | solution.py:255
  64.3 2.4 %shard_map.35 = f32[512,2048]{1,0:T(8,128)S(1)} custom-call(bf16[512,2048]{1,0:T(8,128)(2,1)S(1)} %get-tuple-element.592.handed_ref, bf16[128,2048]{1,0:T(8,128)(2,1)S(1)} %collective-permute-done.refs_0_.refs_2_, bf16[128,2048]{1,0:T(8,128)(2,1)S(1)} %collective-permute-done.1.refs_1_.refs_3_, ...), custom_call_target="tpu_custom_call", output_to_operand_aliasing={{}: (9, {})} | custom-call | flops 1 | bytes 1 | tf_op jit(solution)/shard_map/pallas_call | solution.py:98
  68.3 2.5 %collective-permute-done.12.refs_5_.refs_9_.refs_11_.refs_6_ = bf16[128,2048]{1,0:T(8,128)(2,1)S(1)} collective-permute-done((bf16[128,2048]{1,0:T(8,128)(2,1)S(1)}, bf16[128,2048]{1,0:T(8,128)(2,1)S(1)}, u32[]{:S(2)}, u32[]{:S(2)}) %collective-permute-start.12) | collective-permute-done | bytes 524320 | tf_op jit(solution)/shard_map/ppermute | solution.py:263
  70.9 4.7 %collective-permute-start.16 = (bf16[128,2048]{1,0:T(8,128)(2,1)S(1)}, bf16[128,2048]{1,0:T(8,128)(2,1)S(1)}, u32[]{:S(2)}, u32[]{:S(2)}) collective-permute-start(bf16[128,2048]{1,0:T(8,128)(2,1)S(1)} %shard_map.36), channel_id=1, source_target_pairs={{0,120},{2,122},{4,124},{6,126},{8,0},{10,2},{12,4},{14,6},{16,8},... | collective-permute-start | bytes 1572872 | tf_op jit(solution)/shard_map/ppermute | solution.py:255
  75.6 3.0 %collective-permute-start.17 = (bf16[128,2048]{1,0:T(8,128)(2,1)S(1)}, bf16[128,2048]{1,0:T(8,128)(2,1)S(1)}, u32[]{:S(2)}, u32[]{:S(2)}) collective-permute-start(bf16[128,2048]{1,0:T(8,128)(2,1)S(1)} %get-tuple-element.606), channel_id=1, source_target_pairs={{0,6},{2,0},{4,2},{6,4},{8,14},{10,8},{12,10},{14,12},{16,22},{18,... | collective-permute-start | bytes 1572872 | tf_op jit(solution)/shard_map/ppermute | solution.py:259
  78.6 2.6 %collective-permute-done.15.refs_4_.refs_12_.refs_11_ = bf16[128,2048]{1,0:T(8,128)(2,1)S(1)} collective-permute-done((bf16[128,2048]{1,0:T(8,128)(2,1)S(1)}, bf16[128,2048]{1,0:T(8,128)(2,1)S(1)}, u32[]{:S(2)}, u32[]{:S(2)}) %collective-permute-start.15) | collective-permute-done | bytes 524320 | tf_op jit(solution)/shard_map/ppermute | solution.py:263
  81.2 5.7 %collective-permute-start.19 = (bf16[128,2048]{1,0:T(8,128)(2,1)S(1)}, bf16[128,2048]{1,0:T(8,128)(2,1)S(1)}, u32[]{:S(2)}, u32[]{:S(2)}) collective-permute-start(bf16[128,2048]{1,0:T(8,128)(2,1)S(1)} %shard_map.37), channel_id=1, source_target_pairs={{0,120},{2,122},{4,124},{6,126},{8,0},{10,2},{12,4},{14,6},{16,8},... | collective-permute-start | bytes 1572872 | tf_op jit(solution)/shard_map/ppermute | solution.py:255
  90.4 2.9 %collective-permute-done.18.refs_5_.refs_13_.refs_12_ = bf16[128,2048]{1,0:T(8,128)(2,1)S(1)} collective-permute-done((bf16[128,2048]{1,0:T(8,128)(2,1)S(1)}, bf16[128,2048]{1,0:T(8,128)(2,1)S(1)}, u32[]{:S(2)}, u32[]{:S(2)}) %collective-permute-start.18) | collective-permute-done | bytes 524320 | tf_op jit(solution)/shard_map/ppermute | solution.py:263
  93.3 2.4 %collective-permute-done.19.refs_1_.refs_8_ = bf16[128,2048]{1,0:T(8,128)(2,1)S(1)} collective-permute-done((bf16[128,2048]{1,0:T(8,128)(2,1)S(1)}, bf16[128,2048]{1,0:T(8,128)(2,1)S(1)}, u32[]{:S(2)}, u32[]{:S(2)}) %collective-permute-start.19) | collective-permute-done | bytes 524320 | tf_op jit(solution)/shard_map/ppermute | solution.py:255
  95.8 5.3 %collective-permute-start.24 = (bf16[128,2048]{1,0:T(8,128)(2,1)S(1)}, bf16[128,2048]{1,0:T(8,128)(2,1)S(1)}, u32[]{:S(2)}, u32[]{:S(2)}) collective-permute-start(bf16[128,2048]{1,0:T(8,128)(2,1)S(1)} %get-tuple-element.602), channel_id=1, source_target_pairs={{0,6},{2,0},{4,2},{6,4},{8,14},{10,8},{12,10},{14,12},{16,22},{18,... | collective-permute-start | bytes 1572872 | tf_op jit(solution)/shard_map/ppermute | solution.py:259
  101.1 2.9 %collective-permute-done.21.refs_0_.refs_5_ = bf16[128,2048]{1,0:T(8,128)(2,1)S(1)} collective-permute-done((bf16[128,2048]{1,0:T(8,128)(2,1)S(1)}, bf16[128,2048]{1,0:T(8,128)(2,1)S(1)}, u32[]{:S(2)}, u32[]{:S(2)}) %collective-permute-start.21) | collective-permute-done | bytes 524320 | tf_op jit(solution)/shard_map/ppermute | solution.py:263
  105.1 6.7 %collective-permute-start.22 = (f32[384,256]{1,0:T(8,128)S(1)}, f32[384,256]{1,0:T(8,128)S(1)}, u32[]{:S(2)}, u32[]{:S(2)}) collective-permute-start(f32[384,256]{1,0:T(8,128)S(1)} %get-tuple-element.540), channel_id=1, source_target_pairs={{0,1},{1,0},{2,3},{3,2},{4,5},{5,4},{6,7},{7,6},{8,9},{9,8},{10,11... | collective-permute-start | bytes 1179656 | tf_op jit(solution)/shard_map/ppermute | solution.py:242
  116.3 3.0 %collective-permute-start.29 = (f32[512,2048]{1,0:T(8,128)S(1)}, f32[512,2048]{1,0:T(8,128)S(1)}, u32[]{:S(2)}, u32[]{:S(2)}) collective-permute-start(f32[512,2048]{1,0:T(8,128)S(1)} %shard_map.35), channel_id=1, source_target_pairs={{0,1},{1,0},{2,3},{3,2},{4,5},{5,4},{6,7},{7,6},{8,9},{9,8},{10,11... | collective-permute-start | bytes 12582920 | tf_op jit(solution)/shard_map/ppermute | solution.py:242
  119.3 2.3 %shard_map.42 = f32[256,768]{1,0:T(8,128)S(1)} custom-call(s32[1]{0:T(128)} %bitcast.1._.where_ref, bf16[128,2048]{1,0:T(8,128)(2,1)S(1)} %collective-permute-done.2.refs_4_.refs_0_.refs_6_, bf16[128,2048]{1,0:T(8,128)(2,1)S(1)} %collective-permute-done.5.refs_5_.refs_1_.refs_7_, bf16[128,2048]{1,0:T(8,128)(2,1)S(1)} %collective-permute-done.8.refs_2_.refs_3_, ...), custom_call_target="tpu_custom_call" | custom-call | flops 1 | bytes 1 | tf_op jit(solution)/shard_map/pallas_call | solution.py:186
  122.3 4.8 %collective-permute-start.30 = (bf16[256,2048]{1,0:T(8,128)(2,1)S(1)}, bf16[256,2048]{1,0:T(8,128)(2,1)S(1)}, u32[]{:S(2)}, u32[]{:S(2)}) collective-permute-start(bf16[256,2048]{1,0:T(8,128)(2,1)S(1)} %pad_maximum_fusion), channel_id=1, source_target_pairs={{0,126},{2,0},{4,2},{6,4},{8,6},{10,8},{12,10},{14,12},{16,14},{18... | collective-permute-start | bytes 3145736 | tf_op jit(solution)/shard_map/ppermute | solution.py:326
  127.2 4.5 %collective-permute-done.26.refs_14_ = f32[256,768]{1,0:T(8,128)S(1)} collective-permute-done((f32[256,768]{1,0:T(8,128)S(1)}, f32[256,768]{1,0:T(8,128)S(1)}, u32[]{:S(2)}, u32[]{:S(2)}) %collective-permute-start.26) | collective-permute-done | bytes 786464 | tf_op jit(solution)/shard_map/ppermute | solution.py:242
  131.7 2.3 %shard_map.43 = f32[256,768]{1,0:T(8,128)S(1)} custom-call(s32[1]{0:T(128)} %bitcast.1._.where_ref, bf16[128,2048]{1,0:T(8,128)(2,1)S(1)} %collective-permute-done.2.refs_4_.refs_0_.refs_6_, bf16[128,2048]{1,0:T(8,128)(2,1)S(1)} %collective-permute-done.5.refs_5_.refs_1_.refs_7_, bf16[128,2048]{1,0:T(8,128)(2,1)S(1)} %collective-permute-done.8.refs_2_.refs_3_, ...), custom_call_target="tpu_custom_call" | custom-call | flops 1 | bytes 1 | tf_op jit(solution)/shard_map/pallas_call | solution.py:186
  136.0 7.1 %shard_map.46.refs_13_ = f32[5,512,1024]{2,1,0:T(8,128)} custom-call(f32[5]{0:T(128)S(1)} %pad_maximum_fusion.1.weights_ref, bf16[512,2048]{1,0:T(8,128)(2,1)S(1)} %copy-done.3, f32[512,2048]{1,0:T(8,128)S(1)} %collective-permute-done.29.refs_0_, bf16[1024,2048]{1,0:T(8,128)(2,1)S(1)} %copy-done.2, ...), custom_call_target="tpu_custom_call" | custom-call | flops 1 | bytes 1 | tf_op jit(solution)/shard_map/pallas_call | solution.py:140
  143.1 5.2 %shard_map.47.refs_8_ = f32[5,512,1024]{2,1,0:T(8,128)} custom-call(f32[5]{0:T(128)S(1)} %pad_maximum_fusion.1.weights_ref, bf16[512,2048]{1,0:T(8,128)(2,1)S(1)} %copy-done.3, f32[512,1536]{1,0:T(8,128)S(1)} %collective-permute-done.28.refs_0_, bf16[128,2048]{1,0:T(8,128)(2,1)S(1)} %collective-permute-done.10.refs_0_.refs_1_, ...), custom_call_target="tpu_custom_call", output_to_operand_aliasing={{}: (15, {})} | custom-call | flops 1 | bytes 1 | tf_op jit(solution)/shard_map/pallas_call | solution.py:140
  148.3 3.2 %collective-permute-done.31.summed_ref = f32[384,512]{1,0:T(8,128)S(1)} collective-permute-done((f32[384,512]{1,0:T(8,128)S(1)}, f32[384,512]{1,0:T(8,128)S(1)}, u32[]{:S(2)}, u32[]{:S(2)}) %collective-permute-start.31) | collective-permute-done | bytes 786464 | tf_op jit(solution)/shard_map/ppermute | solution.py:325
  157.2 3.4 %shard_map.49._ = f32[5,512,1024]{2,1,0:T(8,128)} custom-call(f32[5]{0:T(128)S(1)} %pad_maximum_fusion.1.weights_ref, bf16[512,2048]{1,0:T(8,128)(2,1)S(1)} %copy-done.3, f32[512,256]{1,0:T(8,128)S(1)} %collective-permute-done.32.refs_0_, f32[512,256]{1,0:T(8,128)S(1)} %collective-permute-done.33.refs_1_, ...), custom_call_target="tpu_custom_call", output_to_operand_aliasing={{}: (10, {})} | custom-call | flops 1 | bytes 1 | tf_op jit(solution)/shard_map/pallas_call | solution.py:140
  162.1 6.2 %collective-permute-done.27.summed_ref = f32[256,768]{1,0:T(8,128)S(1)} collective-permute-done((f32[256,768]{1,0:T(8,128)S(1)}, f32[256,768]{1,0:T(8,128)S(1)}, u32[]{:S(2)}, u32[]{:S(2)}) %collective-permute-start.27) | collective-permute-done | bytes 786464 | tf_op jit(solution)/shard_map/ppermute | solution.py:327
  (84 shorter events, 36.0 us)
Async XLA Ops:
  3.0 17.8 %collective-permute-start = (bf16[128,2048]{1,0:T(8,128)(2,1)}, bf16[128,2048]{1,0:T(8,128)(2,1)S(1)}, u32[]{:S(2)}, u32[]{:S(2)}) collective-permute-start(bf16[128,2048]{1,0:T(8,128)(2,1)} %shard_map.28), channel_id=1, source_target_pairs={{0,120},{2,122},{4,124},{6,126},{8,0},{10,2},{12,4},{14,6},{16,8},... | collective-permute-start | bytes 1572872 | tf_op jit(solution)/shard_map/ppermute | solution.py:255
  10.8 21.7 %collective-permute-start.1 = (bf16[128,2048]{1,0:T(8,128)(2,1)}, bf16[128,2048]{1,0:T(8,128)(2,1)S(1)}, u32[]{:S(2)}, u32[]{:S(2)}) collective-permute-start(bf16[128,2048]{1,0:T(8,128)(2,1)} %shard_map.29), channel_id=1, source_target_pairs={{0,120},{2,122},{4,124},{6,126},{8,0},{10,2},{12,4},{14,6},{16,8},... | collective-permute-start | bytes 1572872 | tf_op jit(solution)/shard_map/ppermute | solution.py:255
  21.9 14.4 %collective-permute-start.2 = (bf16[128,2048]{1,0:T(8,128)(2,1)S(1)}, bf16[128,2048]{1,0:T(8,128)(2,1)S(1)}, u32[]{:S(2)}, u32[]{:S(2)}) collective-permute-start(bf16[128,2048]{1,0:T(8,128)(2,1)S(1)} %get-tuple-element.616), channel_id=1, source_target_pairs={{0,6},{2,0},{4,2},{6,4},{8,14},{10,8},{12,10},{14,12},{16,22},{18,... | collective-permute-start | bytes 1572872 | tf_op jit(solution)/shard_map/ppermute | solution.py:259
  24.7 11.7 %collective-permute-start.3 = (bf16[128,2048]{1,0:T(8,128)(2,1)S(1)}, bf16[128,2048]{1,0:T(8,128)(2,1)S(1)}, u32[]{:S(2)}, u32[]{:S(2)}) collective-permute-start(bf16[128,2048]{1,0:T(8,128)(2,1)S(1)} %get-tuple-element.615), channel_id=1, source_target_pairs={{0,2},{2,4},{4,6},{6,0},{8,10},{10,12},{12,14},{14,8},{16,18},{18,... | collective-permute-start | bytes 1572872 | tf_op jit(solution)/shard_map/ppermute | solution.py:263
  27.0 17.9 %collective-permute-start.4 = (bf16[128,2048]{1,0:T(8,128)(2,1)S(1)}, bf16[128,2048]{1,0:T(8,128)(2,1)S(1)}, u32[]{:S(2)}, u32[]{:S(2)}) collective-permute-start(bf16[128,2048]{1,0:T(8,128)(2,1)S(1)} %shard_map.30), channel_id=1, source_target_pairs={{0,120},{2,122},{4,124},{6,126},{8,0},{10,2},{12,4},{14,6},{16,8},... | collective-permute-start | bytes 1572872 | tf_op jit(solution)/shard_map/ppermute | solution.py:255
  33.6 13.8 %collective-permute-start.5 = (bf16[128,2048]{1,0:T(8,128)(2,1)S(1)}, bf16[128,2048]{1,0:T(8,128)(2,1)S(1)}, u32[]{:S(2)}, u32[]{:S(2)}) collective-permute-start(bf16[128,2048]{1,0:T(8,128)(2,1)S(1)} %get-tuple-element.614), channel_id=1, source_target_pairs={{0,6},{2,0},{4,2},{6,4},{8,14},{10,8},{12,10},{14,12},{16,22},{18,... | collective-permute-start | bytes 1572872 | tf_op jit(solution)/shard_map/ppermute | solution.py:259
  36.3 11.0 %collective-permute-start.6 = (bf16[128,2048]{1,0:T(8,128)(2,1)S(1)}, bf16[128,2048]{1,0:T(8,128)(2,1)S(1)}, u32[]{:S(2)}, u32[]{:S(2)}) collective-permute-start(bf16[128,2048]{1,0:T(8,128)(2,1)S(1)} %get-tuple-element.613), channel_id=1, source_target_pairs={{0,2},{2,4},{4,6},{6,0},{8,10},{10,12},{12,14},{14,8},{16,18},{18,... | collective-permute-start | bytes 1572872 | tf_op jit(solution)/shard_map/ppermute | solution.py:263
  36.4 17.7 %collective-permute-start.7 = (bf16[128,2048]{1,0:T(8,128)(2,1)S(1)}, bf16[128,2048]{1,0:T(8,128)(2,1)S(1)}, u32[]{:S(2)}, u32[]{:S(2)}) collective-permute-start(bf16[128,2048]{1,0:T(8,128)(2,1)S(1)} %shard_map.31), channel_id=1, source_target_pairs={{0,120},{2,122},{4,124},{6,126},{8,0},{10,2},{12,4},{14,6},{16,8},... | collective-permute-start | bytes 1572872 | tf_op jit(solution)/shard_map/ppermute | solution.py:255
  45.0 11.4 %collective-permute-start.8 = (bf16[128,2048]{1,0:T(8,128)(2,1)S(1)}, bf16[128,2048]{1,0:T(8,128)(2,1)S(1)}, u32[]{:S(2)}, u32[]{:S(2)}) collective-permute-start(bf16[128,2048]{1,0:T(8,128)(2,1)S(1)} %get-tuple-element.612), channel_id=1, source_target_pairs={{0,6},{2,0},{4,2},{6,4},{8,14},{10,8},{12,10},{14,12},{16,22},{18,... | collective-permute-start | bytes 1572872 | tf_op jit(solution)/shard_map/ppermute | solution.py:259
  47.3 12.2 %collective-permute-start.9 = (bf16[128,2048]{1,0:T(8,128)(2,1)S(1)}, bf16[128,2048]{1,0:T(8,128)(2,1)S(1)}, u32[]{:S(2)}, u32[]{:S(2)}) collective-permute-start(bf16[128,2048]{1,0:T(8,128)(2,1)S(1)} %get-tuple-element.611), channel_id=1, source_target_pairs={{0,2},{2,4},{4,6},{6,0},{8,10},{10,12},{12,14},{14,8},{16,18},{18,... | collective-permute-start | bytes 1572872 | tf_op jit(solution)/shard_map/ppermute | solution.py:263
  47.4 19.2 %collective-permute-start.10 = (bf16[128,2048]{1,0:T(8,128)(2,1)S(1)}, bf16[128,2048]{1,0:T(8,128)(2,1)S(1)}, u32[]{:S(2)}, u32[]{:S(2)}) collective-permute-start(bf16[128,2048]{1,0:T(8,128)(2,1)S(1)} %shard_map.33), channel_id=1, source_target_pairs={{0,120},{2,122},{4,124},{6,126},{8,0},{10,2},{12,4},{14,6},{16,8},... | collective-permute-start | bytes 1572872 | tf_op jit(solution)/shard_map/ppermute | solution.py:255
  54.3 14.0 %collective-permute-start.11 = (bf16[128,2048]{1,0:T(8,128)(2,1)S(1)}, bf16[128,2048]{1,0:T(8,128)(2,1)S(1)}, u32[]{:S(2)}, u32[]{:S(2)}) collective-permute-start(bf16[128,2048]{1,0:T(8,128)(2,1)S(1)} %get-tuple-element.610), channel_id=1, source_target_pairs={{0,6},{2,0},{4,2},{6,4},{8,14},{10,8},{12,10},{14,12},{16,22},{18,... | collective-permute-start | bytes 1572872 | tf_op jit(solution)/shard_map/ppermute | solution.py:259
  56.1 14.7 %collective-permute-start.12 = (bf16[128,2048]{1,0:T(8,128)(2,1)S(1)}, bf16[128,2048]{1,0:T(8,128)(2,1)S(1)}, u32[]{:S(2)}, u32[]{:S(2)}) collective-permute-start(bf16[128,2048]{1,0:T(8,128)(2,1)S(1)} %get-tuple-element.609), channel_id=1, source_target_pairs={{0,2},{2,4},{4,6},{6,0},{8,10},{10,12},{12,14},{14,8},{16,18},{18,... | collective-permute-start | bytes 1572872 | tf_op jit(solution)/shard_map/ppermute | solution.py:263
  59.6 15.9 %collective-permute-start.13 = (bf16[128,2048]{1,0:T(8,128)(2,1)S(1)}, bf16[128,2048]{1,0:T(8,128)(2,1)S(1)}, u32[]{:S(2)}, u32[]{:S(2)}) collective-permute-start(bf16[128,2048]{1,0:T(8,128)(2,1)S(1)} %shard_map.34), channel_id=1, source_target_pairs={{0,120},{2,122},{4,124},{6,126},{8,0},{10,2},{12,4},{14,6},{16,8},... | collective-permute-start | bytes 1572872 | tf_op jit(solution)/shard_map/ppermute | solution.py:255
  66.7 11.9 %collective-permute-start.14 = (bf16[128,2048]{1,0:T(8,128)(2,1)S(1)}, bf16[128,2048]{1,0:T(8,128)(2,1)S(1)}, u32[]{:S(2)}, u32[]{:S(2)}) collective-permute-start(bf16[128,2048]{1,0:T(8,128)(2,1)S(1)} %get-tuple-element.608), channel_id=1, source_target_pairs={{0,6},{2,0},{4,2},{6,4},{8,14},{10,8},{12,10},{14,12},{16,22},{18,... | collective-permute-start | bytes 1572872 | tf_op jit(solution)/shard_map/ppermute | solution.py:259
  67.4 13.8 %collective-permute-start.15 = (bf16[128,2048]{1,0:T(8,128)(2,1)S(1)}, bf16[128,2048]{1,0:T(8,128)(2,1)S(1)}, u32[]{:S(2)}, u32[]{:S(2)}) collective-permute-start(bf16[128,2048]{1,0:T(8,128)(2,1)S(1)} %get-tuple-element.607), channel_id=1, source_target_pairs={{0,2},{2,4},{4,6},{6,0},{8,10},{10,12},{12,14},{14,8},{16,18},{18,... | collective-permute-start | bytes 1572872 | tf_op jit(solution)/shard_map/ppermute | solution.py:263
  70.9 17.9 %collective-permute-start.16 = (bf16[128,2048]{1,0:T(8,128)(2,1)S(1)}, bf16[128,2048]{1,0:T(8,128)(2,1)S(1)}, u32[]{:S(2)}, u32[]{:S(2)}) collective-permute-start(bf16[128,2048]{1,0:T(8,128)(2,1)S(1)} %shard_map.36), channel_id=1, source_target_pairs={{0,120},{2,122},{4,124},{6,126},{8,0},{10,2},{12,4},{14,6},{16,8},... | collective-permute-start | bytes 1572872 | tf_op jit(solution)/shard_map/ppermute | solution.py:255
  75.6 14.8 %collective-permute-start.17 = (bf16[128,2048]{1,0:T(8,128)(2,1)S(1)}, bf16[128,2048]{1,0:T(8,128)(2,1)S(1)}, u32[]{:S(2)}, u32[]{:S(2)}) collective-permute-start(bf16[128,2048]{1,0:T(8,128)(2,1)S(1)} %get-tuple-element.606), channel_id=1, source_target_pairs={{0,6},{2,0},{4,2},{6,4},{8,14},{10,8},{12,10},{14,12},{16,22},{18,... | collective-permute-start | bytes 1572872 | tf_op jit(solution)/shard_map/ppermute | solution.py:259
  78.6 14.7 %collective-permute-start.18 = (bf16[128,2048]{1,0:T(8,128)(2,1)S(1)}, bf16[128,2048]{1,0:T(8,128)(2,1)S(1)}, u32[]{:S(2)}, u32[]{:S(2)}) collective-permute-start(bf16[128,2048]{1,0:T(8,128)(2,1)S(1)} %get-tuple-element.605), channel_id=1, source_target_pairs={{0,2},{2,4},{4,6},{6,0},{8,10},{10,12},{12,14},{14,8},{16,18},{18,... | collective-permute-start | bytes 1572872 | tf_op jit(solution)/shard_map/ppermute | solution.py:263
  81.2 14.4 %collective-permute-start.19 = (bf16[128,2048]{1,0:T(8,128)(2,1)S(1)}, bf16[128,2048]{1,0:T(8,128)(2,1)S(1)}, u32[]{:S(2)}, u32[]{:S(2)}) collective-permute-start(bf16[128,2048]{1,0:T(8,128)(2,1)S(1)} %shard_map.37), channel_id=1, source_target_pairs={{0,120},{2,122},{4,124},{6,126},{8,0},{10,2},{12,4},{14,6},{16,8},... | collective-permute-start | bytes 1572872 | tf_op jit(solution)/shard_map/ppermute | solution.py:255
  88.9 12.2 %collective-permute-start.20 = (bf16[128,2048]{1,0:T(8,128)(2,1)S(1)}, bf16[128,2048]{1,0:T(8,128)(2,1)S(1)}, u32[]{:S(2)}, u32[]{:S(2)}) collective-permute-start(bf16[128,2048]{1,0:T(8,128)(2,1)S(1)} %get-tuple-element.604), channel_id=1, source_target_pairs={{0,6},{2,0},{4,2},{6,4},{8,14},{10,8},{12,10},{14,12},{16,22},{18,... | collective-permute-start | bytes 1572872 | tf_op jit(solution)/shard_map/ppermute | solution.py:259
  89.9 14.2 %collective-permute-start.21 = (bf16[128,2048]{1,0:T(8,128)(2,1)S(1)}, bf16[128,2048]{1,0:T(8,128)(2,1)S(1)}, u32[]{:S(2)}, u32[]{:S(2)}) collective-permute-start(bf16[128,2048]{1,0:T(8,128)(2,1)S(1)} %get-tuple-element.603), channel_id=1, source_target_pairs={{0,2},{2,4},{4,6},{6,0},{8,10},{10,12},{12,14},{14,8},{16,18},{18,... | collective-permute-start | bytes 1572872 | tf_op jit(solution)/shard_map/ppermute | solution.py:263
  95.8 19.1 %collective-permute-start.24 = (bf16[128,2048]{1,0:T(8,128)(2,1)S(1)}, bf16[128,2048]{1,0:T(8,128)(2,1)S(1)}, u32[]{:S(2)}, u32[]{:S(2)}) collective-permute-start(bf16[128,2048]{1,0:T(8,128)(2,1)S(1)} %get-tuple-element.602), channel_id=1, source_target_pairs={{0,6},{2,0},{4,2},{6,4},{8,14},{10,8},{12,10},{14,12},{16,22},{18,... | collective-permute-start | bytes 1572872 | tf_op jit(solution)/shard_map/ppermute | solution.py:259
  101.1 15.2 %collective-permute-start.25 = (bf16[128,2048]{1,0:T(8,128)(2,1)S(1)}, bf16[128,2048]{1,0:T(8,128)(2,1)S(1)}, u32[]{:S(2)}, u32[]{:S(2)}) collective-permute-start(bf16[128,2048]{1,0:T(8,128)(2,1)S(1)} %get-tuple-element.601), channel_id=1, source_target_pairs={{0,2},{2,4},{4,6},{6,0},{8,10},{10,12},{12,14},{14,8},{16,18},{18,... | collective-permute-start | bytes 1572872 | tf_op jit(solution)/shard_map/ppermute | solution.py:263
  105.1 8.6 %collective-permute-start.22 = (f32[384,256]{1,0:T(8,128)S(1)}, f32[384,256]{1,0:T(8,128)S(1)}, u32[]{:S(2)}, u32[]{:S(2)}) collective-permute-start(f32[384,256]{1,0:T(8,128)S(1)} %get-tuple-element.540), channel_id=1, source_target_pairs={{0,1},{1,0},{2,3},{3,2},{4,5},{5,4},{6,7},{7,6},{8,9},{9,8},{10,11... | collective-permute-start | bytes 1179656 | tf_op jit(solution)/shard_map/ppermute | solution.py:242
  116.3 19.7 %collective-permute-start.29 = (f32[512,2048]{1,0:T(8,128)S(1)}, f32[512,2048]{1,0:T(8,128)S(1)}, u32[]{:S(2)}, u32[]{:S(2)}) collective-permute-start(f32[512,2048]{1,0:T(8,128)S(1)} %shard_map.35), channel_id=1, source_target_pairs={{0,1},{1,0},{2,3},{3,2},{4,5},{5,4},{6,7},{7,6},{8,9},{9,8},{10,11... | collective-permute-start | bytes 12582920 | tf_op jit(solution)/shard_map/ppermute | solution.py:242
  119.3 23.8 %collective-permute-start.28 = (f32[512,1536]{1,0:T(8,128)S(1)}, f32[512,1536]{1,0:T(8,128)S(1)}, u32[]{:S(2)}, u32[]{:S(2)}) collective-permute-start(f32[512,1536]{1,0:T(8,128)S(1)} %shard_map.41), channel_id=1, source_target_pairs={{0,1},{1,0},{2,3},{3,2},{4,5},{5,4},{6,7},{7,6},{8,9},{9,8},{10,11... | collective-permute-start | bytes 9437192 | tf_op jit(solution)/shard_map/ppermute | solution.py:242
  121.6 10.1 %collective-permute-start.26 = (f32[256,768]{1,0:T(8,128)S(1)}, f32[256,768]{1,0:T(8,128)S(1)}, u32[]{:S(2)}, u32[]{:S(2)}) collective-permute-start(f32[256,768]{1,0:T(8,128)S(1)} %shard_map.42), channel_id=1, source_target_pairs={{0,1},{1,0},{2,3},{3,2},{4,5},{5,4},{6,7},{7,6},{8,9},{9,8},{10,11... | collective-permute-start | bytes 2359304 | tf_op jit(solution)/shard_map/ppermute | solution.py:242
  122.3 29.1 %collective-permute-start.30 = (bf16[256,2048]{1,0:T(8,128)(2,1)S(1)}, bf16[256,2048]{1,0:T(8,128)(2,1)S(1)}, u32[]{:S(2)}, u32[]{:S(2)}) collective-permute-start(bf16[256,2048]{1,0:T(8,128)(2,1)S(1)} %pad_maximum_fusion), channel_id=1, source_target_pairs={{0,126},{2,0},{4,2},{6,4},{8,6},{10,8},{12,10},{14,12},{16,14},{18... | collective-permute-start | bytes 3145736 | tf_op jit(solution)/shard_map/ppermute | solution.py:326
  127.2 24.3 %collective-permute-start.31 = (f32[384,512]{1,0:T(8,128)S(1)}, f32[384,512]{1,0:T(8,128)S(1)}, u32[]{:S(2)}, u32[]{:S(2)}) collective-permute-start(f32[384,512]{1,0:T(8,128)S(1)} %shard_map.40), channel_id=1, source_target_pairs={{0,2},{2,4},{4,6},{6,8},{8,10},{10,12},{12,14},{14,16},{16,18},{18... | collective-permute-start | bytes 2359304 | tf_op jit(solution)/shard_map/ppermute | solution.py:325
  134.1 34.2 %collective-permute-start.27 = (f32[256,768]{1,0:T(8,128)S(1)}, f32[256,768]{1,0:T(8,128)S(1)}, u32[]{:S(2)}, u32[]{:S(2)}) collective-permute-start(f32[256,768]{1,0:T(8,128)S(1)} %shard_map.43), channel_id=1, source_target_pairs={{0,2},{2,4},{4,6},{6,8},{8,10},{10,12},{12,14},{14,16},{16,18},{18... | collective-permute-start | bytes 2359304 | tf_op jit(solution)/shard_map/ppermute | solution.py:327
  152.2 3.4 %collective-permute-start.34 = (f32[512,256]{1,0:T(8,128)S(1)}, f32[512,256]{1,0:T(8,128)S(1)}, u32[]{:S(2)}, u32[]{:S(2)}) collective-permute-start(f32[512,256]{1,0:T(8,128)S(1)} %shard_map.48), channel_id=1, source_target_pairs={{0,1},{1,0},{2,3},{3,2},{4,5},{5,4},{6,7},{7,6},{8,9},{9,8},{10,11... | collective-permute-start | bytes 1572872 | tf_op jit(solution)/shard_map/ppermute | solution.py:242
  (8 other events, 35.0 us)
where the time goes:
time: 170 us
  starting transfers between devices  79.3 us (47%)
  waiting for transfers between devices  40.1 us (24%)
  Pallas kernels  38.8 us (23%)
  local copies, waits for them, and re-layouts  8.38 us (5%)
  other arithmetic  2.86 us (2%)
    ppermute x8, starting transfers between devices, fetch4(): return ((4, p), lax.ppermute(s['held'][0, p], 'blk', below(4)))  40.2 us
    ppermute x8, starting transfers between devices, fetch1(): return ((1, p), lax.ppermute(send, 'blk', around(-1)))  19.7 us
    pallas_call x3, Pallas kernels, kept_products(): pl.pallas_call(kernel, out_shape=jax.ShapeDtypeStruct((5, half, 2 * half)...  15.7 us
    ppermute x8, waiting for transfers between devices, fetch3(): return ((3, p), lax.ppermute(send, 'blk', around(1)))  15.5 us
    ppermute x8, starting transfers between devices, swap(): return lax.ppermute(array, 'col', [(0, 1), (1, 0)])  12.7 us
    pallas_call x7, Pallas kernels, handed_products(): pl.pallas_call(kernel, out_shape=jax.ShapeDtypeStruct((half, room), jnp.f...  11.2 us
    ppermute x8, waiting for transfers between devices, fetch4(): return ((4, p), lax.ppermute(s['held'][0, p], 'blk', below(4)))  7.84 us
    ppermute x8, waiting for transfers between devices, swap(): return lax.ppermute(array, 'col', [(0, 1), (1, 0)])  7.04 us
  transfers between devices with their start and end apart: 35, of which 16 were waited for; matrix products, arithmetic and copies ran while one was open for 4% of the time, Pallas kernels for 21%

commit v1 on v0

--- a/solution.py
+++ b/solution.py
@@ -78,11 +78,9 @@
     return [[next(refs) for _ in arrays] for arrays in partners]
 
 
-def handed_products(handed, partners, group, before=None, total=None):
+def handed_products(handed, partners, group, before=None, room=None, offset=0):
     half, many = handed.shape[0], sum(map(len, partners))
-    size = width(group, half)
-    room = total or size
-    offset = 0 if before is None else room - size
+    room = room or width(group, half)
 
     def kernel(handed_ref, *refs):
         made_ref = refs[-1]
@@ -106,7 +104,7 @@
     )(handed, *sum(partners, []), *([] if before is None else [before]))
 
 
-def kept_products(out, weights, kept, theirs, partners, groups):
+def kept_products(out, weights, kept, theirs, partners, groups, offset=0):
     half, first_call = kept.shape[0], out is None
     many = sum(map(len, partners))
 
@@ -120,7 +118,8 @@
                 def span(column, columns, partner):
                     def strip(at):
                         across = pl.ds(first + column, columns)
-                        total = product(kept_ref[at, :], partner()) + theirs_ref[at, across]
+                        there = pl.ds(offset + first + column, columns)
+                        total = product(kept_ref[at, :], partner()) + theirs_ref[at, there]
                         made_ref[at, across] = total * weights_ref[k]
                     strips(half, strip)
 
@@ -270,20 +269,24 @@
     def partners(*groups):
         return [part(k, j) for group in groups for k, j in group]
 
-    def make(group, new=(), total=None):
-        s["made"][group] = handed_products(
-            s["handed"], partners(new or group), new or group, s["made"].get(group), total
+    def make(group, into=None, room=None, offset=0):
+        into = into or group
+        s["made"][into] = handed_products(
+            s["handed"], partners(group), group, s["made"].get(into), room, offset
         )
 
-    def finish(*groups):
-        theirs = [swap(s["made"].pop(group)) for group in groups]
-        s["out"] = kept_products(s["out"], weights, s["kept"], theirs, partners(*groups), groups)
+    def finish(theirs, *groups, offset=0):
+        s["out"] = kept_products(
+            s["out"], weights, s["kept"], theirs, partners(*groups), groups, offset
+        )
 
     own, ones = ((0, None),), ((4, 0), (4, 1), (1, 0), (3, 0))
     twos, threes = ((4, 2), (1, 1), (3, 1)), ((4, 3), (1, 2), (3, 2))
-    first, second = own + ones, twos + threes
-
-    mine(0)
+    everything = own + ones + twos + threes
+    room = width(everything, half)
+    places = [sum(width(group, half) for group in (own, ones, twos, threes)[:n]) for n in range(4)]
+
+    s["held"][0, 0] = basis_rows[:e]
     fence()
     mine(1)
     s["kept"] = lax.dynamic_slice_in_dim(basis_rows, core * half, half, 0)
@@ -297,21 +300,21 @@
             mine(p + 2)
             x.append(fetch4(p + 2))
         if p == 1:
-            make(first, own, width(first, half))
+            make(own, everything, room, places[0])
         if p == 3:
-            make(first, ones, width(first, half))
+            make(ones, everything, room, places[1])
         if p == 5:
-            make(second, twos, width(second, half))
+            make(twos, everything, room, places[2])
         fence(x[p + 1])
         d.append(fetch1(p + 1))
         u.append(fetch3(p + 1))
         fence(d[p], u[p])
 
-    make(second, threes, width(second, half))
+    make(threes, everything, room, places[3])
     some = (0, 1, 2)
     early = [(some, n, (n, 0, 0, e), (0, 0, n * e, (2 + n) * e)) for n in range(2)]
-    late = [((3,), n) + 2 * ((0, 0, n * e, (3 + n) * e),) for n in range(3)]
-    late += [((j,), 2) + 2 * ((0, e, 2 * j * e, (2 * j + 1) * e),) for j in some]
+    late = [((3,), n, (0, 0, n * e, (3 + n) * e), (0, 0, n * e, (3 + n) * e)) for n in range(3)]
+    late += [((j,), 2, (1, 0, 2 * j * e, (2 * j + 1) * e), (0, e, 2 * j * e, (2 * j + 1) * e)) for j in some]
 
     def ahead(blocks):
         rows = [part(1, j) for j in range(1 + max(max(parts) for parts, *_ in blocks))]
@@ -328,13 +331,15 @@
     third, fourth, fifth = ((1, 3),), ((3, 3),), ((2, 3),)
     make(third)
     make(fourth)
-    finish(first)
-    finish(second)
+    theirs = [swap(s["made"].pop(everything))]
+    finish(theirs, own + ones)
+    finish(theirs, twos + threes, offset=places[2])
     s["sums"], s["relayed"] = first_sums, relayed
     fence()
 
     make(fifth)
-    finish(third, fourth, fifth)
+    theirs = [swap(s["made"].pop(group)) for group in (third, fourth, fifth)]
+    finish(theirs, third, fourth, fifth)
     regions = [(0, n * 2 * e, 3 * e, 2 * e, 0, n * half) for n in range(2)]
     out = scaled_write(s["out"], weights, s["sums"], 2, regions)
     regions = [(0, n * 3 * e, e, 3 * e, 3 * e, n * half) for n in range(2)]

time: 170 us -> 166 us (0.976)
  waiting for transfers between devices: 40.1 us -> 35 us
  local copies, waits for them, and re-layouts: 8.38 us -> 10.3 us
    ppermute x1, waiting for transfers between devices: 3.16 us -> 0.23 us  [body(): first_sums = lax.ppermute(s['ahead'], 'blk', below(-1))]
    ppermute x8, waiting for transfers between devices: 7.84 us -> 5.65 us  [fetch4(): return ((4, p), lax.ppermute(s['held'][0, p], 'blk', below(4)))]
    slice x0 -> x1, local copies, waits for them, and re-layouts: none -> 1.89 us  [body(): s['held'][0, 0] = basis_rows[:e]]
  transfers between devices with their start and end apart: 35 -> 35, of which waited for: 16 -> 17; matrix products, arithmetic and copies ran while one was open for 4% -> 4% of each run, Pallas kernels for 21% -> 22%
where the time goes in v1:
time: 166 us
  starting transfers between devices  79.2 us (48%)
  Pallas kernels  37.9 us (23%)
  waiting for transfers between devices  35 us (21%)
  local copies, waits for them, and re-layouts  10.3 us (6%)
  other arithmetic  2.82 us (2%)
    ppermute x8, starting transfers between devices, fetch4(): return ((4, p), lax.ppermute(s['held'][0, p], 'blk', below(4)))  40.1 us
    ppermute x8, starting transfers between devices, fetch1(): return ((1, p), lax.ppermute(send, 'blk', around(-1)))  19.7 us
    pallas_call x3, Pallas kernels, kept_products(): pl.pallas_call(kernel, out_shape=jax.ShapeDtypeStruct((5, half, 2 * half)...  15.7 us
    ppermute x8, waiting for transfers between devices, fetch3(): return ((3, p), lax.ppermute(send, 'blk', around(1)))  15.5 us
    ppermute x8, starting transfers between devices, swap(): return lax.ppermute(array, 'col', [(0, 1), (1, 0)])  12.7 us
    pallas_call x7, Pallas kernels, handed_products(): pl.pallas_call(kernel, out_shape=jax.ShapeDtypeStruct((half, room), jnp.f...  11.2 us
    ppermute x8, waiting for transfers between devices, swap(): return lax.ppermute(array, 'col', [(0, 1), (1, 0)])  7.07 us
    pallas_call x4, Pallas kernels, relayed_products(): pl.pallas_call(kernel, out_shape=[jax.ShapeDtypeStruct(sizes[n], jnp.floa...  6.91 us
  transfers between devices with their start and end apart: 35, of which 17 were waited for; matrix products, arithmetic and copies ran while one was open for 4% of the time, Pallas kernels for 22%

profile of v1, /device:TPU:1, one launch (start us, length us, event | category | flops | bytes accessed | tf_op | source)
XLA Modules:
  0.0 165.8 jit_solution(931695127947136718)
XLA Ops:
  1.9 6.8 %collective-permute-start = (bf16[128,2048]{1,0:T(8,128)(2,1)}, bf16[128,2048]{1,0:T(8,128)(2,1)S(1)}, u32[]{:S(2)}, u32[]{:S(2)}) collective-permute-start(bf16[128,2048]{1,0:T(8,128)(2,1)} %slice.3), channel_id=1, source_target_pairs={{0,120},{2,122},{4,124},{6,126},{8,0},{10,2},{12,4},{14,6},{16,8},... | collective-permute-start | bytes 1572872 | tf_op jit(solution)/shard_map/ppermute | solution.py:254
  12.4 4.0 %constant_dynamic-slice_fusion = (bf16[512,2048]{1,0:T(8,128)(2,1)}, bf16[512,2048]{1,0:T(8,128)(2,1)S(1)}) fusion(bf16[1024,2048]{1,0:T(8,128)(2,1)} %refs_1_.1, s32[]{:T(128)S(6)} %select_n.84, s32[]{:T(128)S(6)} %select_n.83), kind=kLoop, calls=%fused_computation.18 | loop fusion | bytes 8388616 | tf_op jit(solution)/shard_map/dynamic_slice | solution.py:292
  16.3 3.2 %collective-permute-done.refs_0_.refs_2_ = bf16[128,2048]{1,0:T(8,128)(2,1)S(1)} collective-permute-done((bf16[128,2048]{1,0:T(8,128)(2,1)}, bf16[128,2048]{1,0:T(8,128)(2,1)S(1)}, u32[]{:S(2)}, u32[]{:S(2)}) %collective-permute-start) | collective-permute-done | bytes 524320 | tf_op jit(solution)/shard_map/ppermute | solution.py:254
  20.7 2.8 %collective-permute-start.2 = (bf16[128,2048]{1,0:T(8,128)(2,1)S(1)}, bf16[128,2048]{1,0:T(8,128)(2,1)S(1)}, u32[]{:S(2)}, u32[]{:S(2)}) collective-permute-start(bf16[128,2048]{1,0:T(8,128)(2,1)S(1)} %get-tuple-element.610), channel_id=1, source_target_pairs={{0,6},{2,0},{4,2},{6,4},{8,14},{10,8},{12,10},{14,12},{16,22},{18,... | collective-permute-start | bytes 1572872 | tf_op jit(solution)/shard_map/ppermute | solution.py:258
  25.7 5.5 %collective-permute-start.4 = (bf16[128,2048]{1,0:T(8,128)(2,1)S(1)}, bf16[128,2048]{1,0:T(8,128)(2,1)S(1)}, u32[]{:S(2)}, u32[]{:S(2)}) collective-permute-start(bf16[128,2048]{1,0:T(8,128)(2,1)S(1)} %shard_map.29), channel_id=1, source_target_pairs={{0,120},{2,122},{4,124},{6,126},{8,0},{10,2},{12,4},{14,6},{16,8},... | collective-permute-start | bytes 1572872 | tf_op jit(solution)/shard_map/ppermute | solution.py:254
  32.4 2.7 %collective-permute-start.5 = (bf16[128,2048]{1,0:T(8,128)(2,1)S(1)}, bf16[128,2048]{1,0:T(8,128)(2,1)S(1)}, u32[]{:S(2)}, u32[]{:S(2)}) collective-permute-start(bf16[128,2048]{1,0:T(8,128)(2,1)S(1)} %get-tuple-element.608), channel_id=1, source_target_pairs={{0,6},{2,0},{4,2},{6,4},{8,14},{10,8},{12,10},{14,12},{16,22},{18,... | collective-permute-start | bytes 1572872 | tf_op jit(solution)/shard_map/ppermute | solution.py:258
  35.2 5.5 %collective-permute-start.7 = (bf16[128,2048]{1,0:T(8,128)(2,1)S(1)}, bf16[128,2048]{1,0:T(8,128)(2,1)S(1)}, u32[]{:S(2)}, u32[]{:S(2)}) collective-permute-start(bf16[128,2048]{1,0:T(8,128)(2,1)S(1)} %shard_map.30), channel_id=1, source_target_pairs={{0,120},{2,122},{4,124},{6,126},{8,0},{10,2},{12,4},{14,6},{16,8},... | collective-permute-start | bytes 1572872 | tf_op jit(solution)/shard_map/ppermute | solution.py:254
  40.7 3.0 %shard_map.31.refs_8_ = f32[512,3584]{1,0:T(8,128)S(1)} custom-call(bf16[512,2048]{1,0:T(8,128)(2,1)S(1)} %get-tuple-element.586.handed_ref, bf16[1024,2048]{1,0:T(8,128)(2,1)S(1)} %copy-done.2), custom_call_target="tpu_custom_call" | custom-call | flops 1 | bytes 1 | tf_op jit(solution)/shard_map/pallas_call | solution.py:96
  43.8 2.3 %collective-permute-start.8 = (bf16[128,2048]{1,0:T(8,128)(2,1)S(1)}, bf16[128,2048]{1,0:T(8,128)(2,1)S(1)}, u32[]{:S(2)}, u32[]{:S(2)}) collective-permute-start(bf16[128,2048]{1,0:T(8,128)(2,1)S(1)} %get-tuple-element.606), channel_id=1, source_target_pairs={{0,6},{2,0},{4,2},{6,4},{8,14},{10,8},{12,10},{14,12},{16,22},{18,... | collective-permute-start | bytes 1572872 | tf_op jit(solution)/shard_map/ppermute | solution.py:258
  46.2 6.8 %collective-permute-start.10 = (bf16[128,2048]{1,0:T(8,128)(2,1)S(1)}, bf16[128,2048]{1,0:T(8,128)(2,1)S(1)}, u32[]{:S(2)}, u32[]{:S(2)}) collective-permute-start(bf16[128,2048]{1,0:T(8,128)(2,1)S(1)} %shard_map.32), channel_id=1, source_target_pairs={{0,120},{2,122},{4,124},{6,126},{8,0},{10,2},{12,4},{14,6},{16,8},... | collective-permute-start | bytes 1572872 | tf_op jit(solution)/shard_map/ppermute | solution.py:254
  55.2 3.1 %collective-permute-done.9.refs_4_.refs_8_.refs_10_.refs_5_ = bf16[128,2048]{1,0:T(8,128)(2,1)S(1)} collective-permute-done((bf16[128,2048]{1,0:T(8,128)(2,1)S(1)}, bf16[128,2048]{1,0:T(8,128)(2,1)S(1)}, u32[]{:S(2)}, u32[]{:S(2)}) %collective-permute-start.9) | collective-permute-done | bytes 524320 | tf_op jit(solution)/shard_map/ppermute | solution.py:262
  58.4 4.7 %collective-permute-start.13 = (bf16[128,2048]{1,0:T(8,128)(2,1)S(1)}, bf16[128,2048]{1,0:T(8,128)(2,1)S(1)}, u32[]{:S(2)}, u32[]{:S(2)}) collective-permute-start(bf16[128,2048]{1,0:T(8,128)(2,1)S(1)} %shard_map.33), channel_id=1, source_target_pairs={{0,120},{2,122},{4,124},{6,126},{8,0},{10,2},{12,4},{14,6},{16,8},... | collective-permute-start | bytes 1572872 | tf_op jit(solution)/shard_map/ppermute | solution.py:254
  63.1 2.4 %shard_map.34.refs_6_ = f32[512,3584]{1,0:T(8,128)S(1)} custom-call(bf16[512,2048]{1,0:T(8,128)(2,1)S(1)} %get-tuple-element.586.handed_ref, bf16[128,2048]{1,0:T(8,128)(2,1)S(1)} %collective-permute-done.refs_0_.refs_2_, bf16[128,2048]{1,0:T(8,128)(2,1)S(1)} %collective-permute-done.1.refs_1_.refs_3_, ...), custom_call_target="tpu_custom_call", output_to_operand_aliasing={{}: (9, {})} | custom-call | flops 1 | bytes 1 | tf_op jit(solution)/shard_map/pallas_call | solution.py:96
  67.1 2.5 %collective-permute-done.12.refs_5_.refs_9_.refs_11_.refs_6_ = bf16[128,2048]{1,0:T(8,128)(2,1)S(1)} collective-permute-done((bf16[128,2048]{1,0:T(8,128)(2,1)S(1)}, bf16[128,2048]{1,0:T(8,128)(2,1)S(1)}, u32[]{:S(2)}, u32[]{:S(2)}) %collective-permute-start.12) | collective-permute-done | bytes 524320 | tf_op jit(solution)/shard_map/ppermute | solution.py:262
  69.6 4.7 %collective-permute-start.16 = (bf16[128,2048]{1,0:T(8,128)(2,1)S(1)}, bf16[128,2048]{1,0:T(8,128)(2,1)S(1)}, u32[]{:S(2)}, u32[]{:S(2)}) collective-permute-start(bf16[128,2048]{1,0:T(8,128)(2,1)S(1)} %shard_map.35), channel_id=1, source_target_pairs={{0,120},{2,122},{4,124},{6,126},{8,0},{10,2},{12,4},{14,6},{16,8},... | collective-permute-start | bytes 1572872 | tf_op jit(solution)/shard_map/ppermute | solution.py:254
  74.4 3.0 %collective-permute-start.17 = (bf16[128,2048]{1,0:T(8,128)(2,1)S(1)}, bf16[128,2048]{1,0:T(8,128)(2,1)S(1)}, u32[]{:S(2)}, u32[]{:S(2)}) collective-permute-start(bf16[128,2048]{1,0:T(8,128)(2,1)S(1)} %get-tuple-element.600), channel_id=1, source_target_pairs={{0,6},{2,0},{4,2},{6,4},{8,14},{10,8},{12,10},{14,12},{16,22},{18,... | collective-permute-start | bytes 1572872 | tf_op jit(solution)/shard_map/ppermute | solution.py:258
  77.4 2.6 %collective-permute-done.15.refs_4_.refs_12_.refs_11_ = bf16[128,2048]{1,0:T(8,128)(2,1)S(1)} collective-permute-done((bf16[128,2048]{1,0:T(8,128)(2,1)S(1)}, bf16[128,2048]{1,0:T(8,128)(2,1)S(1)}, u32[]{:S(2)}, u32[]{:S(2)}) %collective-permute-start.15) | collective-permute-done | bytes 524320 | tf_op jit(solution)/shard_map/ppermute | solution.py:262
  80.0 5.7 %collective-permute-start.19 = (bf16[128,2048]{1,0:T(8,128)(2,1)S(1)}, bf16[128,2048]{1,0:T(8,128)(2,1)S(1)}, u32[]{:S(2)}, u32[]{:S(2)}) collective-permute-start(bf16[128,2048]{1,0:T(8,128)(2,1)S(1)} %shard_map.36), channel_id=1, source_target_pairs={{0,120},{2,122},{4,124},{6,126},{8,0},{10,2},{12,4},{14,6},{16,8},... | collective-permute-start | bytes 1572872 | tf_op jit(solution)/shard_map/ppermute | solution.py:254
  89.2 2.9 %collective-permute-done.18.refs_5_.refs_13_.refs_12_ = bf16[128,2048]{1,0:T(8,128)(2,1)S(1)} collective-permute-done((bf16[128,2048]{1,0:T(8,128)(2,1)S(1)}, bf16[128,2048]{1,0:T(8,128)(2,1)S(1)}, u32[]{:S(2)}, u32[]{:S(2)}) %collective-permute-start.18) | collective-permute-done | bytes 524320 | tf_op jit(solution)/shard_map/ppermute | solution.py:262
  92.1 2.4 %collective-permute-done.19.refs_1_.refs_8_ = bf16[128,2048]{1,0:T(8,128)(2,1)S(1)} collective-permute-done((bf16[128,2048]{1,0:T(8,128)(2,1)S(1)}, bf16[128,2048]{1,0:T(8,128)(2,1)S(1)}, u32[]{:S(2)}, u32[]{:S(2)}) %collective-permute-start.19) | collective-permute-done | bytes 524320 | tf_op jit(solution)/shard_map/ppermute | solution.py:254
  94.5 5.3 %collective-permute-start.24 = (bf16[128,2048]{1,0:T(8,128)(2,1)S(1)}, bf16[128,2048]{1,0:T(8,128)(2,1)S(1)}, u32[]{:S(2)}, u32[]{:S(2)}) collective-permute-start(bf16[128,2048]{1,0:T(8,128)(2,1)S(1)} %get-tuple-element.596), channel_id=1, source_target_pairs={{0,6},{2,0},{4,2},{6,4},{8,14},{10,8},{12,10},{14,12},{16,22},{18,... | collective-permute-start | bytes 1572872 | tf_op jit(solution)/shard_map/ppermute | solution.py:258
  99.9 2.9 %collective-permute-done.21.refs_0_.refs_5_ = bf16[128,2048]{1,0:T(8,128)(2,1)S(1)} collective-permute-done((bf16[128,2048]{1,0:T(8,128)(2,1)S(1)}, bf16[128,2048]{1,0:T(8,128)(2,1)S(1)}, u32[]{:S(2)}, u32[]{:S(2)}) %collective-permute-start.21) | collective-permute-done | bytes 524320 | tf_op jit(solution)/shard_map/ppermute | solution.py:262
  103.9 6.7 %collective-permute-start.22 = (f32[384,256]{1,0:T(8,128)S(1)}, f32[384,256]{1,0:T(8,128)S(1)}, u32[]{:S(2)}, u32[]{:S(2)}) collective-permute-start(f32[384,256]{1,0:T(8,128)S(1)} %get-tuple-element.534), channel_id=1, source_target_pairs={{0,1},{1,0},{2,3},{3,2},{4,5},{5,4},{6,7},{7,6},{8,9},{9,8},{10,11... | collective-permute-start | bytes 1179656 | tf_op jit(solution)/shard_map/ppermute | solution.py:241
  115.1 3.0 %collective-permute-start.29 = (f32[512,3584]{1,0:T(8,128)S(1)}, f32[512,3584]{1,0:T(8,128)S(1)}, u32[]{:S(2)}, u32[]{:S(2)}) collective-permute-start(f32[512,3584]{1,0:T(8,128)S(1)} %shard_map.40), channel_id=1, source_target_pairs={{0,1},{1,0},{2,3},{3,2},{4,5},{5,4},{6,7},{7,6},{8,9},{9,8},{10,11... | collective-permute-start | bytes 22020104 | tf_op jit(solution)/shard_map/ppermute | solution.py:241
  118.1 4.8 %collective-permute-start.30 = (bf16[256,2048]{1,0:T(8,128)(2,1)S(1)}, bf16[256,2048]{1,0:T(8,128)(2,1)S(1)}, u32[]{:S(2)}, u32[]{:S(2)}) collective-permute-start(bf16[256,2048]{1,0:T(8,128)(2,1)S(1)} %pad_maximum_fusion), channel_id=1, source_target_pairs={{0,126},{2,0},{4,2},{6,4},{8,6},{10,8},{12,10},{14,12},{16,14},{18... | collective-permute-start | bytes 3145736 | tf_op jit(solution)/shard_map/ppermute | solution.py:329
  123.0 2.3 %shard_map.41 = (f32[128,768]{1,0:T(8,128)S(1)}, f32[128,768]{1,0:T(8,128)S(1)}) custom-call(s32[1]{0:T(128)} %bitcast.1._.where_ref, bf16[128,2048]{1,0:T(8,128)(2,1)S(1)} %collective-permute-done.2.refs_4_.refs_0_.refs_6_, bf16[128,2048]{1,0:T(8,128)(2,1)S(1)} %collective-permute-done.5.refs_5_.refs_1_.refs_7_, ...), custom_call_target="tpu_custom_call" | custom-call | flops 1 | bytes 1 | tf_op jit(solution)/shard_map/pallas_call | solution.py:185
  125.9 4.0 %collective-permute-done.26.refs_14_ = f32[128,768]{1,0:T(8,128)S(1)} collective-permute-done((f32[128,768]{1,0:T(8,128)S(1)}, f32[128,768]{1,0:T(8,128)S(1)}, u32[]{:S(2)}, u32[]{:S(2)}) %collective-permute-start.26) | collective-permute-done | bytes 393248 | tf_op jit(solution)/shard_map/ppermute | solution.py:241
  130.5 2.3 %shard_map.42 = f32[256,768]{1,0:T(8,128)S(1)} custom-call(s32[1]{0:T(128)} %bitcast.1._.where_ref, bf16[128,2048]{1,0:T(8,128)(2,1)S(1)} %collective-permute-done.2.refs_4_.refs_0_.refs_6_, bf16[128,2048]{1,0:T(8,128)(2,1)S(1)} %collective-permute-done.5.refs_5_.refs_1_.refs_7_, bf16[128,2048]{1,0:T(8,128)(2,1)S(1)} %collective-permute-done.8.refs_2_.refs_3_, ...), custom_call_target="tpu_custom_call" | custom-call | flops 1 | bytes 1 | tf_op jit(solution)/shard_map/pallas_call | solution.py:185
  134.7 7.1 %shard_map.45.refs_13_ = f32[5,512,1024]{2,1,0:T(8,128)} custom-call(f32[5]{0:T(128)S(1)} %pad_maximum_fusion.1.weights_ref, bf16[512,2048]{1,0:T(8,128)(2,1)S(1)} %copy-done.3, f32[512,3584]{1,0:T(8,128)S(1)} %collective-permute-done.29.refs_0_, bf16[1024,2048]{1,0:T(8,128)(2,1)S(1)} %copy-done.2, ...), custom_call_target="tpu_custom_call" | custom-call | flops 1 | bytes 1 | tf_op jit(solution)/shard_map/pallas_call | solution.py:139
  141.8 5.2 %shard_map.46.refs_8_ = f32[5,512,1024]{2,1,0:T(8,128)} custom-call(f32[5]{0:T(128)S(1)} %pad_maximum_fusion.1.weights_ref, bf16[512,2048]{1,0:T(8,128)(2,1)S(1)} %copy-done.3, f32[512,3584]{1,0:T(8,128)S(1)} %collective-permute-done.29.refs_0_, bf16[128,2048]{1,0:T(8,128)(2,1)S(1)} %collective-permute-done.10.refs_0_.refs_1_, ...), custom_call_target="tpu_custom_call", output_to_operand_aliasing={{}: (15, {})} | custom-call | flops 1 | bytes 1 | tf_op jit(solution)/shard_map/pallas_call | solution.py:139
  152.9 3.4 %shard_map.48._ = f32[5,512,1024]{2,1,0:T(8,128)} custom-call(f32[5]{0:T(128)S(1)} %pad_maximum_fusion.1.weights_ref, bf16[512,2048]{1,0:T(8,128)(2,1)S(1)} %copy-done.3, f32[512,256]{1,0:T(8,128)S(1)} %collective-permute-done.32.refs_0_, f32[512,256]{1,0:T(8,128)S(1)} %collective-permute-done.33.refs_1_, ...), custom_call_target="tpu_custom_call", output_to_operand_aliasing={{}: (10, {})} | custom-call | flops 1 | bytes 1 | tf_op jit(solution)/shard_map/pallas_call | solution.py:139
  157.8 6.3 %collective-permute-done.28.summed_ref = f32[256,768]{1,0:T(8,128)S(1)} collective-permute-done((f32[256,768]{1,0:T(8,128)S(1)}, f32[256,768]{1,0:T(8,128)S(1)}, u32[]{:S(2)}, u32[]{:S(2)}) %collective-permute-start.28) | collective-permute-done | bytes 786464 | tf_op jit(solution)/shard_map/ppermute | solution.py:330
  (84 shorter events, 35.4 us)
Async XLA Ops:
  1.9 17.7 %collective-permute-start = (bf16[128,2048]{1,0:T(8,128)(2,1)}, bf16[128,2048]{1,0:T(8,128)(2,1)S(1)}, u32[]{:S(2)}, u32[]{:S(2)}) collective-permute-start(bf16[128,2048]{1,0:T(8,128)(2,1)} %slice.3), channel_id=1, source_target_pairs={{0,120},{2,122},{4,124},{6,126},{8,0},{10,2},{12,4},{14,6},{16,8},... | collective-permute-start | bytes 1572872 | tf_op jit(solution)/shard_map/ppermute | solution.py:254
  11.7 19.5 %collective-permute-start.1 = (bf16[128,2048]{1,0:T(8,128)(2,1)}, bf16[128,2048]{1,0:T(8,128)(2,1)S(1)}, u32[]{:S(2)}, u32[]{:S(2)}) collective-permute-start(bf16[128,2048]{1,0:T(8,128)(2,1)} %shard_map.28), channel_id=1, source_target_pairs={{0,120},{2,122},{4,124},{6,126},{8,0},{10,2},{12,4},{14,6},{16,8},... | collective-permute-start | bytes 1572872 | tf_op jit(solution)/shard_map/ppermute | solution.py:254
  20.7 14.4 %collective-permute-start.2 = (bf16[128,2048]{1,0:T(8,128)(2,1)S(1)}, bf16[128,2048]{1,0:T(8,128)(2,1)S(1)}, u32[]{:S(2)}, u32[]{:S(2)}) collective-permute-start(bf16[128,2048]{1,0:T(8,128)(2,1)S(1)} %get-tuple-element.610), channel_id=1, source_target_pairs={{0,6},{2,0},{4,2},{6,4},{8,14},{10,8},{12,10},{14,12},{16,22},{18,... | collective-permute-start | bytes 1572872 | tf_op jit(solution)/shard_map/ppermute | solution.py:258
  23.5 11.7 %collective-permute-start.3 = (bf16[128,2048]{1,0:T(8,128)(2,1)S(1)}, bf16[128,2048]{1,0:T(8,128)(2,1)S(1)}, u32[]{:S(2)}, u32[]{:S(2)}) collective-permute-start(bf16[128,2048]{1,0:T(8,128)(2,1)S(1)} %get-tuple-element.609), channel_id=1, source_target_pairs={{0,2},{2,4},{4,6},{6,0},{8,10},{10,12},{12,14},{14,8},{16,18},{18,... | collective-permute-start | bytes 1572872 | tf_op jit(solution)/shard_map/ppermute | solution.py:262
  25.7 17.9 %collective-permute-start.4 = (bf16[128,2048]{1,0:T(8,128)(2,1)S(1)}, bf16[128,2048]{1,0:T(8,128)(2,1)S(1)}, u32[]{:S(2)}, u32[]{:S(2)}) collective-permute-start(bf16[128,2048]{1,0:T(8,128)(2,1)S(1)} %shard_map.29), channel_id=1, source_target_pairs={{0,120},{2,122},{4,124},{6,126},{8,0},{10,2},{12,4},{14,6},{16,8},... | collective-permute-start | bytes 1572872 | tf_op jit(solution)/shard_map/ppermute | solution.py:254
  32.4 13.8 %collective-permute-start.5 = (bf16[128,2048]{1,0:T(8,128)(2,1)S(1)}, bf16[128,2048]{1,0:T(8,128)(2,1)S(1)}, u32[]{:S(2)}, u32[]{:S(2)}) collective-permute-start(bf16[128,2048]{1,0:T(8,128)(2,1)S(1)} %get-tuple-element.608), channel_id=1, source_target_pairs={{0,6},{2,0},{4,2},{6,4},{8,14},{10,8},{12,10},{14,12},{16,22},{18,... | collective-permute-start | bytes 1572872 | tf_op jit(solution)/shard_map/ppermute | solution.py:258
  35.1 11.0 %collective-permute-start.6 = (bf16[128,2048]{1,0:T(8,128)(2,1)S(1)}, bf16[128,2048]{1,0:T(8,128)(2,1)S(1)}, u32[]{:S(2)}, u32[]{:S(2)}) collective-permute-start(bf16[128,2048]{1,0:T(8,128)(2,1)S(1)} %get-tuple-element.607), channel_id=1, source_target_pairs={{0,2},{2,4},{4,6},{6,0},{8,10},{10,12},{12,14},{14,8},{16,18},{18,... | collective-permute-start | bytes 1572872 | tf_op jit(solution)/shard_map/ppermute | solution.py:262
  35.2 17.7 %collective-permute-start.7 = (bf16[128,2048]{1,0:T(8,128)(2,1)S(1)}, bf16[128,2048]{1,0:T(8,128)(2,1)S(1)}, u32[]{:S(2)}, u32[]{:S(2)}) collective-permute-start(bf16[128,2048]{1,0:T(8,128)(2,1)S(1)} %shard_map.30), channel_id=1, source_target_pairs={{0,120},{2,122},{4,124},{6,126},{8,0},{10,2},{12,4},{14,6},{16,8},... | collective-permute-start | bytes 1572872 | tf_op jit(solution)/shard_map/ppermute | solution.py:254
  43.8 11.4 %collective-permute-start.8 = (bf16[128,2048]{1,0:T(8,128)(2,1)S(1)}, bf16[128,2048]{1,0:T(8,128)(2,1)S(1)}, u32[]{:S(2)}, u32[]{:S(2)}) collective-permute-start(bf16[128,2048]{1,0:T(8,128)(2,1)S(1)} %get-tuple-element.606), channel_id=1, source_target_pairs={{0,6},{2,0},{4,2},{6,4},{8,14},{10,8},{12,10},{14,12},{16,22},{18,... | collective-permute-start | bytes 1572872 | tf_op jit(solution)/shard_map/ppermute | solution.py:258
  46.1 12.2 %collective-permute-start.9 = (bf16[128,2048]{1,0:T(8,128)(2,1)S(1)}, bf16[128,2048]{1,0:T(8,128)(2,1)S(1)}, u32[]{:S(2)}, u32[]{:S(2)}) collective-permute-start(bf16[128,2048]{1,0:T(8,128)(2,1)S(1)} %get-tuple-element.605), channel_id=1, source_target_pairs={{0,2},{2,4},{4,6},{6,0},{8,10},{10,12},{12,14},{14,8},{16,18},{18,... | collective-permute-start | bytes 1572872 | tf_op jit(solution)/shard_map/ppermute | solution.py:262
  46.2 19.2 %collective-permute-start.10 = (bf16[128,2048]{1,0:T(8,128)(2,1)S(1)}, bf16[128,2048]{1,0:T(8,128)(2,1)S(1)}, u32[]{:S(2)}, u32[]{:S(2)}) collective-permute-start(bf16[128,2048]{1,0:T(8,128)(2,1)S(1)} %shard_map.32), channel_id=1, source_target_pairs={{0,120},{2,122},{4,124},{6,126},{8,0},{10,2},{12,4},{14,6},{16,8},... | collective-permute-start | bytes 1572872 | tf_op jit(solution)/shard_map/ppermute | solution.py:254
  53.0 14.0 %collective-permute-start.11 = (bf16[128,2048]{1,0:T(8,128)(2,1)S(1)}, bf16[128,2048]{1,0:T(8,128)(2,1)S(1)}, u32[]{:S(2)}, u32[]{:S(2)}) collective-permute-start(bf16[128,2048]{1,0:T(8,128)(2,1)S(1)} %get-tuple-element.604), channel_id=1, source_target_pairs={{0,6},{2,0},{4,2},{6,4},{8,14},{10,8},{12,10},{14,12},{16,22},{18,... | collective-permute-start | bytes 1572872 | tf_op jit(solution)/shard_map/ppermute | solution.py:258
  54.9 14.7 %collective-permute-start.12 = (bf16[128,2048]{1,0:T(8,128)(2,1)S(1)}, bf16[128,2048]{1,0:T(8,128)(2,1)S(1)}, u32[]{:S(2)}, u32[]{:S(2)}) collective-permute-start(bf16[128,2048]{1,0:T(8,128)(2,1)S(1)} %get-tuple-element.603), channel_id=1, source_target_pairs={{0,2},{2,4},{4,6},{6,0},{8,10},{10,12},{12,14},{14,8},{16,18},{18,... | collective-permute-start | bytes 1572872 | tf_op jit(solution)/shard_map/ppermute | solution.py:262
  58.4 15.9 %collective-permute-start.13 = (bf16[128,2048]{1,0:T(8,128)(2,1)S(1)}, bf16[128,2048]{1,0:T(8,128)(2,1)S(1)}, u32[]{:S(2)}, u32[]{:S(2)}) collective-permute-start(bf16[128,2048]{1,0:T(8,128)(2,1)S(1)} %shard_map.33), channel_id=1, source_target_pairs={{0,120},{2,122},{4,124},{6,126},{8,0},{10,2},{12,4},{14,6},{16,8},... | collective-permute-start | bytes 1572872 | tf_op jit(solution)/shard_map/ppermute | solution.py:254
  65.5 11.9 %collective-permute-start.14 = (bf16[128,2048]{1,0:T(8,128)(2,1)S(1)}, bf16[128,2048]{1,0:T(8,128)(2,1)S(1)}, u32[]{:S(2)}, u32[]{:S(2)}) collective-permute-start(bf16[128,2048]{1,0:T(8,128)(2,1)S(1)} %get-tuple-element.602), channel_id=1, source_target_pairs={{0,6},{2,0},{4,2},{6,4},{8,14},{10,8},{12,10},{14,12},{16,22},{18,... | collective-permute-start | bytes 1572872 | tf_op jit(solution)/shard_map/ppermute | solution.py:258
  66.2 13.8 %collective-permute-start.15 = (bf16[128,2048]{1,0:T(8,128)(2,1)S(1)}, bf16[128,2048]{1,0:T(8,128)(2,1)S(1)}, u32[]{:S(2)}, u32[]{:S(2)}) collective-permute-start(bf16[128,2048]{1,0:T(8,128)(2,1)S(1)} %get-tuple-element.601), channel_id=1, source_target_pairs={{0,2},{2,4},{4,6},{6,0},{8,10},{10,12},{12,14},{14,8},{16,18},{18,... | collective-permute-start | bytes 1572872 | tf_op jit(solution)/shard_map/ppermute | solution.py:262
  69.6 17.9 %collective-permute-start.16 = (bf16[128,2048]{1,0:T(8,128)(2,1)S(1)}, bf16[128,2048]{1,0:T(8,128)(2,1)S(1)}, u32[]{:S(2)}, u32[]{:S(2)}) collective-permute-start(bf16[128,2048]{1,0:T(8,128)(2,1)S(1)} %shard_map.35), channel_id=1, source_target_pairs={{0,120},{2,122},{4,124},{6,126},{8,0},{10,2},{12,4},{14,6},{16,8},... | collective-permute-start | bytes 1572872 | tf_op jit(solution)/shard_map/ppermute | solution.py:254
  74.4 14.8 %collective-permute-start.17 = (bf16[128,2048]{1,0:T(8,128)(2,1)S(1)}, bf16[128,2048]{1,0:T(8,128)(2,1)S(1)}, u32[]{:S(2)}, u32[]{:S(2)}) collective-permute-start(bf16[128,2048]{1,0:T(8,128)(2,1)S(1)} %get-tuple-element.600), channel_id=1, source_target_pairs={{0,6},{2,0},{4,2},{6,4},{8,14},{10,8},{12,10},{14,12},{16,22},{18,... | collective-permute-start | bytes 1572872 | tf_op jit(solution)/shard_map/ppermute | solution.py:258
  77.4 14.7 %collective-permute-start.18 = (bf16[128,2048]{1,0:T(8,128)(2,1)S(1)}, bf16[128,2048]{1,0:T(8,128)(2,1)S(1)}, u32[]{:S(2)}, u32[]{:S(2)}) collective-permute-start(bf16[128,2048]{1,0:T(8,128)(2,1)S(1)} %get-tuple-element.599), channel_id=1, source_target_pairs={{0,2},{2,4},{4,6},{6,0},{8,10},{10,12},{12,14},{14,8},{16,18},{18,... | collective-permute-start | bytes 1572872 | tf_op jit(solution)/shard_map/ppermute | solution.py:262
  80.0 14.4 %collective-permute-start.19 = (bf16[128,2048]{1,0:T(8,128)(2,1)S(1)}, bf16[128,2048]{1,0:T(8,128)(2,1)S(1)}, u32[]{:S(2)}, u32[]{:S(2)}) collective-permute-start(bf16[128,2048]{1,0:T(8,128)(2,1)S(1)} %shard_map.36), channel_id=1, source_target_pairs={{0,120},{2,122},{4,124},{6,126},{8,0},{10,2},{12,4},{14,6},{16,8},... | collective-permute-start | bytes 1572872 | tf_op jit(solution)/shard_map/ppermute | solution.py:254
  87.6 12.2 %collective-permute-start.20 = (bf16[128,2048]{1,0:T(8,128)(2,1)S(1)}, bf16[128,2048]{1,0:T(8,128)(2,1)S(1)}, u32[]{:S(2)}, u32[]{:S(2)}) collective-permute-start(bf16[128,2048]{1,0:T(8,128)(2,1)S(1)} %get-tuple-element.598), channel_id=1, source_target_pairs={{0,6},{2,0},{4,2},{6,4},{8,14},{10,8},{12,10},{14,12},{16,22},{18,... | collective-permute-start | bytes 1572872 | tf_op jit(solution)/shard_map/ppermute | solution.py:258
  88.6 14.2 %collective-permute-start.21 = (bf16[128,2048]{1,0:T(8,128)(2,1)S(1)}, bf16[128,2048]{1,0:T(8,128)(2,1)S(1)}, u32[]{:S(2)}, u32[]{:S(2)}) collective-permute-start(bf16[128,2048]{1,0:T(8,128)(2,1)S(1)} %get-tuple-element.597), channel_id=1, source_target_pairs={{0,2},{2,4},{4,6},{6,0},{8,10},{10,12},{12,14},{14,8},{16,18},{18,... | collective-permute-start | bytes 1572872 | tf_op jit(solution)/shard_map/ppermute | solution.py:262
  94.5 19.1 %collective-permute-start.24 = (bf16[128,2048]{1,0:T(8,128)(2,1)S(1)}, bf16[128,2048]{1,0:T(8,128)(2,1)S(1)}, u32[]{:S(2)}, u32[]{:S(2)}) collective-permute-start(bf16[128,2048]{1,0:T(8,128)(2,1)S(1)} %get-tuple-element.596), channel_id=1, source_target_pairs={{0,6},{2,0},{4,2},{6,4},{8,14},{10,8},{12,10},{14,12},{16,22},{18,... | collective-permute-start | bytes 1572872 | tf_op jit(solution)/shard_map/ppermute | solution.py:258
  99.9 15.2 %collective-permute-start.25 = (bf16[128,2048]{1,0:T(8,128)(2,1)S(1)}, bf16[128,2048]{1,0:T(8,128)(2,1)S(1)}, u32[]{:S(2)}, u32[]{:S(2)}) collective-permute-start(bf16[128,2048]{1,0:T(8,128)(2,1)S(1)} %get-tuple-element.595), channel_id=1, source_target_pairs={{0,2},{2,4},{4,6},{6,0},{8,10},{10,12},{12,14},{14,8},{16,18},{18,... | collective-permute-start | bytes 1572872 | tf_op jit(solution)/shard_map/ppermute | solution.py:262
  103.9 8.6 %collective-permute-start.22 = (f32[384,256]{1,0:T(8,128)S(1)}, f32[384,256]{1,0:T(8,128)S(1)}, u32[]{:S(2)}, u32[]{:S(2)}) collective-permute-start(f32[384,256]{1,0:T(8,128)S(1)} %get-tuple-element.534), channel_id=1, source_target_pairs={{0,1},{1,0},{2,3},{3,2},{4,5},{5,4},{6,7},{7,6},{8,9},{9,8},{10,11... | collective-permute-start | bytes 1179656 | tf_op jit(solution)/shard_map/ppermute | solution.py:241
  115.1 19.6 %collective-permute-start.29 = (f32[512,3584]{1,0:T(8,128)S(1)}, f32[512,3584]{1,0:T(8,128)S(1)}, u32[]{:S(2)}, u32[]{:S(2)}) collective-permute-start(f32[512,3584]{1,0:T(8,128)S(1)} %shard_map.40), channel_id=1, source_target_pairs={{0,1},{1,0},{2,3},{3,2},{4,5},{5,4},{6,7},{7,6},{8,9},{9,8},{10,11... | collective-permute-start | bytes 22020104 | tf_op jit(solution)/shard_map/ppermute | solution.py:241
  118.1 29.1 %collective-permute-start.30 = (bf16[256,2048]{1,0:T(8,128)(2,1)S(1)}, bf16[256,2048]{1,0:T(8,128)(2,1)S(1)}, u32[]{:S(2)}, u32[]{:S(2)}) collective-permute-start(bf16[256,2048]{1,0:T(8,128)(2,1)S(1)} %pad_maximum_fusion), channel_id=1, source_target_pairs={{0,126},{2,0},{4,2},{6,4},{8,6},{10,8},{12,10},{14,12},{16,14},{18... | collective-permute-start | bytes 3145736 | tf_op jit(solution)/shard_map/ppermute | solution.py:329
  123.0 24.3 %collective-permute-start.31 = (f32[384,512]{1,0:T(8,128)S(1)}, f32[384,512]{1,0:T(8,128)S(1)}, u32[]{:S(2)}, u32[]{:S(2)}) collective-permute-start(f32[384,512]{1,0:T(8,128)S(1)} %shard_map.39), channel_id=1, source_target_pairs={{0,2},{2,4},{4,6},{6,8},{8,10},{10,12},{12,14},{14,16},{16,18},{18... | collective-permute-start | bytes 2359304 | tf_op jit(solution)/shard_map/ppermute | solution.py:328
  125.3 4.6 %collective-permute-start.26 = (f32[128,768]{1,0:T(8,128)S(1)}, f32[128,768]{1,0:T(8,128)S(1)}, u32[]{:S(2)}, u32[]{:S(2)}) collective-permute-start(f32[128,768]{1,0:T(8,128)S(1)} %get-tuple-element.566), channel_id=1, source_target_pairs={{0,1},{1,0},{2,3},{3,2},{4,5},{5,4},{6,7},{7,6},{8,9},{9,8},{10,11... | collective-permute-start | bytes 1179656 | tf_op jit(solution)/shard_map/ppermute | solution.py:241
  125.7 4.8 %collective-permute-start.27 = (f32[128,768]{1,0:T(8,128)S(1)}, f32[128,768]{1,0:T(8,128)S(1)}, u32[]{:S(2)}, u32[]{:S(2)}) collective-permute-start(f32[128,768]{1,0:T(8,128)S(1)} %get-tuple-element.567), channel_id=1, source_target_pairs={{0,1},{1,0},{2,3},{3,2},{4,5},{5,4},{6,7},{7,6},{8,9},{9,8},{10,11... | collective-permute-start | bytes 1179656 | tf_op jit(solution)/shard_map/ppermute | solution.py:241
  132.8 31.3 %collective-permute-start.28 = (f32[256,768]{1,0:T(8,128)S(1)}, f32[256,768]{1,0:T(8,128)S(1)}, u32[]{:S(2)}, u32[]{:S(2)}) collective-permute-start(f32[256,768]{1,0:T(8,128)S(1)} %shard_map.42), channel_id=1, source_target_pairs={{0,2},{2,4},{4,6},{6,8},{8,10},{10,12},{12,14},{14,16},{16,18},{18... | collective-permute-start | bytes 2359304 | tf_op jit(solution)/shard_map/ppermute | solution.py:330
  148.0 3.4 %collective-permute-start.34 = (f32[512,256]{1,0:T(8,128)S(1)}, f32[512,256]{1,0:T(8,128)S(1)}, u32[]{:S(2)}, u32[]{:S(2)}) collective-permute-start(f32[512,256]{1,0:T(8,128)S(1)} %shard_map.47), channel_id=1, source_target_pairs={{0,1},{1,0},{2,3},{3,2},{4,5},{5,4},{6,7},{7,6},{8,9},{9,8},{10,11... | collective-permute-start | bytes 1572872 | tf_op jit(solution)/shard_map/ppermute | solution.py:241
  (8 other events, 45.0 us)

commit v2 on v1

--- a/solution.py
+++ b/solution.py
@@ -269,7 +269,9 @@
     def partners(*groups):
         return [part(k, j) for group in groups for k, j in group]
 
-    def make(group, into=None, room=None, offset=0):
+    def make(group, *others, into=None, room=None, offset=0):
+        for other in others:
+            make(other)
         into = into or group
         s["made"][into] = handed_products(
             s["handed"], partners(group), group, s["made"].get(into), room, offset
@@ -300,26 +302,31 @@
             mine(p + 2)
             x.append(fetch4(p + 2))
         if p == 1:
-            make(own, everything, room, places[0])
+            make(own, into=everything, room=room, offset=places[0])
         if p == 3:
-            make(ones, everything, room, places[1])
+            make(ones, into=everything, room=room, offset=places[1])
         if p == 5:
-            make(twos, everything, room, places[2])
+            make(twos, into=everything, room=room, offset=places[2])
         fence(x[p + 1])
         d.append(fetch1(p + 1))
         u.append(fetch3(p + 1))
         fence(d[p], u[p])
 
-    make(threes, everything, room, places[3])
+    make(threes, into=everything, room=room, offset=places[3])
     some = (0, 1, 2)
     early = [(some, n, (n, 0, 0, e), (0, 0, n * e, (2 + n) * e)) for n in range(2)]
     late = [((3,), n, (0, 0, n * e, (3 + n) * e), (0, 0, n * e, (3 + n) * e)) for n in range(3)]
     late += [((j,), 2, (1, 0, 2 * j * e, (2 * j + 1) * e), (0, e, 2 * j * e, (2 * j + 1) * e)) for j in some]
 
-    def ahead(blocks):
+    def ahead(blocks, *meanwhile):
         rows = [part(1, j) for j in range(1 + max(max(parts) for parts, *_ in blocks))]
         others = [part(3, j) for j in range(1 + max(n for _, n, *_ in blocks))]
         theirs = [swap(array) for array in relayed_products(s["where"], rows, others, blocks)]
+        if meanwhile:
+            make(*meanwhile)
+            fresh = {group: s["made"][group] for group in meanwhile}
+            theirs, fresh = lax.optimization_barrier((theirs, fresh))
+            s["made"].update(fresh)
         return relayed_products(s["where"], rows, others, blocks, theirs)[0]
 
     s["ahead"] = ahead(early)
@@ -327,10 +334,8 @@
 
     first_sums = lax.ppermute(s["ahead"], "blk", below(-1))
     relayed = lax.ppermute(jnp.concatenate(part(1, 3)), "blk", below(1))
-    last_sums = lax.ppermute(ahead(late), "blk", below(-1))
     third, fourth, fifth = ((1, 3),), ((3, 3),), ((2, 3),)
-    make(third)
-    make(fourth)
+    last_sums = lax.ppermute(ahead(late, third, fourth), "blk", below(-1))
     theirs = [swap(s["made"].pop(everything))]
     finish(theirs, own + ones)
     finish(theirs, twos + threes, offset=places[2])
@@ -338,13 +343,13 @@
     fence()
 
     make(fifth)
+    regions = [(0, n * 2 * e, 3 * e, 2 * e, 0, n * half) for n in range(2)]
+    s["out"] = scaled_write(s["out"], weights, s["sums"], 2, regions)
     theirs = [swap(s["made"].pop(group)) for group in (third, fourth, fifth)]
     finish(theirs, third, fourth, fifth)
-    regions = [(0, n * 2 * e, 3 * e, 2 * e, 0, n * half) for n in range(2)]
-    out = scaled_write(s["out"], weights, s["sums"], 2, regions)
     regions = [(0, n * 3 * e, e, 3 * e, 3 * e, n * half) for n in range(2)]
     regions += [(e, (2 * j + n) * e, e, e, j * e, n * half + 2 * e) for j in some for n in range(2)]
-    out = scaled_write(out, weights, last_sums, 2, regions)
+    out = scaled_write(s["out"], weights, last_sums, 2, regions)
     return out[None]
 
 

time: 166 us -> 166 us (level)
    ppermute x8, waiting for transfers between devices: 7.07 us -> 4.08 us  [swap(): return lax.ppermute(array, 'col', [(0, 1), (1, 0)])]
  transfers between devices with their start and end apart: 35 -> 35, of which waited for: 17 -> 16; matrix products, arithmetic and copies ran while one was open for 4% -> 4% of each run, Pallas kernels for 22% -> 22%
where the time goes in v2:
time: 166 us
  starting transfers between devices  79 us (48%)
  Pallas kernels  38.1 us (23%)
  waiting for transfers between devices  35.1 us (21%)
  local copies, waits for them, and re-layouts  10.3 us (6%)
  other arithmetic  2.82 us (2%)
    ppermute x8, starting transfers between devices, fetch4(): return ((4, p), lax.ppermute(s['held'][0, p], 'blk', below(4)))  40.1 us
    ppermute x8, starting transfers between devices, fetch1(): return ((1, p), lax.ppermute(send, 'blk', around(-1)))  19.7 us
    pallas_call x3, Pallas kernels, kept_products(): pl.pallas_call(kernel, out_shape=jax.ShapeDtypeStruct((5, half, 2 * half)...  15.7 us
    ppermute x8, waiting for transfers between devices, fetch3(): return ((3, p), lax.ppermute(send, 'blk', around(1)))  15.5 us
    ppermute x8, starting transfers between devices, swap(): return lax.ppermute(array, 'col', [(0, 1), (1, 0)])  12.7 us
    pallas_call x7, Pallas kernels, handed_products(): pl.pallas_call(kernel, out_shape=jax.ShapeDtypeStruct((half, room), jnp.f...  11.2 us
    ppermute x1, waiting for transfers between devices, body(): last_sums = lax.ppermute(ahead(late, third, fourth), 'blk', below(-1))  7.79 us
    pallas_call x4, Pallas kernels, relayed_products(): pl.pallas_call(kernel, out_shape=[jax.ShapeDtypeStruct(sizes[n], jnp.floa...  7.12 us
  transfers between devices with their start and end apart: 35, of which 16 were waited for; matrix products, arithmetic and copies ran while one was open for 4% of the time, Pallas kernels for 22%

profile of v2, /device:TPU:1, one launch (start us, length us, event | category | flops | bytes accessed | tf_op | source)
XLA Modules:
  0.0 165.8 jit_solution(15623581845763007013)
XLA Ops:
  1.9 6.8 %collective-permute-start = (bf16[128,2048]{1,0:T(8,128)(2,1)}, bf16[128,2048]{1,0:T(8,128)(2,1)S(1)}, u32[]{:S(2)}, u32[]{:S(2)}) collective-permute-start(bf16[128,2048]{1,0:T(8,128)(2,1)} %slice.3), channel_id=1, source_target_pairs={{0,120},{2,122},{4,124},{6,126},{8,0},{10,2},{12,4},{14,6},{16,8},... | collective-permute-start | bytes 1572872 | tf_op jit(solution)/shard_map/ppermute | solution.py:254
  12.4 4.0 %constant_dynamic-slice_fusion = (bf16[512,2048]{1,0:T(8,128)(2,1)}, bf16[512,2048]{1,0:T(8,128)(2,1)S(1)}) fusion(bf16[1024,2048]{1,0:T(8,128)(2,1)} %refs_1_.1, s32[]{:T(128)S(6)} %select_n.84, s32[]{:T(128)S(6)} %select_n.83), kind=kLoop, calls=%fused_computation.18 | loop fusion | bytes 8388616 | tf_op jit(solution)/shard_map/dynamic_slice | solution.py:294
  16.3 3.2 %collective-permute-done.refs_0_.refs_2_ = bf16[128,2048]{1,0:T(8,128)(2,1)S(1)} collective-permute-done((bf16[128,2048]{1,0:T(8,128)(2,1)}, bf16[128,2048]{1,0:T(8,128)(2,1)S(1)}, u32[]{:S(2)}, u32[]{:S(2)}) %collective-permute-start) | collective-permute-done | bytes 524320 | tf_op jit(solution)/shard_map/ppermute | solution.py:254
  20.7 2.8 %collective-permute-start.2 = (bf16[128,2048]{1,0:T(8,128)(2,1)S(1)}, bf16[128,2048]{1,0:T(8,128)(2,1)S(1)}, u32[]{:S(2)}, u32[]{:S(2)}) collective-permute-start(bf16[128,2048]{1,0:T(8,128)(2,1)S(1)} %get-tuple-element.618), channel_id=1, source_target_pairs={{0,6},{2,0},{4,2},{6,4},{8,14},{10,8},{12,10},{14,12},{16,22},{18,... | collective-permute-start | bytes 1572872 | tf_op jit(solution)/shard_map/ppermute | solution.py:258
  25.7 5.5 %collective-permute-start.4 = (bf16[128,2048]{1,0:T(8,128)(2,1)S(1)}, bf16[128,2048]{1,0:T(8,128)(2,1)S(1)}, u32[]{:S(2)}, u32[]{:S(2)}) collective-permute-start(bf16[128,2048]{1,0:T(8,128)(2,1)S(1)} %shard_map.29), channel_id=1, source_target_pairs={{0,120},{2,122},{4,124},{6,126},{8,0},{10,2},{12,4},{14,6},{16,8},... | collective-permute-start | bytes 1572872 | tf_op jit(solution)/shard_map/ppermute | solution.py:254
  32.4 2.7 %collective-permute-start.5 = (bf16[128,2048]{1,0:T(8,128)(2,1)S(1)}, bf16[128,2048]{1,0:T(8,128)(2,1)S(1)}, u32[]{:S(2)}, u32[]{:S(2)}) collective-permute-start(bf16[128,2048]{1,0:T(8,128)(2,1)S(1)} %get-tuple-element.616), channel_id=1, source_target_pairs={{0,6},{2,0},{4,2},{6,4},{8,14},{10,8},{12,10},{14,12},{16,22},{18,... | collective-permute-start | bytes 1572872 | tf_op jit(solution)/shard_map/ppermute | solution.py:258
  35.2 5.5 %collective-permute-start.7 = (bf16[128,2048]{1,0:T(8,128)(2,1)S(1)}, bf16[128,2048]{1,0:T(8,128)(2,1)S(1)}, u32[]{:S(2)}, u32[]{:S(2)}) collective-permute-start(bf16[128,2048]{1,0:T(8,128)(2,1)S(1)} %shard_map.30), channel_id=1, source_target_pairs={{0,120},{2,122},{4,124},{6,126},{8,0},{10,2},{12,4},{14,6},{16,8},... | collective-permute-start | bytes 1572872 | tf_op jit(solution)/shard_map/ppermute | solution.py:254
  40.7 3.0 %shard_map.31.refs_8_ = f32[512,3584]{1,0:T(8,128)S(1)} custom-call(bf16[512,2048]{1,0:T(8,128)(2,1)S(1)} %get-tuple-element.593.handed_ref, bf16[1024,2048]{1,0:T(8,128)(2,1)S(1)} %copy-done.2), custom_call_target="tpu_custom_call" | custom-call | flops 1 | bytes 1 | tf_op jit(solution)/shard_map/pallas_call | solution.py:96
  43.8 2.3 %collective-permute-start.8 = (bf16[128,2048]{1,0:T(8,128)(2,1)S(1)}, bf16[128,2048]{1,0:T(8,128)(2,1)S(1)}, u32[]{:S(2)}, u32[]{:S(2)}) collective-permute-start(bf16[128,2048]{1,0:T(8,128)(2,1)S(1)} %get-tuple-element.614), channel_id=1, source_target_pairs={{0,6},{2,0},{4,2},{6,4},{8,14},{10,8},{12,10},{14,12},{16,22},{18,... | collective-permute-start | bytes 1572872 | tf_op jit(solution)/shard_map/ppermute | solution.py:258
  46.2 6.8 %collective-permute-start.10 = (bf16[128,2048]{1,0:T(8,128)(2,1)S(1)}, bf16[128,2048]{1,0:T(8,128)(2,1)S(1)}, u32[]{:S(2)}, u32[]{:S(2)}) collective-permute-start(bf16[128,2048]{1,0:T(8,128)(2,1)S(1)} %shard_map.32), channel_id=1, source_target_pairs={{0,120},{2,122},{4,124},{6,126},{8,0},{10,2},{12,4},{14,6},{16,8},... | collective-permute-start | bytes 1572872 | tf_op jit(solution)/shard_map/ppermute | solution.py:254
  55.2 3.1 %collective-permute-done.9.refs_4_.refs_8_.refs_10_.refs_5_ = bf16[128,2048]{1,0:T(8,128)(2,1)S(1)} collective-permute-done((bf16[128,2048]{1,0:T(8,128)(2,1)S(1)}, bf16[128,2048]{1,0:T(8,128)(2,1)S(1)}, u32[]{:S(2)}, u32[]{:S(2)}) %collective-permute-start.9) | collective-permute-done | bytes 524320 | tf_op jit(solution)/shard_map/ppermute | solution.py:262
  58.4 4.7 %collective-permute-start.13 = (bf16[128,2048]{1,0:T(8,128)(2,1)S(1)}, bf16[128,2048]{1,0:T(8,128)(2,1)S(1)}, u32[]{:S(2)}, u32[]{:S(2)}) collective-permute-start(bf16[128,2048]{1,0:T(8,128)(2,1)S(1)} %shard_map.33), channel_id=1, source_target_pairs={{0,120},{2,122},{4,124},{6,126},{8,0},{10,2},{12,4},{14,6},{16,8},... | collective-permute-start | bytes 1572872 | tf_op jit(solution)/shard_map/ppermute | solution.py:254
  63.1 2.4 %shard_map.34.refs_6_ = f32[512,3584]{1,0:T(8,128)S(1)} custom-call(bf16[512,2048]{1,0:T(8,128)(2,1)S(1)} %get-tuple-element.593.handed_ref, bf16[128,2048]{1,0:T(8,128)(2,1)S(1)} %collective-permute-done.refs_0_.refs_2_, bf16[128,2048]{1,0:T(8,128)(2,1)S(1)} %collective-permute-done.1.refs_1_.refs_3_, ...), custom_call_target="tpu_custom_call", output_to_operand_aliasing={{}: (9, {})} | custom-call | flops 1 | bytes 1 | tf_op jit(solution)/shard_map/pallas_call | solution.py:96
  67.1 2.5 %collective-permute-done.12.refs_5_.refs_9_.refs_11_.refs_6_ = bf16[128,2048]{1,0:T(8,128)(2,1)S(1)} collective-permute-done((bf16[128,2048]{1,0:T(8,128)(2,1)S(1)}, bf16[128,2048]{1,0:T(8,128)(2,1)S(1)}, u32[]{:S(2)}, u32[]{:S(2)}) %collective-permute-start.12) | collective-permute-done | bytes 524320 | tf_op jit(solution)/shard_map/ppermute | solution.py:262
  69.6 4.7 %collective-permute-start.16 = (bf16[128,2048]{1,0:T(8,128)(2,1)S(1)}, bf16[128,2048]{1,0:T(8,128)(2,1)S(1)}, u32[]{:S(2)}, u32[]{:S(2)}) collective-permute-start(bf16[128,2048]{1,0:T(8,128)(2,1)S(1)} %shard_map.35), channel_id=1, source_target_pairs={{0,120},{2,122},{4,124},{6,126},{8,0},{10,2},{12,4},{14,6},{16,8},... | collective-permute-start | bytes 1572872 | tf_op jit(solution)/shard_map/ppermute | solution.py:254
  74.4 3.0 %collective-permute-start.17 = (bf16[128,2048]{1,0:T(8,128)(2,1)S(1)}, bf16[128,2048]{1,0:T(8,128)(2,1)S(1)}, u32[]{:S(2)}, u32[]{:S(2)}) collective-permute-start(bf16[128,2048]{1,0:T(8,128)(2,1)S(1)} %get-tuple-element.608), channel_id=1, source_target_pairs={{0,6},{2,0},{4,2},{6,4},{8,14},{10,8},{12,10},{14,12},{16,22},{18,... | collective-permute-start | bytes 1572872 | tf_op jit(solution)/shard_map/ppermute | solution.py:258
  77.4 2.6 %collective-permute-done.15.refs_4_.refs_12_.refs_11_ = bf16[128,2048]{1,0:T(8,128)(2,1)S(1)} collective-permute-done((bf16[128,2048]{1,0:T(8,128)(2,1)S(1)}, bf16[128,2048]{1,0:T(8,128)(2,1)S(1)}, u32[]{:S(2)}, u32[]{:S(2)}) %collective-permute-start.15) | collective-permute-done | bytes 524320 | tf_op jit(solution)/shard_map/ppermute | solution.py:262
  80.0 5.7 %collective-permute-start.19 = (bf16[128,2048]{1,0:T(8,128)(2,1)S(1)}, bf16[128,2048]{1,0:T(8,128)(2,1)S(1)}, u32[]{:S(2)}, u32[]{:S(2)}) collective-permute-start(bf16[128,2048]{1,0:T(8,128)(2,1)S(1)} %shard_map.36), channel_id=1, source_target_pairs={{0,120},{2,122},{4,124},{6,126},{8,0},{10,2},{12,4},{14,6},{16,8},... | collective-permute-start | bytes 1572872 | tf_op jit(solution)/shard_map/ppermute | solution.py:254
  89.2 2.9 %collective-permute-done.18.refs_5_.refs_13_.refs_12_ = bf16[128,2048]{1,0:T(8,128)(2,1)S(1)} collective-permute-done((bf16[128,2048]{1,0:T(8,128)(2,1)S(1)}, bf16[128,2048]{1,0:T(8,128)(2,1)S(1)}, u32[]{:S(2)}, u32[]{:S(2)}) %collective-permute-start.18) | collective-permute-done | bytes 524320 | tf_op jit(solution)/shard_map/ppermute | solution.py:262
  92.1 2.4 %collective-permute-done.19.refs_1_.refs_8_ = bf16[128,2048]{1,0:T(8,128)(2,1)S(1)} collective-permute-done((bf16[128,2048]{1,0:T(8,128)(2,1)S(1)}, bf16[128,2048]{1,0:T(8,128)(2,1)S(1)}, u32[]{:S(2)}, u32[]{:S(2)}) %collective-permute-start.19) | collective-permute-done | bytes 524320 | tf_op jit(solution)/shard_map/ppermute | solution.py:254
  94.5 5.3 %collective-permute-start.24 = (bf16[128,2048]{1,0:T(8,128)(2,1)S(1)}, bf16[128,2048]{1,0:T(8,128)(2,1)S(1)}, u32[]{:S(2)}, u32[]{:S(2)}) collective-permute-start(bf16[128,2048]{1,0:T(8,128)(2,1)S(1)} %get-tuple-element.604), channel_id=1, source_target_pairs={{0,6},{2,0},{4,2},{6,4},{8,14},{10,8},{12,10},{14,12},{16,22},{18,... | collective-permute-start | bytes 1572872 | tf_op jit(solution)/shard_map/ppermute | solution.py:258
  99.9 2.9 %collective-permute-done.21.refs_0_.refs_5_ = bf16[128,2048]{1,0:T(8,128)(2,1)S(1)} collective-permute-done((bf16[128,2048]{1,0:T(8,128)(2,1)S(1)}, bf16[128,2048]{1,0:T(8,128)(2,1)S(1)}, u32[]{:S(2)}, u32[]{:S(2)}) %collective-permute-start.21) | collective-permute-done | bytes 524320 | tf_op jit(solution)/shard_map/ppermute | solution.py:262
  103.9 6.7 %collective-permute-start.22 = (f32[384,256]{1,0:T(8,128)S(1)}, f32[384,256]{1,0:T(8,128)S(1)}, u32[]{:S(2)}, u32[]{:S(2)}) collective-permute-start(f32[384,256]{1,0:T(8,128)S(1)} %get-tuple-element.538), channel_id=1, source_target_pairs={{0,1},{1,0},{2,3},{3,2},{4,5},{5,4},{6,7},{7,6},{8,9},{9,8},{10,11... | collective-permute-start | bytes 1179656 | tf_op jit(solution)/shard_map/ppermute | solution.py:241
  115.1 3.0 %collective-permute-start.29 = (f32[512,3584]{1,0:T(8,128)S(1)}, f32[512,3584]{1,0:T(8,128)S(1)}, u32[]{:S(2)}, u32[]{:S(2)}) collective-permute-start(f32[512,3584]{1,0:T(8,128)S(1)} %shard_map.40), channel_id=1, source_target_pairs={{0,1},{1,0},{2,3},{3,2},{4,5},{5,4},{6,7},{7,6},{8,9},{9,8},{10,11... | collective-permute-start | bytes 22020104 | tf_op jit(solution)/shard_map/ppermute | solution.py:241
  118.1 4.8 %collective-permute-start.30 = (bf16[256,2048]{1,0:T(8,128)(2,1)S(1)}, bf16[256,2048]{1,0:T(8,128)(2,1)S(1)}, u32[]{:S(2)}, u32[]{:S(2)}) collective-permute-start(bf16[256,2048]{1,0:T(8,128)(2,1)S(1)} %pad_maximum_fusion), channel_id=1, source_target_pairs={{0,126},{2,0},{4,2},{6,4},{8,6},{10,8},{12,10},{14,12},{16,14},{18... | collective-permute-start | bytes 3145736 | tf_op jit(solution)/shard_map/ppermute | solution.py:336
  123.0 2.3 %shard_map.41 = (f32[128,768]{1,0:T(8,128)S(1)}, f32[128,768]{1,0:T(8,128)S(1)}) custom-call(s32[1]{0:T(128)} %bitcast.1._.where_ref, bf16[128,2048]{1,0:T(8,128)(2,1)S(1)} %collective-permute-done.2.refs_4_.refs_0_.refs_6_, bf16[128,2048]{1,0:T(8,128)(2,1)S(1)} %collective-permute-done.5.refs_5_.refs_1_.refs_7_, ...), custom_call_target="tpu_custom_call" | custom-call | flops 1 | bytes 1 | tf_op jit(solution)/shard_map/pallas_call | solution.py:185
  127.4 2.5 %collective-permute-done.26.refs_14_ = f32[128,768]{1,0:T(8,128)S(1)} collective-permute-done((f32[128,768]{1,0:T(8,128)S(1)}, f32[128,768]{1,0:T(8,128)S(1)}, u32[]{:S(2)}, u32[]{:S(2)}) %collective-permute-start.26) | collective-permute-done | bytes 393248 | tf_op jit(solution)/shard_map/ppermute | solution.py:241
  130.5 2.6 %shard_map.44 = f32[256,768]{1,0:T(8,128)S(1)} custom-call(s32[1]{0:T(128)} %bitcast.1._.where_ref, bf16[128,2048]{1,0:T(8,128)(2,1)S(1)} %collective-permute-done.2.refs_4_.refs_0_.refs_6_, bf16[128,2048]{1,0:T(8,128)(2,1)S(1)} %collective-permute-done.5.refs_5_.refs_1_.refs_7_, bf16[128,2048]{1,0:T(8,128)(2,1)S(1)} %collective-permute-done.8.refs_2_.refs_3_, ...), custom_call_target="tpu_custom_call" | custom-call | flops 1 | bytes 1 | tf_op jit(solution)/shard_map/pallas_call | solution.py:185
  133.2 7.1 %shard_map.45.refs_13_ = f32[5,512,1024]{2,1,0:T(8,128)} custom-call(f32[5]{0:T(128)S(1)} %pad_maximum_fusion.1.weights_ref, bf16[512,2048]{1,0:T(8,128)(2,1)S(1)} %copy-done.3, f32[512,3584]{1,0:T(8,128)S(1)} %collective-permute-done.29.refs_0_, bf16[1024,2048]{1,0:T(8,128)(2,1)S(1)} %copy-done.2, ...), custom_call_target="tpu_custom_call" | custom-call | flops 1 | bytes 1 | tf_op jit(solution)/shard_map/pallas_call | solution.py:139
  140.3 5.2 %shard_map.46._ = f32[5,512,1024]{2,1,0:T(8,128)} custom-call(f32[5]{0:T(128)S(1)} %pad_maximum_fusion.1.weights_ref, bf16[512,2048]{1,0:T(8,128)(2,1)S(1)} %copy-done.3, f32[512,3584]{1,0:T(8,128)S(1)} %collective-permute-done.29.refs_0_, bf16[128,2048]{1,0:T(8,128)(2,1)S(1)} %collective-permute-done.10.refs_0_.refs_1_, ...), custom_call_target="tpu_custom_call", output_to_operand_aliasing={{}: (15, {})} | custom-call | flops 1 | bytes 1 | tf_op jit(solution)/shard_map/pallas_call | solution.py:139
  152.9 3.4 %shard_map.49._ = f32[5,512,1024]{2,1,0:T(8,128)} custom-call(f32[5]{0:T(128)S(1)} %pad_maximum_fusion.1.weights_ref, bf16[512,2048]{1,0:T(8,128)(2,1)S(1)} %copy-done.3, f32[512,256]{1,0:T(8,128)S(1)} %collective-permute-done.32.refs_0_, f32[512,256]{1,0:T(8,128)S(1)} %collective-permute-done.33.refs_1_, ...), custom_call_target="tpu_custom_call", output_to_operand_aliasing={{}: (10, {})} | custom-call | flops 1 | bytes 1 | tf_op jit(solution)/shard_map/pallas_call | solution.py:139
  156.3 7.8 %collective-permute-done.28.summed_ref = f32[256,768]{1,0:T(8,128)S(1)} collective-permute-done((f32[256,768]{1,0:T(8,128)S(1)}, f32[256,768]{1,0:T(8,128)S(1)}, u32[]{:S(2)}, u32[]{:S(2)}) %collective-permute-start.28) | collective-permute-done | bytes 786464 | tf_op jit(solution)/shard_map/ppermute | solution.py:338
  (84 shorter events, 35.2 us)
Async XLA Ops:
  1.9 17.7 %collective-permute-start = (bf16[128,2048]{1,0:T(8,128)(2,1)}, bf16[128,2048]{1,0:T(8,128)(2,1)S(1)}, u32[]{:S(2)}, u32[]{:S(2)}) collective-permute-start(bf16[128,2048]{1,0:T(8,128)(2,1)} %slice.3), channel_id=1, source_target_pairs={{0,120},{2,122},{4,124},{6,126},{8,0},{10,2},{12,4},{14,6},{16,8},... | collective-permute-start | bytes 1572872 | tf_op jit(solution)/shard_map/ppermute | solution.py:254
  11.7 19.5 %collective-permute-start.1 = (bf16[128,2048]{1,0:T(8,128)(2,1)}, bf16[128,2048]{1,0:T(8,128)(2,1)S(1)}, u32[]{:S(2)}, u32[]{:S(2)}) collective-permute-start(bf16[128,2048]{1,0:T(8,128)(2,1)} %shard_map.28), channel_id=1, source_target_pairs={{0,120},{2,122},{4,124},{6,126},{8,0},{10,2},{12,4},{14,6},{16,8},... | collective-permute-start | bytes 1572872 | tf_op jit(solution)/shard_map/ppermute | solution.py:254
  20.7 14.4 %collective-permute-start.2 = (bf16[128,2048]{1,0:T(8,128)(2,1)S(1)}, bf16[128,2048]{1,0:T(8,128)(2,1)S(1)}, u32[]{:S(2)}, u32[]{:S(2)}) collective-permute-start(bf16[128,2048]{1,0:T(8,128)(2,1)S(1)} %get-tuple-element.618), channel_id=1, source_target_pairs={{0,6},{2,0},{4,2},{6,4},{8,14},{10,8},{12,10},{14,12},{16,22},{18,... | collective-permute-start | bytes 1572872 | tf_op jit(solution)/shard_map/ppermute | solution.py:258
  23.5 11.7 %collective-permute-start.3 = (bf16[128,2048]{1,0:T(8,128)(2,1)S(1)}, bf16[128,2048]{1,0:T(8,128)(2,1)S(1)}, u32[]{:S(2)}, u32[]{:S(2)}) collective-permute-start(bf16[128,2048]{1,0:T(8,128)(2,1)S(1)} %get-tuple-element.617), channel_id=1, source_target_pairs={{0,2},{2,4},{4,6},{6,0},{8,10},{10,12},{12,14},{14,8},{16,18},{18,... | collective-permute-start | bytes 1572872 | tf_op jit(solution)/shard_map/ppermute | solution.py:262
  25.7 17.9 %collective-permute-start.4 = (bf16[128,2048]{1,0:T(8,128)(2,1)S(1)}, bf16[128,2048]{1,0:T(8,128)(2,1)S(1)}, u32[]{:S(2)}, u32[]{:S(2)}) collective-permute-start(bf16[128,2048]{1,0:T(8,128)(2,1)S(1)} %shard_map.29), channel_id=1, source_target_pairs={{0,120},{2,122},{4,124},{6,126},{8,0},{10,2},{12,4},{14,6},{16,8},... | collective-permute-start | bytes 1572872 | tf_op jit(solution)/shard_map/ppermute | solution.py:254
  32.4 13.8 %collective-permute-start.5 = (bf16[128,2048]{1,0:T(8,128)(2,1)S(1)}, bf16[128,2048]{1,0:T(8,128)(2,1)S(1)}, u32[]{:S(2)}, u32[]{:S(2)}) collective-permute-start(bf16[128,2048]{1,0:T(8,128)(2,1)S(1)} %get-tuple-element.616), channel_id=1, source_target_pairs={{0,6},{2,0},{4,2},{6,4},{8,14},{10,8},{12,10},{14,12},{16,22},{18,... | collective-permute-start | bytes 1572872 | tf_op jit(solution)/shard_map/ppermute | solution.py:258
  35.1 11.0 %collective-permute-start.6 = (bf16[128,2048]{1,0:T(8,128)(2,1)S(1)}, bf16[128,2048]{1,0:T(8,128)(2,1)S(1)}, u32[]{:S(2)}, u32[]{:S(2)}) collective-permute-start(bf16[128,2048]{1,0:T(8,128)(2,1)S(1)} %get-tuple-element.615), channel_id=1, source_target_pairs={{0,2},{2,4},{4,6},{6,0},{8,10},{10,12},{12,14},{14,8},{16,18},{18,... | collective-permute-start | bytes 1572872 | tf_op jit(solution)/shard_map/ppermute | solution.py:262
  35.2 17.7 %collective-permute-start.7 = (bf16[128,2048]{1,0:T(8,128)(2,1)S(1)}, bf16[128,2048]{1,0:T(8,128)(2,1)S(1)}, u32[]{:S(2)}, u32[]{:S(2)}) collective-permute-start(bf16[128,2048]{1,0:T(8,128)(2,1)S(1)} %shard_map.30), channel_id=1, source_target_pairs={{0,120},{2,122},{4,124},{6,126},{8,0},{10,2},{12,4},{14,6},{16,8},... | collective-permute-start | bytes 1572872 | tf_op jit(solution)/shard_map/ppermute | solution.py:254
  43.8 11.4 %collective-permute-start.8 = (bf16[128,2048]{1,0:T(8,128)(2,1)S(1)}, bf16[128,2048]{1,0:T(8,128)(2,1)S(1)}, u32[]{:S(2)}, u32[]{:S(2)}) collective-permute-start(bf16[128,2048]{1,0:T(8,128)(2,1)S(1)} %get-tuple-element.614), channel_id=1, source_target_pairs={{0,6},{2,0},{4,2},{6,4},{8,14},{10,8},{12,10},{14,12},{16,22},{18,... | collective-permute-start | bytes 1572872 | tf_op jit(solution)/shard_map/ppermute | solution.py:258
  46.1 12.2 %collective-permute-start.9 = (bf16[128,2048]{1,0:T(8,128)(2,1)S(1)}, bf16[128,2048]{1,0:T(8,128)(2,1)S(1)}, u32[]{:S(2)}, u32[]{:S(2)}) collective-permute-start(bf16[128,2048]{1,0:T(8,128)(2,1)S(1)} %get-tuple-element.613), channel_id=1, source_target_pairs={{0,2},{2,4},{4,6},{6,0},{8,10},{10,12},{12,14},{14,8},{16,18},{18,... | collective-permute-start | bytes 1572872 | tf_op jit(solution)/shard_map/ppermute | solution.py:262
  46.2 19.2 %collective-permute-start.10 = (bf16[128,2048]{1,0:T(8,128)(2,1)S(1)}, bf16[128,2048]{1,0:T(8,128)(2,1)S(1)}, u32[]{:S(2)}, u32[]{:S(2)}) collective-permute-start(bf16[128,2048]{1,0:T(8,128)(2,1)S(1)} %shard_map.32), channel_id=1, source_target_pairs={{0,120},{2,122},{4,124},{6,126},{8,0},{10,2},{12,4},{14,6},{16,8},... | collective-permute-start | bytes 1572872 | tf_op jit(solution)/shard_map/ppermute | solution.py:254
  53.0 14.0 %collective-permute-start.11 = (bf16[128,2048]{1,0:T(8,128)(2,1)S(1)}, bf16[128,2048]{1,0:T(8,128)(2,1)S(1)}, u32[]{:S(2)}, u32[]{:S(2)}) collective-permute-start(bf16[128,2048]{1,0:T(8,128)(2,1)S(1)} %get-tuple-element.612), channel_id=1, source_target_pairs={{0,6},{2,0},{4,2},{6,4},{8,14},{10,8},{12,10},{14,12},{16,22},{18,... | collective-permute-start | bytes 1572872 | tf_op jit(solution)/shard_map/ppermute | solution.py:258
  54.9 14.7 %collective-permute-start.12 = (bf16[128,2048]{1,0:T(8,128)(2,1)S(1)}, bf16[128,2048]{1,0:T(8,128)(2,1)S(1)}, u32[]{:S(2)}, u32[]{:S(2)}) collective-permute-start(bf16[128,2048]{1,0:T(8,128)(2,1)S(1)} %get-tuple-element.611), channel_id=1, source_target_pairs={{0,2},{2,4},{4,6},{6,0},{8,10},{10,12},{12,14},{14,8},{16,18},{18,... | collective-permute-start | bytes 1572872 | tf_op jit(solution)/shard_map/ppermute | solution.py:262
  58.4 15.9 %collective-permute-start.13 = (bf16[128,2048]{1,0:T(8,128)(2,1)S(1)}, bf16[128,2048]{1,0:T(8,128)(2,1)S(1)}, u32[]{:S(2)}, u32[]{:S(2)}) collective-permute-start(bf16[128,2048]{1,0:T(8,128)(2,1)S(1)} %shard_map.33), channel_id=1, source_target_pairs={{0,120},{2,122},{4,124},{6,126},{8,0},{10,2},{12,4},{14,6},{16,8},... | collective-permute-start | bytes 1572872 | tf_op jit(solution)/shard_map/ppermute | solution.py:254
  65.5 11.9 %collective-permute-start.14 = (bf16[128,2048]{1,0:T(8,128)(2,1)S(1)}, bf16[128,2048]{1,0:T(8,128)(2,1)S(1)}, u32[]{:S(2)}, u32[]{:S(2)}) collective-permute-start(bf16[128,2048]{1,0:T(8,128)(2,1)S(1)} %get-tuple-element.610), channel_id=1, source_target_pairs={{0,6},{2,0},{4,2},{6,4},{8,14},{10,8},{12,10},{14,12},{16,22},{18,... | collective-permute-start | bytes 1572872 | tf_op jit(solution)/shard_map/ppermute | solution.py:258
  66.2 13.8 %collective-permute-start.15 = (bf16[128,2048]{1,0:T(8,128)(2,1)S(1)}, bf16[128,2048]{1,0:T(8,128)(2,1)S(1)}, u32[]{:S(2)}, u32[]{:S(2)}) collective-permute-start(bf16[128,2048]{1,0:T(8,128)(2,1)S(1)} %get-tuple-element.609), channel_id=1, source_target_pairs={{0,2},{2,4},{4,6},{6,0},{8,10},{10,12},{12,14},{14,8},{16,18},{18,... | collective-permute-start | bytes 1572872 | tf_op jit(solution)/shard_map/ppermute | solution.py:262
  69.6 17.9 %collective-permute-start.16 = (bf16[128,2048]{1,0:T(8,128)(2,1)S(1)}, bf16[128,2048]{1,0:T(8,128)(2,1)S(1)}, u32[]{:S(2)}, u32[]{:S(2)}) collective-permute-start(bf16[128,2048]{1,0:T(8,128)(2,1)S(1)} %shard_map.35), channel_id=1, source_target_pairs={{0,120},{2,122},{4,124},{6,126},{8,0},{10,2},{12,4},{14,6},{16,8},... | collective-permute-start | bytes 1572872 | tf_op jit(solution)/shard_map/ppermute | solution.py:254
  74.4 14.8 %collective-permute-start.17 = (bf16[128,2048]{1,0:T(8,128)(2,1)S(1)}, bf16[128,2048]{1,0:T(8,128)(2,1)S(1)}, u32[]{:S(2)}, u32[]{:S(2)}) collective-permute-start(bf16[128,2048]{1,0:T(8,128)(2,1)S(1)} %get-tuple-element.608), channel_id=1, source_target_pairs={{0,6},{2,0},{4,2},{6,4},{8,14},{10,8},{12,10},{14,12},{16,22},{18,... | collective-permute-start | bytes 1572872 | tf_op jit(solution)/shard_map/ppermute | solution.py:258
  77.4 14.7 %collective-permute-start.18 = (bf16[128,2048]{1,0:T(8,128)(2,1)S(1)}, bf16[128,2048]{1,0:T(8,128)(2,1)S(1)}, u32[]{:S(2)}, u32[]{:S(2)}) collective-permute-start(bf16[128,2048]{1,0:T(8,128)(2,1)S(1)} %get-tuple-element.607), channel_id=1, source_target_pairs={{0,2},{2,4},{4,6},{6,0},{8,10},{10,12},{12,14},{14,8},{16,18},{18,... | collective-permute-start | bytes 1572872 | tf_op jit(solution)/shard_map/ppermute | solution.py:262
  80.0 14.4 %collective-permute-start.19 = (bf16[128,2048]{1,0:T(8,128)(2,1)S(1)}, bf16[128,2048]{1,0:T(8,128)(2,1)S(1)}, u32[]{:S(2)}, u32[]{:S(2)}) collective-permute-start(bf16[128,2048]{1,0:T(8,128)(2,1)S(1)} %shard_map.36), channel_id=1, source_target_pairs={{0,120},{2,122},{4,124},{6,126},{8,0},{10,2},{12,4},{14,6},{16,8},... | collective-permute-start | bytes 1572872 | tf_op jit(solution)/shard_map/ppermute | solution.py:254
  87.6 12.2 %collective-permute-start.20 = (bf16[128,2048]{1,0:T(8,128)(2,1)S(1)}, bf16[128,2048]{1,0:T(8,128)(2,1)S(1)}, u32[]{:S(2)}, u32[]{:S(2)}) collective-permute-start(bf16[128,2048]{1,0:T(8,128)(2,1)S(1)} %get-tuple-element.606), channel_id=1, source_target_pairs={{0,6},{2,0},{4,2},{6,4},{8,14},{10,8},{12,10},{14,12},{16,22},{18,... | collective-permute-start | bytes 1572872 | tf_op jit(solution)/shard_map/ppermute | solution.py:258
  88.6 14.2 %collective-permute-start.21 = (bf16[128,2048]{1,0:T(8,128)(2,1)S(1)}, bf16[128,2048]{1,0:T(8,128)(2,1)S(1)}, u32[]{:S(2)}, u32[]{:S(2)}) collective-permute-start(bf16[128,2048]{1,0:T(8,128)(2,1)S(1)} %get-tuple-element.605), channel_id=1, source_target_pairs={{0,2},{2,4},{4,6},{6,0},{8,10},{10,12},{12,14},{14,8},{16,18},{18,... | collective-permute-start | bytes 1572872 | tf_op jit(solution)/shard_map/ppermute | solution.py:262
  94.5 19.1 %collective-permute-start.24 = (bf16[128,2048]{1,0:T(8,128)(2,1)S(1)}, bf16[128,2048]{1,0:T(8,128)(2,1)S(1)}, u32[]{:S(2)}, u32[]{:S(2)}) collective-permute-start(bf16[128,2048]{1,0:T(8,128)(2,1)S(1)} %get-tuple-element.604), channel_id=1, source_target_pairs={{0,6},{2,0},{4,2},{6,4},{8,14},{10,8},{12,10},{14,12},{16,22},{18,... | collective-permute-start | bytes 1572872 | tf_op jit(solution)/shard_map/ppermute | solution.py:258
  99.9 15.2 %collective-permute-start.25 = (bf16[128,2048]{1,0:T(8,128)(2,1)S(1)}, bf16[128,2048]{1,0:T(8,128)(2,1)S(1)}, u32[]{:S(2)}, u32[]{:S(2)}) collective-permute-start(bf16[128,2048]{1,0:T(8,128)(2,1)S(1)} %get-tuple-element.603), channel_id=1, source_target_pairs={{0,2},{2,4},{4,6},{6,0},{8,10},{10,12},{12,14},{14,8},{16,18},{18,... | collective-permute-start | bytes 1572872 | tf_op jit(solution)/shard_map/ppermute | solution.py:262
  103.9 8.6 %collective-permute-start.22 = (f32[384,256]{1,0:T(8,128)S(1)}, f32[384,256]{1,0:T(8,128)S(1)}, u32[]{:S(2)}, u32[]{:S(2)}) collective-permute-start(f32[384,256]{1,0:T(8,128)S(1)} %get-tuple-element.538), channel_id=1, source_target_pairs={{0,1},{1,0},{2,3},{3,2},{4,5},{5,4},{6,7},{7,6},{8,9},{9,8},{10,11... | collective-permute-start | bytes 1179656 | tf_op jit(solution)/shard_map/ppermute | solution.py:241
  115.1 18.1 %collective-permute-start.29 = (f32[512,3584]{1,0:T(8,128)S(1)}, f32[512,3584]{1,0:T(8,128)S(1)}, u32[]{:S(2)}, u32[]{:S(2)}) collective-permute-start(f32[512,3584]{1,0:T(8,128)S(1)} %shard_map.40), channel_id=1, source_target_pairs={{0,1},{1,0},{2,3},{3,2},{4,5},{5,4},{6,7},{7,6},{8,9},{9,8},{10,11... | collective-permute-start | bytes 22020104 | tf_op jit(solution)/shard_map/ppermute | solution.py:241
  118.1 29.1 %collective-permute-start.30 = (bf16[256,2048]{1,0:T(8,128)(2,1)S(1)}, bf16[256,2048]{1,0:T(8,128)(2,1)S(1)}, u32[]{:S(2)}, u32[]{:S(2)}) collective-permute-start(bf16[256,2048]{1,0:T(8,128)(2,1)S(1)} %pad_maximum_fusion), channel_id=1, source_target_pairs={{0,126},{2,0},{4,2},{6,4},{8,6},{10,8},{12,10},{14,12},{16,14},{18... | collective-permute-start | bytes 3145736 | tf_op jit(solution)/shard_map/ppermute | solution.py:336
  123.0 24.3 %collective-permute-start.31 = (f32[384,512]{1,0:T(8,128)S(1)}, f32[384,512]{1,0:T(8,128)S(1)}, u32[]{:S(2)}, u32[]{:S(2)}) collective-permute-start(f32[384,512]{1,0:T(8,128)S(1)} %shard_map.39), channel_id=1, source_target_pairs={{0,2},{2,4},{4,6},{6,8},{8,10},{10,12},{12,14},{14,16},{16,18},{18... | collective-permute-start | bytes 2359304 | tf_op jit(solution)/shard_map/ppermute | solution.py:335
  125.3 4.6 %collective-permute-start.26 = (f32[128,768]{1,0:T(8,128)S(1)}, f32[128,768]{1,0:T(8,128)S(1)}, u32[]{:S(2)}, u32[]{:S(2)}) collective-permute-start(f32[128,768]{1,0:T(8,128)S(1)} %get-tuple-element.570), channel_id=1, source_target_pairs={{0,1},{1,0},{2,3},{3,2},{4,5},{5,4},{6,7},{7,6},{8,9},{9,8},{10,11... | collective-permute-start | bytes 1179656 | tf_op jit(solution)/shard_map/ppermute | solution.py:241
  125.7 4.8 %collective-permute-start.27 = (f32[128,768]{1,0:T(8,128)S(1)}, f32[128,768]{1,0:T(8,128)S(1)}, u32[]{:S(2)}, u32[]{:S(2)}) collective-permute-start(f32[128,768]{1,0:T(8,128)S(1)} %get-tuple-element.571), channel_id=1, source_target_pairs={{0,1},{1,0},{2,3},{3,2},{4,5},{5,4},{6,7},{7,6},{8,9},{9,8},{10,11... | collective-permute-start | bytes 1179656 | tf_op jit(solution)/shard_map/ppermute | solution.py:241
  133.0 31.1 %collective-permute-start.28 = (f32[256,768]{1,0:T(8,128)S(1)}, f32[256,768]{1,0:T(8,128)S(1)}, u32[]{:S(2)}, u32[]{:S(2)}) collective-permute-start(f32[256,768]{1,0:T(8,128)S(1)} %shard_map.44), channel_id=1, source_target_pairs={{0,2},{2,4},{4,6},{6,8},{8,10},{10,12},{12,14},{14,16},{16,18},{18... | collective-permute-start | bytes 2359304 | tf_op jit(solution)/shard_map/ppermute | solution.py:338
  148.0 3.9 %collective-permute-start.34 = (f32[512,256]{1,0:T(8,128)S(1)}, f32[512,256]{1,0:T(8,128)S(1)}, u32[]{:S(2)}, u32[]{:S(2)}) collective-permute-start(f32[512,256]{1,0:T(8,128)S(1)} %shard_map.47), channel_id=1, source_target_pairs={{0,1},{1,0},{2,3},{3,2},{4,5},{5,4},{6,7},{7,6},{8,9},{9,8},{10,11... | collective-permute-start | bytes 1572872 | tf_op jit(solution)/shard_map/ppermute | solution.py:241
  (8 other events, 36.0 us)

commit v3 on v2

--- a/solution.py
+++ b/solution.py
@@ -44,6 +44,28 @@
         compiler_params=LIMIT,
         cost_estimate=SMALL,
     )(after, own)
+
+
+def rows_to_send(place, received, mine):
+    def kernel(place_ref, received_ref, mine_ref, down_ref, up_ref, sems):
+        def send(chosen, to_ref, n, act):
+            for ref, use in ((received_ref, chosen), (mine_ref, jnp.logical_not(chosen))):
+                pl.when(use)(lambda ref=ref: act(pltpu.make_async_copy(ref, to_ref, sems.at[n])))
+
+        passed_down, passed_up = place_ref[0] == 0, place_ref[0] != RING - 1
+        for act in (lambda copy: copy.start(), lambda copy: copy.wait()):
+            send(passed_down, down_ref, 0, act)
+            send(passed_up, up_ref, 1, act)
+
+    return pl.pallas_call(
+        kernel,
+        out_shape=[jax.ShapeDtypeStruct(mine.shape, mine.dtype)] * 2,
+        in_specs=[SMEM, ANY, ANY],
+        out_specs=[HBM, HBM],
+        scratch_shapes=[pltpu.SemaphoreType.DMA((2,))],
+        compiler_params=LIMIT,
+        cost_estimate=SMALL,
+    )(place, received, mine)
 
 
 def columns(group, half):
@@ -240,7 +262,8 @@
     def swap(array):
         return lax.ppermute(array, "col", [(0, 1), (1, 0)])
 
-    s = dict(where=core.astype(jnp.int32)[None], held={}, made={}, out=None)
+    place = column.astype(jnp.int32)[None]
+    s = dict(where=core.astype(jnp.int32)[None], place=place, held={}, made={}, out=None)
 
     def fence(*arrived):
         s["held"].update(arrived)
@@ -253,13 +276,10 @@
     def fetch4(p):
         return (4, p), lax.ppermute(s["held"][0, p], "blk", below(4))
 
-    def fetch1(p):
-        send = jnp.where(column == 0, s["held"][4, p], s["held"][0, p])
-        return (1, p), lax.ppermute(send, "blk", around(-1))
-
-    def fetch3(p):
-        send = jnp.where(column == RING - 1, s["held"][0, p], s["held"][4, p])
-        return (3, p), lax.ppermute(send, "blk", around(1))
+    def fetch13(p):
+        down, up = rows_to_send(s["place"], s["held"][4, p], s["held"][0, p])
+        d.append(((1, p), lax.ppermute(down, "blk", around(-1))))
+        u.append(((3, p), lax.ppermute(up, "blk", around(1))))
 
     def part(k, j):
         if j is None:
@@ -296,7 +316,8 @@
     pieces = 2 * PARTS
     x = [fetch4(0), fetch4(1)]
     fence(x[0])
-    d, u = [fetch1(0)], [fetch3(0)]
+    d, u = [], []
+    fetch13(0)
     for p in range(pieces - 1):
         if p + 2 < pieces:
             mine(p + 2)
@@ -308,8 +329,7 @@
         if p == 5:
             make(twos, into=everything, room=room, offset=places[2])
         fence(x[p + 1])
-        d.append(fetch1(p + 1))
-        u.append(fetch3(p + 1))
+        fetch13(p + 1)
         fence(d[p], u[p])
 
     make(threes, into=everything, room=room, offset=places[3])

time: 166 us -> 164 us (0.988)
  waiting for transfers between devices: 35.1 us -> 39.8 us
  local copies, waits for them, and re-layouts: 10.3 us -> 6.15 us
  other arithmetic: 2.82 us -> 0.18 us
    ppermute x8, waiting for transfers between devices: 5.65 us -> 18.1 us  [fetch4(): return ((4, p), lax.ppermute(s['held'][0, p], 'blk', below(4)))]
    ppermute x16, waiting for transfers between devices: 15.8 us -> 8.09 us  [the longest x8 6.52 us: fetch13(): u.append(((3, p), lax.ppermute(up, 'blk', around(1))))]
    ppermute x8, starting transfers between devices: 12.7 us -> 9.6 us  [swap(): return lax.ppermute(array, 'col', [(0, 1), (1, 0)])]
    select_n x8 -> x0, other arithmetic: 2.67 us -> none  [fetch3(): send = jnp.where(column == RING - 1, s['held'][0, p], s['held'][4, p])]
    unnamed x10 -> x6, local copies, waits for them, and re-layouts: 4.39 us -> 2.19 us
    ppermute x16, starting transfers between devices: 21.2 us -> 23.3 us  [the longest x8 23.3 us: fetch13(): d.append(((1, p), lax.ppermute(down, 'blk', around(-1))))]
  transfers between devices with their start and end apart: 35 -> 35, of which waited for: 16 -> 19; matrix products, arithmetic and copies ran while one was open for 4% -> 2% of each run, Pallas kernels for 22% -> 22%
where the time goes in v3:
time: 164 us
  starting transfers between devices  79 us (48%)
  waiting for transfers between devices  39.8 us (24%)
  Pallas kernels  38.2 us (23%)
  local copies, waits for them, and re-layouts  6.15 us (4%)
    ppermute x8, starting transfers between devices, fetch4(): return ((4, p), lax.ppermute(s['held'][0, p], 'blk', below(4)))  41 us
    ppermute x8, starting transfers between devices, fetch13(): d.append(((1, p), lax.ppermute(down, 'blk', around(-1))))  23.3 us
    ppermute x8, waiting for transfers between devices, fetch4(): return ((4, p), lax.ppermute(s['held'][0, p], 'blk', below(4)))  18.1 us
    pallas_call x3, Pallas kernels, kept_products(): pl.pallas_call(kernel, out_shape=jax.ShapeDtypeStruct((5, half, 2 * half)...  15.6 us
    pallas_call x7, Pallas kernels, handed_products(): pl.pallas_call(kernel, out_shape=jax.ShapeDtypeStruct((half, room), jnp.f...  11.2 us
    ppermute x8, starting transfers between devices, swap(): return lax.ppermute(array, 'col', [(0, 1), (1, 0)])  9.6 us
    ppermute x1, waiting for transfers between devices, body(): last_sums = lax.ppermute(ahead(late, third, fourth), 'blk', below(-1))  7.78 us
    pallas_call x4, Pallas kernels, relayed_products(): pl.pallas_call(kernel, out_shape=[jax.ShapeDtypeStruct(sizes[n], jnp.floa...  7.19 us
  transfers between devices with their start and end apart: 35, of which 19 were waited for; matrix products, arithmetic and copies ran while one was open for 2% of the time, Pallas kernels for 22%

profile of v3, /device:TPU:1, one launch (start us, length us, event | category | flops | bytes accessed | tf_op | source)
XLA Modules:
  0.0 163.9 jit_solution(9970949809698759598)
XLA Ops:
  1.1 6.8 %collective-permute-start = (bf16[128,2048]{1,0:T(8,128)(2,1)S(1)}, bf16[128,2048]{1,0:T(8,128)(2,1)S(1)}, u32[]{:S(2)}, u32[]{:S(2)}) collective-permute-start(bf16[128,2048]{1,0:T(8,128)(2,1)S(1)} %slice.3.mine_ref), channel_id=1, source_target_pairs={{0,120},{2,122},{4,124},{6,126},{8,0},{10,2},{12,4},{14,6},{16,8},... | collective-permute-start | bytes 1572872 | tf_op jit(solution)/shard_map/ppermute | solution.py:277
  10.8 2.9 %constant_dynamic-slice_fusion = (bf16[512,2048]{1,0:T(8,128)(2,1)S(1)}, bf16[512,2048]{1,0:T(8,128)(2,1)S(1)}) fusion(bf16[1024,2048]{1,0:T(8,128)(2,1)} %refs_1_.1, s32[]{:T(128)S(6)} %select_n.15, s32[]{:T(128)S(6)} %select_n.13), kind=kLoop, calls=%fused_computation.2 | loop fusion | bytes 8388616 | tf_op jit(solution)/shard_map/dynamic_slice | solution.py:314
  13.7 4.8 %collective-permute-done.received_ref.refs_0_.refs_2_ = bf16[128,2048]{1,0:T(8,128)(2,1)S(1)} collective-permute-done((bf16[128,2048]{1,0:T(8,128)(2,1)S(1)}, bf16[128,2048]{1,0:T(8,128)(2,1)S(1)}, u32[]{:S(2)}, u32[]{:S(2)}) %collective-permute-start) | collective-permute-done | bytes 524320 | tf_op jit(solution)/shard_map/ppermute | solution.py:277
  18.6 2.8 %collective-permute-start.2 = (bf16[128,2048]{1,0:T(8,128)(2,1)S(1)}, bf16[128,2048]{1,0:T(8,128)(2,1)S(1)}, u32[]{:S(2)}, u32[]{:S(2)}) collective-permute-start(bf16[128,2048]{1,0:T(8,128)(2,1)S(1)} %get-tuple-element.348), channel_id=1, source_target_pairs={{0,6},{2,0},{4,2},{6,4},{8,14},{10,8},{12,10},{14,12},{16,22},{18,... | collective-permute-start | bytes 1572872 | tf_op jit(solution)/shard_map/ppermute | solution.py:281
  21.5 5.6 %collective-permute-start.4 = (bf16[128,2048]{1,0:T(8,128)(2,1)S(1)}, bf16[128,2048]{1,0:T(8,128)(2,1)S(1)}, u32[]{:S(2)}, u32[]{:S(2)}) collective-permute-start(bf16[128,2048]{1,0:T(8,128)(2,1)S(1)} %shard_map.29.mine_ref), channel_id=1, source_target_pairs={{0,120},{2,122},{4,124},{6,126},{8,0},{10,2},{12,4},{14,6},{16,8},... | collective-permute-start | bytes 1572872 | tf_op jit(solution)/shard_map/ppermute | solution.py:277
  27.1 2.7 %collective-permute-done.1.received_ref.refs_1_.refs_3_ = bf16[128,2048]{1,0:T(8,128)(2,1)S(1)} collective-permute-done((bf16[128,2048]{1,0:T(8,128)(2,1)S(1)}, bf16[128,2048]{1,0:T(8,128)(2,1)S(1)}, u32[]{:S(2)}, u32[]{:S(2)}) %collective-permute-start.1) | collective-permute-done | bytes 524320 | tf_op jit(solution)/shard_map/ppermute | solution.py:277
  29.9 2.8 %collective-permute-start.5 = (bf16[128,2048]{1,0:T(8,128)(2,1)S(1)}, bf16[128,2048]{1,0:T(8,128)(2,1)S(1)}, u32[]{:S(2)}, u32[]{:S(2)}) collective-permute-start(bf16[128,2048]{1,0:T(8,128)(2,1)S(1)} %get-tuple-element.368), channel_id=1, source_target_pairs={{0,6},{2,0},{4,2},{6,4},{8,14},{10,8},{12,10},{14,12},{16,22},{18,... | collective-permute-start | bytes 1572872 | tf_op jit(solution)/shard_map/ppermute | solution.py:281
  33.1 5.6 %collective-permute-start.7 = (bf16[128,2048]{1,0:T(8,128)(2,1)S(1)}, bf16[128,2048]{1,0:T(8,128)(2,1)S(1)}, u32[]{:S(2)}, u32[]{:S(2)}) collective-permute-start(bf16[128,2048]{1,0:T(8,128)(2,1)S(1)} %shard_map.31.mine_ref), channel_id=1, source_target_pairs={{0,120},{2,122},{4,124},{6,126},{8,0},{10,2},{12,4},{14,6},{16,8},... | collective-permute-start | bytes 1572872 | tf_op jit(solution)/shard_map/ppermute | solution.py:277
  38.7 3.0 %shard_map.32.refs_8_ = f32[512,3584]{1,0:T(8,128)S(1)} custom-call(bf16[512,2048]{1,0:T(8,128)(2,1)S(1)} %get-tuple-element.655.handed_ref, bf16[1024,2048]{1,0:T(8,128)(2,1)S(1)} %copy-done.1), custom_call_target="tpu_custom_call" | custom-call | flops 1 | bytes 1 | tf_op jit(solution)/shard_map/pallas_call | solution.py:118
  41.9 2.3 %collective-permute-start.8 = (bf16[128,2048]{1,0:T(8,128)(2,1)S(1)}, bf16[128,2048]{1,0:T(8,128)(2,1)S(1)}, u32[]{:S(2)}, u32[]{:S(2)}) collective-permute-start(bf16[128,2048]{1,0:T(8,128)(2,1)S(1)} %get-tuple-element.396), channel_id=1, source_target_pairs={{0,6},{2,0},{4,2},{6,4},{8,14},{10,8},{12,10},{14,12},{16,22},{18,... | collective-permute-start | bytes 1572872 | tf_op jit(solution)/shard_map/ppermute | solution.py:281
  44.4 5.6 %collective-permute-start.10 = (bf16[128,2048]{1,0:T(8,128)(2,1)S(1)}, bf16[128,2048]{1,0:T(8,128)(2,1)S(1)}, u32[]{:S(2)}, u32[]{:S(2)}) collective-permute-start(bf16[128,2048]{1,0:T(8,128)(2,1)S(1)} %shard_map.34.mine_ref), channel_id=1, source_target_pairs={{0,120},{2,122},{4,124},{6,126},{8,0},{10,2},{12,4},{14,6},{16,8},... | collective-permute-start | bytes 1572872 | tf_op jit(solution)/shard_map/ppermute | solution.py:277
  52.0 3.2 %collective-permute-start.11 = (bf16[128,2048]{1,0:T(8,128)(2,1)S(1)}, bf16[128,2048]{1,0:T(8,128)(2,1)S(1)}, u32[]{:S(2)}, u32[]{:S(2)}) collective-permute-start(bf16[128,2048]{1,0:T(8,128)(2,1)S(1)} %get-tuple-element.430), channel_id=1, source_target_pairs={{0,6},{2,0},{4,2},{6,4},{8,14},{10,8},{12,10},{14,12},{16,22},{18,... | collective-permute-start | bytes 1572872 | tf_op jit(solution)/shard_map/ppermute | solution.py:281
  55.2 6.0 %collective-permute-start.13 = (bf16[128,2048]{1,0:T(8,128)(2,1)S(1)}, bf16[128,2048]{1,0:T(8,128)(2,1)S(1)}, u32[]{:S(2)}, u32[]{:S(2)}) collective-permute-start(bf16[128,2048]{1,0:T(8,128)(2,1)S(1)} %shard_map.36.mine_ref), channel_id=1, source_target_pairs={{0,120},{2,122},{4,124},{6,126},{8,0},{10,2},{12,4},{14,6},{16,8},... | collective-permute-start | bytes 1572872 | tf_op jit(solution)/shard_map/ppermute | solution.py:277
  61.2 2.4 %shard_map.37.refs_6_ = f32[512,3584]{1,0:T(8,128)S(1)} custom-call(bf16[512,2048]{1,0:T(8,128)(2,1)S(1)} %get-tuple-element.655.handed_ref, bf16[128,2048]{1,0:T(8,128)(2,1)S(1)} %collective-permute-done.received_ref.refs_0_.refs_2_, bf16[128,2048]{1,0:T(8,128)(2,1)S(1)} %collective-permute-done.1.received_ref.refs_1_.refs_3_, ...), custom_call_target="tpu_custom_call", output_to_operand_aliasing={{}: (9, {})} | custom-call | flops 1 | bytes 1 | tf_op jit(solution)/shard_map/pallas_call | solution.py:118
  63.7 2.7 %collective-permute-start.14 = (bf16[128,2048]{1,0:T(8,128)(2,1)S(1)}, bf16[128,2048]{1,0:T(8,128)(2,1)S(1)}, u32[]{:S(2)}, u32[]{:S(2)}) collective-permute-start(bf16[128,2048]{1,0:T(8,128)(2,1)S(1)} %get-tuple-element.470), channel_id=1, source_target_pairs={{0,6},{2,0},{4,2},{6,4},{8,14},{10,8},{12,10},{14,12},{16,22},{18,... | collective-permute-start | bytes 1572872 | tf_op jit(solution)/shard_map/ppermute | solution.py:281
  67.4 5.0 %collective-permute-start.16 = (bf16[128,2048]{1,0:T(8,128)(2,1)S(1)}, bf16[128,2048]{1,0:T(8,128)(2,1)S(1)}, u32[]{:S(2)}, u32[]{:S(2)}) collective-permute-start(bf16[128,2048]{1,0:T(8,128)(2,1)S(1)} %shard_map.39.mine_ref), channel_id=1, source_target_pairs={{0,120},{2,122},{4,124},{6,126},{8,0},{10,2},{12,4},{14,6},{16,8},... | collective-permute-start | bytes 1572872 | tf_op jit(solution)/shard_map/ppermute | solution.py:277
  74.5 3.2 %collective-permute-start.17 = (bf16[128,2048]{1,0:T(8,128)(2,1)S(1)}, bf16[128,2048]{1,0:T(8,128)(2,1)S(1)}, u32[]{:S(2)}, u32[]{:S(2)}) collective-permute-start(bf16[128,2048]{1,0:T(8,128)(2,1)S(1)} %get-tuple-element.516), channel_id=1, source_target_pairs={{0,6},{2,0},{4,2},{6,4},{8,14},{10,8},{12,10},{14,12},{16,22},{18,... | collective-permute-start | bytes 1572872 | tf_op jit(solution)/shard_map/ppermute | solution.py:281
  78.1 5.7 %collective-permute-start.19 = (bf16[128,2048]{1,0:T(8,128)(2,1)S(1)}, bf16[128,2048]{1,0:T(8,128)(2,1)S(1)}, u32[]{:S(2)}, u32[]{:S(2)}) collective-permute-start(bf16[128,2048]{1,0:T(8,128)(2,1)S(1)} %shard_map.41.mine_ref), channel_id=1, source_target_pairs={{0,120},{2,122},{4,124},{6,126},{8,0},{10,2},{12,4},{14,6},{16,8},... | collective-permute-start | bytes 1572872 | tf_op jit(solution)/shard_map/ppermute | solution.py:277
  85.8 3.0 %collective-permute-start.20 = (bf16[128,2048]{1,0:T(8,128)(2,1)S(1)}, bf16[128,2048]{1,0:T(8,128)(2,1)S(1)}, u32[]{:S(2)}, u32[]{:S(2)}) collective-permute-start(bf16[128,2048]{1,0:T(8,128)(2,1)S(1)} %get-tuple-element.567), channel_id=1, source_target_pairs={{0,6},{2,0},{4,2},{6,4},{8,14},{10,8},{12,10},{14,12},{16,22},{18,... | collective-permute-start | bytes 1572872 | tf_op jit(solution)/shard_map/ppermute | solution.py:281
  89.8 6.8 %collective-permute-done.19.received_ref.refs_1_.refs_8_ = bf16[128,2048]{1,0:T(8,128)(2,1)S(1)} collective-permute-done((bf16[128,2048]{1,0:T(8,128)(2,1)S(1)}, bf16[128,2048]{1,0:T(8,128)(2,1)S(1)}, u32[]{:S(2)}, u32[]{:S(2)}) %collective-permute-start.19) | collective-permute-done | bytes 524320 | tf_op jit(solution)/shard_map/ppermute | solution.py:277
  96.7 3.3 %collective-permute-start.24 = (bf16[128,2048]{1,0:T(8,128)(2,1)S(1)}, bf16[128,2048]{1,0:T(8,128)(2,1)S(1)}, u32[]{:S(2)}, u32[]{:S(2)}) collective-permute-start(bf16[128,2048]{1,0:T(8,128)(2,1)S(1)} %get-tuple-element.602), channel_id=1, source_target_pairs={{0,6},{2,0},{4,2},{6,4},{8,14},{10,8},{12,10},{14,12},{16,22},{18,... | collective-permute-start | bytes 1572872 | tf_op jit(solution)/shard_map/ppermute | solution.py:281
  102.0 4.1 %collective-permute-start.22 = (f32[384,256]{1,0:T(8,128)S(1)}, f32[384,256]{1,0:T(8,128)S(1)}, u32[]{:S(2)}, u32[]{:S(2)}) collective-permute-start(f32[384,256]{1,0:T(8,128)S(1)} %get-tuple-element.598), channel_id=1, source_target_pairs={{0,1},{1,0},{2,3},{3,2},{4,5},{5,4},{6,7},{7,6},{8,9},{9,8},{10,11... | collective-permute-start | bytes 1179656 | tf_op jit(solution)/shard_map/ppermute | solution.py:263
  110.7 2.7 %collective-permute-done.25.refs_1_.refs_6_ = bf16[128,2048]{1,0:T(8,128)(2,1)S(1)} collective-permute-done((bf16[128,2048]{1,0:T(8,128)(2,1)S(1)}, bf16[128,2048]{1,0:T(8,128)(2,1)S(1)}, u32[]{:S(2)}, u32[]{:S(2)}) %collective-permute-start.25) | collective-permute-done | bytes 524320 | tf_op jit(solution)/shard_map/ppermute | solution.py:282
  113.4 2.5 %collective-permute-start.29 = (f32[512,3584]{1,0:T(8,128)S(1)}, f32[512,3584]{1,0:T(8,128)S(1)}, u32[]{:S(2)}, u32[]{:S(2)}) collective-permute-start(f32[512,3584]{1,0:T(8,128)S(1)} %shard_map.48), channel_id=1, source_target_pairs={{0,1},{1,0},{2,3},{3,2},{4,5},{5,4},{6,7},{7,6},{8,9},{9,8},{10,11... | collective-permute-start | bytes 22020104 | tf_op jit(solution)/shard_map/ppermute | solution.py:263
  116.0 5.0 %collective-permute-start.30 = (bf16[256,2048]{1,0:T(8,128)(2,1)S(1)}, bf16[256,2048]{1,0:T(8,128)(2,1)S(1)}, u32[]{:S(2)}, u32[]{:S(2)}) collective-permute-start(bf16[256,2048]{1,0:T(8,128)(2,1)S(1)} %pad_maximum_fusion), channel_id=1, source_target_pairs={{0,126},{2,0},{4,2},{6,4},{8,6},{10,8},{12,10},{14,12},{16,14},{18... | collective-permute-start | bytes 3145736 | tf_op jit(solution)/shard_map/ppermute | solution.py:356
  121.1 2.4 %shard_map.49 = (f32[128,768]{1,0:T(8,128)S(1)}, f32[128,768]{1,0:T(8,128)S(1)}) custom-call(s32[1]{0:T(128)} %bitcast.2._.where_ref, bf16[128,2048]{1,0:T(8,128)(2,1)S(1)} %collective-permute-done.2.refs_4_.refs_0_.refs_6_, bf16[128,2048]{1,0:T(8,128)(2,1)S(1)} %collective-permute-done.5.refs_5_.refs_1_.refs_7_, ...), custom_call_target="tpu_custom_call" | custom-call | flops 1 | bytes 1 | tf_op jit(solution)/shard_map/pallas_call | solution.py:207
  125.5 2.2 %collective-permute-done.26.refs_14_ = f32[128,768]{1,0:T(8,128)S(1)} collective-permute-done((f32[128,768]{1,0:T(8,128)S(1)}, f32[128,768]{1,0:T(8,128)S(1)}, u32[]{:S(2)}, u32[]{:S(2)}) %collective-permute-start.26) | collective-permute-done | bytes 393248 | tf_op jit(solution)/shard_map/ppermute | solution.py:263
  128.3 2.6 %shard_map.52 = f32[256,768]{1,0:T(8,128)S(1)} custom-call(s32[1]{0:T(128)} %bitcast.2._.where_ref, bf16[128,2048]{1,0:T(8,128)(2,1)S(1)} %collective-permute-done.2.refs_4_.refs_0_.refs_6_, bf16[128,2048]{1,0:T(8,128)(2,1)S(1)} %collective-permute-done.5.refs_5_.refs_1_.refs_7_, bf16[128,2048]{1,0:T(8,128)(2,1)S(1)} %collective-permute-done.8.refs_2_.refs_3_, ...), custom_call_target="tpu_custom_call" | custom-call | flops 1 | bytes 1 | tf_op jit(solution)/shard_map/pallas_call | solution.py:207
  131.1 7.0 %shard_map.53.refs_13_ = f32[5,512,1024]{2,1,0:T(8,128)} custom-call(f32[5]{0:T(128)S(1)} %pad_maximum_fusion.1.weights_ref, bf16[512,2048]{1,0:T(8,128)(2,1)S(1)} %get-tuple-element.652.kept_ref, f32[512,3584]{1,0:T(8,128)S(1)} %collective-permute-done.29.refs_0_, bf16[1024,2048]{1,0:T(8,128)(2,1)S(1)} %copy-done.1, ...), custom_call_target="tpu_custom_call" | custom-call | flops 1 | bytes 1 | tf_op jit(solution)/shard_map/pallas_call | solution.py:161
  138.1 5.2 %shard_map.54._ = f32[5,512,1024]{2,1,0:T(8,128)} custom-call(f32[5]{0:T(128)S(1)} %pad_maximum_fusion.1.weights_ref, bf16[512,2048]{1,0:T(8,128)(2,1)S(1)} %get-tuple-element.652.kept_ref, f32[512,3584]{1,0:T(8,128)S(1)} %collective-permute-done.29.refs_0_, ...), custom_call_target="tpu_custom_call", output_to_operand_aliasing={{}: (15, {})} | custom-call | flops 1 | bytes 1 | tf_op jit(solution)/shard_map/pallas_call | solution.py:161
  151.0 3.4 %shard_map.57._ = f32[5,512,1024]{2,1,0:T(8,128)} custom-call(f32[5]{0:T(128)S(1)} %pad_maximum_fusion.1.weights_ref, bf16[512,2048]{1,0:T(8,128)(2,1)S(1)} %get-tuple-element.652.kept_ref, f32[512,256]{1,0:T(8,128)S(1)} %collective-permute-done.32.refs_0_, f32[512,256]{1,0:T(8,128)S(1)} %collective-permute-done.33.refs_1_, ...), custom_call_target="tpu_custom_call", output_to_operand_aliasing={{}: (10, {})} | custom-call | flops 1 | bytes 1 | tf_op jit(solution)/shard_map/pallas_call | solution.py:161
  154.4 7.8 %collective-permute-done.28.summed_ref = f32[256,768]{1,0:T(8,128)S(1)} collective-permute-done((f32[256,768]{1,0:T(8,128)S(1)}, f32[256,768]{1,0:T(8,128)S(1)}, u32[]{:S(2)}, u32[]{:S(2)}) %collective-permute-start.28) | collective-permute-done | bytes 786464 | tf_op jit(solution)/shard_map/ppermute | solution.py:358
  (80 shorter events, 32.3 us)
Async XLA Ops:
  1.1 17.4 %collective-permute-start = (bf16[128,2048]{1,0:T(8,128)(2,1)S(1)}, bf16[128,2048]{1,0:T(8,128)(2,1)S(1)}, u32[]{:S(2)}, u32[]{:S(2)}) collective-permute-start(bf16[128,2048]{1,0:T(8,128)(2,1)S(1)} %slice.3.mine_ref), channel_id=1, source_target_pairs={{0,120},{2,122},{4,124},{6,126},{8,0},{10,2},{12,4},{14,6},{16,8},... | collective-permute-start | bytes 1572872 | tf_op jit(solution)/shard_map/ppermute | solution.py:277
  10.2 19.6 %collective-permute-start.1 = (bf16[128,2048]{1,0:T(8,128)(2,1)S(1)}, bf16[128,2048]{1,0:T(8,128)(2,1)S(1)}, u32[]{:S(2)}, u32[]{:S(2)}) collective-permute-start(bf16[128,2048]{1,0:T(8,128)(2,1)S(1)} %shard_map.28.mine_ref), channel_id=1, source_target_pairs={{0,120},{2,122},{4,124},{6,126},{8,0},{10,2},{12,4},{14,6},{16,8},... | collective-permute-start | bytes 1572872 | tf_op jit(solution)/shard_map/ppermute | solution.py:277
  18.6 14.0 %collective-permute-start.2 = (bf16[128,2048]{1,0:T(8,128)(2,1)S(1)}, bf16[128,2048]{1,0:T(8,128)(2,1)S(1)}, u32[]{:S(2)}, u32[]{:S(2)}) collective-permute-start(bf16[128,2048]{1,0:T(8,128)(2,1)S(1)} %get-tuple-element.348), channel_id=1, source_target_pairs={{0,6},{2,0},{4,2},{6,4},{8,14},{10,8},{12,10},{14,12},{16,22},{18,... | collective-permute-start | bytes 1572872 | tf_op jit(solution)/shard_map/ppermute | solution.py:281
  21.4 11.7 %collective-permute-start.3 = (bf16[128,2048]{1,0:T(8,128)(2,1)S(1)}, bf16[128,2048]{1,0:T(8,128)(2,1)S(1)}, u32[]{:S(2)}, u32[]{:S(2)}) collective-permute-start(bf16[128,2048]{1,0:T(8,128)(2,1)S(1)} %get-tuple-element.349), channel_id=1, source_target_pairs={{0,2},{2,4},{4,6},{6,0},{8,10},{10,12},{12,14},{14,8},{16,18},{18,... | collective-permute-start | bytes 1572872 | tf_op jit(solution)/shard_map/ppermute | solution.py:282
  21.5 20.2 %collective-permute-start.4 = (bf16[128,2048]{1,0:T(8,128)(2,1)S(1)}, bf16[128,2048]{1,0:T(8,128)(2,1)S(1)}, u32[]{:S(2)}, u32[]{:S(2)}) collective-permute-start(bf16[128,2048]{1,0:T(8,128)(2,1)S(1)} %shard_map.29.mine_ref), channel_id=1, source_target_pairs={{0,120},{2,122},{4,124},{6,126},{8,0},{10,2},{12,4},{14,6},{16,8},... | collective-permute-start | bytes 1572872 | tf_op jit(solution)/shard_map/ppermute | solution.py:277
  29.9 14.3 %collective-permute-start.5 = (bf16[128,2048]{1,0:T(8,128)(2,1)S(1)}, bf16[128,2048]{1,0:T(8,128)(2,1)S(1)}, u32[]{:S(2)}, u32[]{:S(2)}) collective-permute-start(bf16[128,2048]{1,0:T(8,128)(2,1)S(1)} %get-tuple-element.368), channel_id=1, source_target_pairs={{0,6},{2,0},{4,2},{6,4},{8,14},{10,8},{12,10},{14,12},{16,22},{18,... | collective-permute-start | bytes 1572872 | tf_op jit(solution)/shard_map/ppermute | solution.py:281
  32.7 11.7 %collective-permute-start.6 = (bf16[128,2048]{1,0:T(8,128)(2,1)S(1)}, bf16[128,2048]{1,0:T(8,128)(2,1)S(1)}, u32[]{:S(2)}, u32[]{:S(2)}) collective-permute-start(bf16[128,2048]{1,0:T(8,128)(2,1)S(1)} %get-tuple-element.370), channel_id=1, source_target_pairs={{0,2},{2,4},{4,6},{6,0},{8,10},{10,12},{12,14},{14,8},{16,18},{18,... | collective-permute-start | bytes 1572872 | tf_op jit(solution)/shard_map/ppermute | solution.py:282
  33.1 18.7 %collective-permute-start.7 = (bf16[128,2048]{1,0:T(8,128)(2,1)S(1)}, bf16[128,2048]{1,0:T(8,128)(2,1)S(1)}, u32[]{:S(2)}, u32[]{:S(2)}) collective-permute-start(bf16[128,2048]{1,0:T(8,128)(2,1)S(1)} %shard_map.31.mine_ref), channel_id=1, source_target_pairs={{0,120},{2,122},{4,124},{6,126},{8,0},{10,2},{12,4},{14,6},{16,8},... | collective-permute-start | bytes 1572872 | tf_op jit(solution)/shard_map/ppermute | solution.py:277
  41.9 13.3 %collective-permute-start.8 = (bf16[128,2048]{1,0:T(8,128)(2,1)S(1)}, bf16[128,2048]{1,0:T(8,128)(2,1)S(1)}, u32[]{:S(2)}, u32[]{:S(2)}) collective-permute-start(bf16[128,2048]{1,0:T(8,128)(2,1)S(1)} %get-tuple-element.396), channel_id=1, source_target_pairs={{0,6},{2,0},{4,2},{6,4},{8,14},{10,8},{12,10},{14,12},{16,22},{18,... | collective-permute-start | bytes 1572872 | tf_op jit(solution)/shard_map/ppermute | solution.py:281
  44.2 11.0 %collective-permute-start.9 = (bf16[128,2048]{1,0:T(8,128)(2,1)S(1)}, bf16[128,2048]{1,0:T(8,128)(2,1)S(1)}, u32[]{:S(2)}, u32[]{:S(2)}) collective-permute-start(bf16[128,2048]{1,0:T(8,128)(2,1)S(1)} %get-tuple-element.399), channel_id=1, source_target_pairs={{0,2},{2,4},{4,6},{6,0},{8,10},{10,12},{12,14},{14,8},{16,18},{18,... | collective-permute-start | bytes 1572872 | tf_op jit(solution)/shard_map/ppermute | solution.py:282
  44.4 19.2 %collective-permute-start.10 = (bf16[128,2048]{1,0:T(8,128)(2,1)S(1)}, bf16[128,2048]{1,0:T(8,128)(2,1)S(1)}, u32[]{:S(2)}, u32[]{:S(2)}) collective-permute-start(bf16[128,2048]{1,0:T(8,128)(2,1)S(1)} %shard_map.34.mine_ref), channel_id=1, source_target_pairs={{0,120},{2,122},{4,124},{6,126},{8,0},{10,2},{12,4},{14,6},{16,8},... | collective-permute-start | bytes 1572872 | tf_op jit(solution)/shard_map/ppermute | solution.py:277
  52.0 14.4 %collective-permute-start.11 = (bf16[128,2048]{1,0:T(8,128)(2,1)S(1)}, bf16[128,2048]{1,0:T(8,128)(2,1)S(1)}, u32[]{:S(2)}, u32[]{:S(2)}) collective-permute-start(bf16[128,2048]{1,0:T(8,128)(2,1)S(1)} %get-tuple-element.430), channel_id=1, source_target_pairs={{0,6},{2,0},{4,2},{6,4},{8,14},{10,8},{12,10},{14,12},{16,22},{18,... | collective-permute-start | bytes 1572872 | tf_op jit(solution)/shard_map/ppermute | solution.py:281
  55.1 12.2 %collective-permute-start.12 = (bf16[128,2048]{1,0:T(8,128)(2,1)S(1)}, bf16[128,2048]{1,0:T(8,128)(2,1)S(1)}, u32[]{:S(2)}, u32[]{:S(2)}) collective-permute-start(bf16[128,2048]{1,0:T(8,128)(2,1)S(1)} %get-tuple-element.434), channel_id=1, source_target_pairs={{0,2},{2,4},{4,6},{6,0},{8,10},{10,12},{12,14},{14,8},{16,18},{18,... | collective-permute-start | bytes 1572872 | tf_op jit(solution)/shard_map/ppermute | solution.py:282
  55.2 19.1 %collective-permute-start.13 = (bf16[128,2048]{1,0:T(8,128)(2,1)S(1)}, bf16[128,2048]{1,0:T(8,128)(2,1)S(1)}, u32[]{:S(2)}, u32[]{:S(2)}) collective-permute-start(bf16[128,2048]{1,0:T(8,128)(2,1)S(1)} %shard_map.36.mine_ref), channel_id=1, source_target_pairs={{0,120},{2,122},{4,124},{6,126},{8,0},{10,2},{12,4},{14,6},{16,8},... | collective-permute-start | bytes 1572872 | tf_op jit(solution)/shard_map/ppermute | solution.py:277
  63.7 13.9 %collective-permute-start.14 = (bf16[128,2048]{1,0:T(8,128)(2,1)S(1)}, bf16[128,2048]{1,0:T(8,128)(2,1)S(1)}, u32[]{:S(2)}, u32[]{:S(2)}) collective-permute-start(bf16[128,2048]{1,0:T(8,128)(2,1)S(1)} %get-tuple-element.470), channel_id=1, source_target_pairs={{0,6},{2,0},{4,2},{6,4},{8,14},{10,8},{12,10},{14,12},{16,22},{18,... | collective-permute-start | bytes 1572872 | tf_op jit(solution)/shard_map/ppermute | solution.py:281
  66.4 11.7 %collective-permute-start.15 = (bf16[128,2048]{1,0:T(8,128)(2,1)S(1)}, bf16[128,2048]{1,0:T(8,128)(2,1)S(1)}, u32[]{:S(2)}, u32[]{:S(2)}) collective-permute-start(bf16[128,2048]{1,0:T(8,128)(2,1)S(1)} %get-tuple-element.475), channel_id=1, source_target_pairs={{0,2},{2,4},{4,6},{6,0},{8,10},{10,12},{12,14},{14,8},{16,18},{18,... | collective-permute-start | bytes 1572872 | tf_op jit(solution)/shard_map/ppermute | solution.py:282
  67.4 18.3 %collective-permute-start.16 = (bf16[128,2048]{1,0:T(8,128)(2,1)S(1)}, bf16[128,2048]{1,0:T(8,128)(2,1)S(1)}, u32[]{:S(2)}, u32[]{:S(2)}) collective-permute-start(bf16[128,2048]{1,0:T(8,128)(2,1)S(1)} %shard_map.39.mine_ref), channel_id=1, source_target_pairs={{0,120},{2,122},{4,124},{6,126},{8,0},{10,2},{12,4},{14,6},{16,8},... | collective-permute-start | bytes 1572872 | tf_op jit(solution)/shard_map/ppermute | solution.py:277
  74.5 14.4 %collective-permute-start.17 = (bf16[128,2048]{1,0:T(8,128)(2,1)S(1)}, bf16[128,2048]{1,0:T(8,128)(2,1)S(1)}, u32[]{:S(2)}, u32[]{:S(2)}) collective-permute-start(bf16[128,2048]{1,0:T(8,128)(2,1)S(1)} %get-tuple-element.516), channel_id=1, source_target_pairs={{0,6},{2,0},{4,2},{6,4},{8,14},{10,8},{12,10},{14,12},{16,22},{18,... | collective-permute-start | bytes 1572872 | tf_op jit(solution)/shard_map/ppermute | solution.py:281
  77.6 12.2 %collective-permute-start.18 = (bf16[128,2048]{1,0:T(8,128)(2,1)S(1)}, bf16[128,2048]{1,0:T(8,128)(2,1)S(1)}, u32[]{:S(2)}, u32[]{:S(2)}) collective-permute-start(bf16[128,2048]{1,0:T(8,128)(2,1)S(1)} %get-tuple-element.522), channel_id=1, source_target_pairs={{0,2},{2,4},{4,6},{6,0},{8,10},{10,12},{12,14},{14,8},{16,18},{18,... | collective-permute-start | bytes 1572872 | tf_op jit(solution)/shard_map/ppermute | solution.py:282
  78.1 18.5 %collective-permute-start.19 = (bf16[128,2048]{1,0:T(8,128)(2,1)S(1)}, bf16[128,2048]{1,0:T(8,128)(2,1)S(1)}, u32[]{:S(2)}, u32[]{:S(2)}) collective-permute-start(bf16[128,2048]{1,0:T(8,128)(2,1)S(1)} %shard_map.41.mine_ref), channel_id=1, source_target_pairs={{0,120},{2,122},{4,124},{6,126},{8,0},{10,2},{12,4},{14,6},{16,8},... | collective-permute-start | bytes 1572872 | tf_op jit(solution)/shard_map/ppermute | solution.py:277
  85.8 14.3 %collective-permute-start.20 = (bf16[128,2048]{1,0:T(8,128)(2,1)S(1)}, bf16[128,2048]{1,0:T(8,128)(2,1)S(1)}, u32[]{:S(2)}, u32[]{:S(2)}) collective-permute-start(bf16[128,2048]{1,0:T(8,128)(2,1)S(1)} %get-tuple-element.567), channel_id=1, source_target_pairs={{0,6},{2,0},{4,2},{6,4},{8,14},{10,8},{12,10},{14,12},{16,22},{18,... | collective-permute-start | bytes 1572872 | tf_op jit(solution)/shard_map/ppermute | solution.py:281
  88.9 12.1 %collective-permute-start.21 = (bf16[128,2048]{1,0:T(8,128)(2,1)S(1)}, bf16[128,2048]{1,0:T(8,128)(2,1)S(1)}, u32[]{:S(2)}, u32[]{:S(2)}) collective-permute-start(bf16[128,2048]{1,0:T(8,128)(2,1)S(1)} %get-tuple-element.574), channel_id=1, source_target_pairs={{0,2},{2,4},{4,6},{6,0},{8,10},{10,12},{12,14},{14,8},{16,18},{18,... | collective-permute-start | bytes 1572872 | tf_op jit(solution)/shard_map/ppermute | solution.py:282
  96.7 14.0 %collective-permute-start.24 = (bf16[128,2048]{1,0:T(8,128)(2,1)S(1)}, bf16[128,2048]{1,0:T(8,128)(2,1)S(1)}, u32[]{:S(2)}, u32[]{:S(2)}) collective-permute-start(bf16[128,2048]{1,0:T(8,128)(2,1)S(1)} %get-tuple-element.602), channel_id=1, source_target_pairs={{0,6},{2,0},{4,2},{6,4},{8,14},{10,8},{12,10},{14,12},{16,22},{18,... | collective-permute-start | bytes 1572872 | tf_op jit(solution)/shard_map/ppermute | solution.py:281
  100.1 13.4 %collective-permute-start.25 = (bf16[128,2048]{1,0:T(8,128)(2,1)S(1)}, bf16[128,2048]{1,0:T(8,128)(2,1)S(1)}, u32[]{:S(2)}, u32[]{:S(2)}) collective-permute-start(bf16[128,2048]{1,0:T(8,128)(2,1)S(1)} %get-tuple-element.606), channel_id=1, source_target_pairs={{0,2},{2,4},{4,6},{6,0},{8,10},{10,12},{12,14},{14,8},{16,18},{18,... | collective-permute-start | bytes 1572872 | tf_op jit(solution)/shard_map/ppermute | solution.py:282
  102.0 6.0 %collective-permute-start.22 = (f32[384,256]{1,0:T(8,128)S(1)}, f32[384,256]{1,0:T(8,128)S(1)}, u32[]{:S(2)}, u32[]{:S(2)}) collective-permute-start(f32[384,256]{1,0:T(8,128)S(1)} %get-tuple-element.598), channel_id=1, source_target_pairs={{0,1},{1,0},{2,3},{3,2},{4,5},{5,4},{6,7},{7,6},{8,9},{9,8},{10,11... | collective-permute-start | bytes 1179656 | tf_op jit(solution)/shard_map/ppermute | solution.py:263
  113.4 17.7 %collective-permute-start.29 = (f32[512,3584]{1,0:T(8,128)S(1)}, f32[512,3584]{1,0:T(8,128)S(1)}, u32[]{:S(2)}, u32[]{:S(2)}) collective-permute-start(f32[512,3584]{1,0:T(8,128)S(1)} %shard_map.48), channel_id=1, source_target_pairs={{0,1},{1,0},{2,3},{3,2},{4,5},{5,4},{6,7},{7,6},{8,9},{9,8},{10,11... | collective-permute-start | bytes 22020104 | tf_op jit(solution)/shard_map/ppermute | solution.py:263
  116.0 29.3 %collective-permute-start.30 = (bf16[256,2048]{1,0:T(8,128)(2,1)S(1)}, bf16[256,2048]{1,0:T(8,128)(2,1)S(1)}, u32[]{:S(2)}, u32[]{:S(2)}) collective-permute-start(bf16[256,2048]{1,0:T(8,128)(2,1)S(1)} %pad_maximum_fusion), channel_id=1, source_target_pairs={{0,126},{2,0},{4,2},{6,4},{8,6},{10,8},{12,10},{14,12},{16,14},{18... | collective-permute-start | bytes 3145736 | tf_op jit(solution)/shard_map/ppermute | solution.py:356
  121.1 24.3 %collective-permute-start.31 = (f32[384,512]{1,0:T(8,128)S(1)}, f32[384,512]{1,0:T(8,128)S(1)}, u32[]{:S(2)}, u32[]{:S(2)}) collective-permute-start(f32[384,512]{1,0:T(8,128)S(1)} %shard_map.46), channel_id=1, source_target_pairs={{0,2},{2,4},{4,6},{6,8},{8,10},{10,12},{12,14},{14,16},{16,18},{18... | collective-permute-start | bytes 2359304 | tf_op jit(solution)/shard_map/ppermute | solution.py:355
  123.4 4.3 %collective-permute-start.26 = (f32[128,768]{1,0:T(8,128)S(1)}, f32[128,768]{1,0:T(8,128)S(1)}, u32[]{:S(2)}, u32[]{:S(2)}) collective-permute-start(f32[128,768]{1,0:T(8,128)S(1)} %get-tuple-element.632), channel_id=1, source_target_pairs={{0,1},{1,0},{2,3},{3,2},{4,5},{5,4},{6,7},{7,6},{8,9},{9,8},{10,11... | collective-permute-start | bytes 1179656 | tf_op jit(solution)/shard_map/ppermute | solution.py:263
  123.8 4.5 %collective-permute-start.27 = (f32[128,768]{1,0:T(8,128)S(1)}, f32[128,768]{1,0:T(8,128)S(1)}, u32[]{:S(2)}, u32[]{:S(2)}) collective-permute-start(f32[128,768]{1,0:T(8,128)S(1)} %get-tuple-element.633), channel_id=1, source_target_pairs={{0,1},{1,0},{2,3},{3,2},{4,5},{5,4},{6,7},{7,6},{8,9},{9,8},{10,11... | collective-permute-start | bytes 1179656 | tf_op jit(solution)/shard_map/ppermute | solution.py:263
  130.9 31.3 %collective-permute-start.28 = (f32[256,768]{1,0:T(8,128)S(1)}, f32[256,768]{1,0:T(8,128)S(1)}, u32[]{:S(2)}, u32[]{:S(2)}) collective-permute-start(f32[256,768]{1,0:T(8,128)S(1)} %shard_map.52), channel_id=1, source_target_pairs={{0,2},{2,4},{4,6},{6,8},{8,10},{10,12},{12,14},{14,16},{16,18},{18... | collective-permute-start | bytes 2359304 | tf_op jit(solution)/shard_map/ppermute | solution.py:358
  146.1 3.9 %collective-permute-start.34 = (f32[512,256]{1,0:T(8,128)S(1)}, f32[512,256]{1,0:T(8,128)S(1)}, u32[]{:S(2)}, u32[]{:S(2)}) collective-permute-start(f32[512,256]{1,0:T(8,128)S(1)} %shard_map.55), channel_id=1, source_target_pairs={{0,1},{1,0},{2,3},{3,2},{4,5},{5,4},{6,7},{7,6},{8,9},{9,8},{10,11... | collective-permute-start | bytes 1572872 | tf_op jit(solution)/shard_map/ppermute | solution.py:263
  (6 other events, 27.2 us)

commit v4 on v3

--- a/solution.py
+++ b/solution.py
@@ -47,7 +47,7 @@
 
 
 def rows_to_send(place, received, mine):
-    def kernel(place_ref, received_ref, mine_ref, down_ref, up_ref, sems):
+    def kernel(place_ref, received_ref, mine_ref, up_ref, down_ref, sems):
         def send(chosen, to_ref, n, act):
             for ref, use in ((received_ref, chosen), (mine_ref, jnp.logical_not(chosen))):
                 pl.when(use)(lambda ref=ref: act(pltpu.make_async_copy(ref, to_ref, sems.at[n])))
@@ -277,9 +277,9 @@
         return (4, p), lax.ppermute(s["held"][0, p], "blk", below(4))
 
     def fetch13(p):
-        down, up = rows_to_send(s["place"], s["held"][4, p], s["held"][0, p])
+        up, down = rows_to_send(s["place"], s["held"][4, p], s["held"][0, p])
+        u.append(((3, p), lax.ppermute(up, "blk", around(1))))
         d.append(((1, p), lax.ppermute(down, "blk", around(-1))))
-        u.append(((3, p), lax.ppermute(up, "blk", around(1))))
 
     def part(k, j):
         if j is None:
@@ -330,7 +330,8 @@
             make(twos, into=everything, room=room, offset=places[2])
         fence(x[p + 1])
         fetch13(p + 1)
-        fence(d[p], u[p])
+        fence(u[p])
+        fence(d[p])
 
     make(threes, into=everything, room=room, offset=places[3])
     some = (0, 1, 2)
@@ -350,7 +351,8 @@
         return relayed_products(s["where"], rows, others, blocks, theirs)[0]
 
     s["ahead"] = ahead(early)
-    fence(d[-1], u[-1])
+    fence(u[-1])
+    fence(d[-1])
 
     first_sums = lax.ppermute(s["ahead"], "blk", below(-1))
     relayed = lax.ppermute(jnp.concatenate(part(1, 3)), "blk", below(1))

time: 164 us -> 164 us (level)
    ppermute x8, starting transfers between devices: 23.3 us -> 12.5 us  [fetch13(): d.append(((1, p), lax.ppermute(down, 'blk', around(-1))))]
    ppermute x8, starting transfers between devices: 0.02 us -> 10.5 us  [fetch13(): u.append(((3, p), lax.ppermute(up, 'blk', around(1))))]
    ppermute x8, waiting for transfers between devices: 18.1 us -> 21.7 us  [fetch4(): return ((4, p), lax.ppermute(s['held'][0, p], 'blk', below(4)))]
    ppermute x1, starting transfers between devices: 5.03 us -> 7.71 us  [body(): relayed = lax.ppermute(jnp.concatenate(part(1, 3)), 'blk', below(1))]
    ppermute x8, waiting for transfers between devices: 3.83 us -> 1.3 us  [swap(): return lax.ppermute(array, 'col', [(0, 1), (1, 0)])]
    ppermute x8, starting transfers between devices: 9.6 us -> 7.42 us  [swap(): return lax.ppermute(array, 'col', [(0, 1), (1, 0)])]
    ppermute x8, waiting for transfers between devices: 6.52 us -> 4.61 us  [fetch13(): u.append(((3, p), lax.ppermute(up, 'blk', around(1))))]
    ppermute x1, waiting for transfers between devices: 1.96 us -> 3.69 us  [body(): first_sums = lax.ppermute(s['ahead'], 'blk', below(-1))]
  transfers between devices with their start and end apart: 35 -> 35, of which waited for: 19 -> 13; matrix products, arithmetic and copies ran while one was open for 2% -> 2% of each run, Pallas kernels for 22% -> 22%
where the time goes in v4:
time: 164 us
  starting transfers between devices  79.8 us (49%)
  waiting for transfers between devices  39.1 us (24%)
  Pallas kernels  38.2 us (23%)
  local copies, waits for them, and re-layouts  6.15 us (4%)
    ppermute x8, starting transfers between devices, fetch4(): return ((4, p), lax.ppermute(s['held'][0, p], 'blk', below(4)))  40.9 us
    ppermute x8, waiting for transfers between devices, fetch4(): return ((4, p), lax.ppermute(s['held'][0, p], 'blk', below(4)))  21.7 us
    pallas_call x3, Pallas kernels, kept_products(): pl.pallas_call(kernel, out_shape=jax.ShapeDtypeStruct((5, half, 2 * half)...  15.6 us
    ppermute x8, starting transfers between devices, fetch13(): d.append(((1, p), lax.ppermute(down, 'blk', around(-1))))  12.5 us
    pallas_call x7, Pallas kernels, handed_products(): pl.pallas_call(kernel, out_shape=jax.ShapeDtypeStruct((half, room), jnp.f...  11.2 us
    ppermute x8, starting transfers between devices, fetch13(): u.append(((3, p), lax.ppermute(up, 'blk', around(1))))  10.5 us
    ppermute x1, waiting for transfers between devices, body(): last_sums = lax.ppermute(ahead(late, third, fourth), 'blk', below(-1))  7.79 us
    ppermute x1, starting transfers between devices, body(): relayed = lax.ppermute(jnp.concatenate(part(1, 3)), 'blk', below(1))  7.71 us
  transfers between devices with their start and end apart: 35, of which 13 were waited for; matrix products, arithmetic and copies ran while one was open for 2% of the time, Pallas kernels for 22%

profile of v4, /device:TPU:1, one launch (start us, length us, event | category | flops | bytes accessed | tf_op | source)
XLA Modules:
  0.0 164.0 jit_solution(6635978382959582448)
XLA Ops:
  1.1 6.8 %collective-permute-start = (bf16[128,2048]{1,0:T(8,128)(2,1)S(1)}, bf16[128,2048]{1,0:T(8,128)(2,1)S(1)}, u32[]{:S(2)}, u32[]{:S(2)}) collective-permute-start(bf16[128,2048]{1,0:T(8,128)(2,1)S(1)} %slice.3.mine_ref), channel_id=1, source_target_pairs={{0,120},{2,122},{4,124},{6,126},{8,0},{10,2},{12,4},{14,6},{16,8},... | collective-permute-start | bytes 1572872 | tf_op jit(solution)/shard_map/ppermute | solution.py:277
  7.9 2.2 %copy-done = bf16[1024,2048]{1,0:T(8,128)(2,1)S(1)} copy-done((bf16[1024,2048]{1,0:T(8,128)(2,1)S(1)}, bf16[1024,2048]{1,0:T(8,128)(2,1)}, u32[]{:S(2)}) %copy-start) | copy-done | bytes 4194328
  10.8 2.9 %constant_dynamic-slice_fusion = (bf16[512,2048]{1,0:T(8,128)(2,1)S(1)}, bf16[512,2048]{1,0:T(8,128)(2,1)S(1)}) fusion(bf16[1024,2048]{1,0:T(8,128)(2,1)} %refs_1_.1, s32[]{:T(128)S(6)} %select_n.15, s32[]{:T(128)S(6)} %select_n.13), kind=kLoop, calls=%fused_computation.2 | loop fusion | bytes 8388616 | tf_op jit(solution)/shard_map/dynamic_slice | solution.py:314
  13.7 4.8 %collective-permute-done.received_ref.refs_0_.refs_2_ = bf16[128,2048]{1,0:T(8,128)(2,1)S(1)} collective-permute-done((bf16[128,2048]{1,0:T(8,128)(2,1)S(1)}, bf16[128,2048]{1,0:T(8,128)(2,1)S(1)}, u32[]{:S(2)}, u32[]{:S(2)}) %collective-permute-start) | collective-permute-done | bytes 524320 | tf_op jit(solution)/shard_map/ppermute | solution.py:277
  21.6 5.6 %collective-permute-start.4 = (bf16[128,2048]{1,0:T(8,128)(2,1)S(1)}, bf16[128,2048]{1,0:T(8,128)(2,1)S(1)}, u32[]{:S(2)}, u32[]{:S(2)}) collective-permute-start(bf16[128,2048]{1,0:T(8,128)(2,1)S(1)} %shard_map.29.mine_ref), channel_id=1, source_target_pairs={{0,120},{2,122},{4,124},{6,126},{8,0},{10,2},{12,4},{14,6},{16,8},... | collective-permute-start | bytes 1572872 | tf_op jit(solution)/shard_map/ppermute | solution.py:277
  27.2 2.6 %collective-permute-done.1.received_ref.refs_1_.refs_3_ = bf16[128,2048]{1,0:T(8,128)(2,1)S(1)} collective-permute-done((bf16[128,2048]{1,0:T(8,128)(2,1)S(1)}, bf16[128,2048]{1,0:T(8,128)(2,1)S(1)}, u32[]{:S(2)}, u32[]{:S(2)}) %collective-permute-start.1) | collective-permute-done | bytes 524320 | tf_op jit(solution)/shard_map/ppermute | solution.py:277
  32.8 5.6 %collective-permute-start.7 = (bf16[128,2048]{1,0:T(8,128)(2,1)S(1)}, bf16[128,2048]{1,0:T(8,128)(2,1)S(1)}, u32[]{:S(2)}, u32[]{:S(2)}) collective-permute-start(bf16[128,2048]{1,0:T(8,128)(2,1)S(1)} %shard_map.31.mine_ref), channel_id=1, source_target_pairs={{0,120},{2,122},{4,124},{6,126},{8,0},{10,2},{12,4},{14,6},{16,8},... | collective-permute-start | bytes 1572872 | tf_op jit(solution)/shard_map/ppermute | solution.py:277
  38.4 3.0 %shard_map.32.refs_8_ = f32[512,3584]{1,0:T(8,128)S(1)} custom-call(bf16[512,2048]{1,0:T(8,128)(2,1)S(1)} %get-tuple-element.1003.handed_ref, bf16[1024,2048]{1,0:T(8,128)(2,1)S(1)} %copy-done.1), custom_call_target="tpu_custom_call" | custom-call | flops 1 | bytes 1 | tf_op jit(solution)/shard_map/pallas_call | solution.py:118
  42.5 1.8 %collective-permute-start.9 = (bf16[128,2048]{1,0:T(8,128)(2,1)S(1)}, bf16[128,2048]{1,0:T(8,128)(2,1)S(1)}, u32[]{:S(2)}, u32[]{:S(2)}) collective-permute-start(bf16[128,2048]{1,0:T(8,128)(2,1)S(1)} %get-tuple-element.624), channel_id=1, source_target_pairs={{0,6},{2,0},{4,2},{6,4},{8,14},{10,8},{12,10},{14,12},{16,22},{18,... | collective-permute-start | bytes 1572872 | tf_op jit(solution)/shard_map/ppermute | solution.py:282
  44.3 5.3 %collective-permute-start.10 = (bf16[128,2048]{1,0:T(8,128)(2,1)S(1)}, bf16[128,2048]{1,0:T(8,128)(2,1)S(1)}, u32[]{:S(2)}, u32[]{:S(2)}) collective-permute-start(bf16[128,2048]{1,0:T(8,128)(2,1)S(1)} %shard_map.34.mine_ref), channel_id=1, source_target_pairs={{0,120},{2,122},{4,124},{6,126},{8,0},{10,2},{12,4},{14,6},{16,8},... | collective-permute-start | bytes 1572872 | tf_op jit(solution)/shard_map/ppermute | solution.py:277
  49.6 2.6 %collective-permute-done.7.refs_3_.received_ref.refs_5_ = bf16[128,2048]{1,0:T(8,128)(2,1)S(1)} collective-permute-done((bf16[128,2048]{1,0:T(8,128)(2,1)S(1)}, bf16[128,2048]{1,0:T(8,128)(2,1)S(1)}, u32[]{:S(2)}, u32[]{:S(2)}) %collective-permute-start.7) | collective-permute-done | bytes 524320 | tf_op jit(solution)/shard_map/ppermute | solution.py:277
  55.3 5.6 %collective-permute-start.13 = (bf16[128,2048]{1,0:T(8,128)(2,1)S(1)}, bf16[128,2048]{1,0:T(8,128)(2,1)S(1)}, u32[]{:S(2)}, u32[]{:S(2)}) collective-permute-start(bf16[128,2048]{1,0:T(8,128)(2,1)S(1)} %shard_map.36.mine_ref), channel_id=1, source_target_pairs={{0,120},{2,122},{4,124},{6,126},{8,0},{10,2},{12,4},{14,6},{16,8},... | collective-permute-start | bytes 1572872 | tf_op jit(solution)/shard_map/ppermute | solution.py:277
  60.9 2.4 %shard_map.37.refs_6_ = f32[512,3584]{1,0:T(8,128)S(1)} custom-call(bf16[512,2048]{1,0:T(8,128)(2,1)S(1)} %get-tuple-element.1003.handed_ref, bf16[128,2048]{1,0:T(8,128)(2,1)S(1)} %collective-permute-done.received_ref.refs_0_.refs_2_, bf16[128,2048]{1,0:T(8,128)(2,1)S(1)} %collective-permute-done.1.received_ref.refs_1_.refs_3_, ...), custom_call_target="tpu_custom_call", output_to_operand_aliasing={{}: (9, {})} | custom-call | flops 1 | bytes 1 | tf_op jit(solution)/shard_map/pallas_call | solution.py:118
  66.5 5.6 %collective-permute-start.16 = (bf16[128,2048]{1,0:T(8,128)(2,1)S(1)}, bf16[128,2048]{1,0:T(8,128)(2,1)S(1)}, u32[]{:S(2)}, u32[]{:S(2)}) collective-permute-start(bf16[128,2048]{1,0:T(8,128)(2,1)S(1)} %shard_map.39.mine_ref), channel_id=1, source_target_pairs={{0,120},{2,122},{4,124},{6,126},{8,0},{10,2},{12,4},{14,6},{16,8},... | collective-permute-start | bytes 1572872 | tf_op jit(solution)/shard_map/ppermute | solution.py:277
  72.1 2.6 %collective-permute-done.13.refs_1_.received_ref.refs_2_ = bf16[128,2048]{1,0:T(8,128)(2,1)S(1)} collective-permute-done((bf16[128,2048]{1,0:T(8,128)(2,1)S(1)}, bf16[128,2048]{1,0:T(8,128)(2,1)S(1)}, u32[]{:S(2)}, u32[]{:S(2)}) %collective-permute-start.13) | collective-permute-done | bytes 524320 | tf_op jit(solution)/shard_map/ppermute | solution.py:277
  77.8 5.8 %collective-permute-start.19 = (bf16[128,2048]{1,0:T(8,128)(2,1)S(1)}, bf16[128,2048]{1,0:T(8,128)(2,1)S(1)}, u32[]{:S(2)}, u32[]{:S(2)}) collective-permute-start(bf16[128,2048]{1,0:T(8,128)(2,1)S(1)} %shard_map.41.mine_ref), channel_id=1, source_target_pairs={{0,120},{2,122},{4,124},{6,126},{8,0},{10,2},{12,4},{14,6},{16,8},... | collective-permute-start | bytes 1572872 | tf_op jit(solution)/shard_map/ppermute | solution.py:277
  83.5 1.8 %shard_map.42.refs_6_ = f32[512,3584]{1,0:T(8,128)S(1)} custom-call(bf16[512,2048]{1,0:T(8,128)(2,1)S(1)} %get-tuple-element.1003.handed_ref, bf16[128,2048]{1,0:T(8,128)(2,1)S(1)} %collective-permute-done.10.received_ref.refs_0_.refs_1_, bf16[128,2048]{1,0:T(8,128)(2,1)S(1)} %collective-permute-done.13.refs_1_.received_ref.refs_2_, ...), custom_call_target="tpu_custom_call", output_to_operand_aliasing={{}: (7, {})} | custom-call | flops 1 | bytes 1 | tf_op jit(solution)/shard_map/pallas_call | solution.py:118
  88.9 8.2 %collective-permute-done.19.received_ref.refs_1_.refs_8_ = bf16[128,2048]{1,0:T(8,128)(2,1)S(1)} collective-permute-done((bf16[128,2048]{1,0:T(8,128)(2,1)S(1)}, bf16[128,2048]{1,0:T(8,128)(2,1)S(1)}, u32[]{:S(2)}, u32[]{:S(2)}) %collective-permute-start.19) | collective-permute-done | bytes 524320 | tf_op jit(solution)/shard_map/ppermute | solution.py:277
  101.3 2.3 %collective-permute-start.22 = (f32[384,256]{1,0:T(8,128)S(1)}, f32[384,256]{1,0:T(8,128)S(1)}, u32[]{:S(2)}, u32[]{:S(2)}) collective-permute-start(f32[384,256]{1,0:T(8,128)S(1)} %get-tuple-element.918), channel_id=1, source_target_pairs={{0,1},{1,0},{2,3},{3,2},{4,5},{5,4},{6,7},{7,6},{8,9},{9,8},{10,11... | collective-permute-start | bytes 1179656 | tf_op jit(solution)/shard_map/ppermute | solution.py:263
  103.7 1.8 %shard_map.48 = f32[512,3584]{1,0:T(8,128)S(1)} custom-call(bf16[512,2048]{1,0:T(8,128)(2,1)S(1)} %get-tuple-element.1003.handed_ref, bf16[128,2048]{1,0:T(8,128)(2,1)S(1)} %collective-permute-done.16.received_ref.refs_0_.refs_7_, bf16[128,2048]{1,0:T(8,128)(2,1)S(1)} %collective-permute-done.19.received_ref.refs_1_.refs_8_, ...), custom_call_target="tpu_custom_call", output_to_operand_aliasing={{}: (7, {})} | custom-call | flops 1 | bytes 1 | tf_op jit(solution)/shard_map/pallas_call | solution.py:118
  106.7 4.6 %collective-permute-done.24.refs_1_.refs_6_ = bf16[128,2048]{1,0:T(8,128)(2,1)S(1)} collective-permute-done((bf16[128,2048]{1,0:T(8,128)(2,1)S(1)}, bf16[128,2048]{1,0:T(8,128)(2,1)S(1)}, u32[]{:S(2)}, u32[]{:S(2)}) %collective-permute-start.24) | collective-permute-done | bytes 524320 | tf_op jit(solution)/shard_map/ppermute | solution.py:281
  111.3 2.1 %collective-permute-start.29 = (f32[512,3584]{1,0:T(8,128)S(1)}, f32[512,3584]{1,0:T(8,128)S(1)}, u32[]{:S(2)}, u32[]{:S(2)}) collective-permute-start(f32[512,3584]{1,0:T(8,128)S(1)} %shard_map.48), channel_id=1, source_target_pairs={{0,1},{1,0},{2,3},{3,2},{4,5},{5,4},{6,7},{7,6},{8,9},{9,8},{10,11... | collective-permute-start | bytes 22020104 | tf_op jit(solution)/shard_map/ppermute | solution.py:263
  113.4 7.7 %collective-permute-start.30 = (bf16[256,2048]{1,0:T(8,128)(2,1)S(1)}, bf16[256,2048]{1,0:T(8,128)(2,1)S(1)}, u32[]{:S(2)}, u32[]{:S(2)}) collective-permute-start(bf16[256,2048]{1,0:T(8,128)(2,1)S(1)} %pad_maximum_fusion), channel_id=1, source_target_pairs={{0,126},{2,0},{4,2},{6,4},{8,6},{10,8},{12,10},{14,12},{16,14},{18... | collective-permute-start | bytes 3145736 | tf_op jit(solution)/shard_map/ppermute | solution.py:358
  121.1 2.4 %shard_map.49 = (f32[128,768]{1,0:T(8,128)S(1)}, f32[128,768]{1,0:T(8,128)S(1)}) custom-call(s32[1]{0:T(128)} %bitcast.2._.where_ref, bf16[128,2048]{1,0:T(8,128)(2,1)S(1)} %collective-permute-done.3.refs_4_.refs_0_.refs_6_, bf16[128,2048]{1,0:T(8,128)(2,1)S(1)} %collective-permute-done.6.refs_5_.refs_1_.refs_7_, ...), custom_call_target="tpu_custom_call" | custom-call | flops 1 | bytes 1 | tf_op jit(solution)/shard_map/pallas_call | solution.py:207
  125.9 2.6 %shard_map.52 = f32[256,768]{1,0:T(8,128)S(1)} custom-call(s32[1]{0:T(128)} %bitcast.2._.where_ref, bf16[128,2048]{1,0:T(8,128)(2,1)S(1)} %collective-permute-done.3.refs_4_.refs_0_.refs_6_, bf16[128,2048]{1,0:T(8,128)(2,1)S(1)} %collective-permute-done.6.refs_5_.refs_1_.refs_7_, bf16[128,2048]{1,0:T(8,128)(2,1)S(1)} %collective-permute-done.9.refs_2_.refs_3_, ...), custom_call_target="tpu_custom_call" | custom-call | flops 1 | bytes 1 | tf_op jit(solution)/shard_map/pallas_call | solution.py:207
  129.5 7.0 %shard_map.53.refs_13_ = f32[5,512,1024]{2,1,0:T(8,128)} custom-call(f32[5]{0:T(128)S(1)} %pad_maximum_fusion.1.weights_ref, bf16[512,2048]{1,0:T(8,128)(2,1)S(1)} %get-tuple-element.1000.kept_ref, f32[512,3584]{1,0:T(8,128)S(1)} %collective-permute-done.29.refs_0_, bf16[1024,2048]{1,0:T(8,128)(2,1)S(1)} %copy-done.1, ...), custom_call_target="tpu_custom_call" | custom-call | flops 1 | bytes 1 | tf_op jit(solution)/shard_map/pallas_call | solution.py:161
  136.5 5.2 %shard_map.54._ = f32[5,512,1024]{2,1,0:T(8,128)} custom-call(f32[5]{0:T(128)S(1)} %pad_maximum_fusion.1.weights_ref, bf16[512,2048]{1,0:T(8,128)(2,1)S(1)} %get-tuple-element.1000.kept_ref, f32[512,3584]{1,0:T(8,128)S(1)} %collective-permute-done.29.refs_0_, ...), custom_call_target="tpu_custom_call", output_to_operand_aliasing={{}: (15, {})} | custom-call | flops 1 | bytes 1 | tf_op jit(solution)/shard_map/pallas_call | solution.py:161
  141.7 3.7 %collective-permute-done.31.summed_ref = f32[384,512]{1,0:T(8,128)S(1)} collective-permute-done((f32[384,512]{1,0:T(8,128)S(1)}, f32[384,512]{1,0:T(8,128)S(1)}, u32[]{:S(2)}, u32[]{:S(2)}) %collective-permute-start.31) | collective-permute-done | bytes 786464 | tf_op jit(solution)/shard_map/ppermute | solution.py:357
  146.2 1.9 %collective-permute-start.34 = (f32[512,256]{1,0:T(8,128)S(1)}, f32[512,256]{1,0:T(8,128)S(1)}, u32[]{:S(2)}, u32[]{:S(2)}) collective-permute-start(f32[512,256]{1,0:T(8,128)S(1)} %shard_map.55), channel_id=1, source_target_pairs={{0,1},{1,0},{2,3},{3,2},{4,5},{5,4},{6,7},{7,6},{8,9},{9,8},{10,11... | collective-permute-start | bytes 1572872 | tf_op jit(solution)/shard_map/ppermute | solution.py:263
  151.1 3.4 %shard_map.57._ = f32[5,512,1024]{2,1,0:T(8,128)} custom-call(f32[5]{0:T(128)S(1)} %pad_maximum_fusion.1.weights_ref, bf16[512,2048]{1,0:T(8,128)(2,1)S(1)} %get-tuple-element.1000.kept_ref, f32[512,256]{1,0:T(8,128)S(1)} %collective-permute-done.32.refs_0_, f32[512,256]{1,0:T(8,128)S(1)} %collective-permute-done.33.refs_1_, ...), custom_call_target="tpu_custom_call", output_to_operand_aliasing={{}: (10, {})} | custom-call | flops 1 | bytes 1 | tf_op jit(solution)/shard_map/pallas_call | solution.py:161
  154.5 7.8 %collective-permute-done.28.summed_ref = f32[256,768]{1,0:T(8,128)S(1)} collective-permute-done((f32[256,768]{1,0:T(8,128)S(1)}, f32[256,768]{1,0:T(8,128)S(1)}, u32[]{:S(2)}, u32[]{:S(2)}) %collective-permute-start.28) | collective-permute-done | bytes 786464 | tf_op jit(solution)/shard_map/ppermute | solution.py:360
  162.3 1.5 shard_map.58
  (80 shorter events, 34.3 us)
Async XLA Ops:
  1.1 17.4 %collective-permute-start = (bf16[128,2048]{1,0:T(8,128)(2,1)S(1)}, bf16[128,2048]{1,0:T(8,128)(2,1)S(1)}, u32[]{:S(2)}, u32[]{:S(2)}) collective-permute-start(bf16[128,2048]{1,0:T(8,128)(2,1)S(1)} %slice.3.mine_ref), channel_id=1, source_target_pairs={{0,120},{2,122},{4,124},{6,126},{8,0},{10,2},{12,4},{14,6},{16,8},... | collective-permute-start | bytes 1572872 | tf_op jit(solution)/shard_map/ppermute | solution.py:277
  10.2 19.6 %collective-permute-start.1 = (bf16[128,2048]{1,0:T(8,128)(2,1)S(1)}, bf16[128,2048]{1,0:T(8,128)(2,1)S(1)}, u32[]{:S(2)}, u32[]{:S(2)}) collective-permute-start(bf16[128,2048]{1,0:T(8,128)(2,1)S(1)} %shard_map.28.mine_ref), channel_id=1, source_target_pairs={{0,120},{2,122},{4,124},{6,126},{8,0},{10,2},{12,4},{14,6},{16,8},... | collective-permute-start | bytes 1572872 | tf_op jit(solution)/shard_map/ppermute | solution.py:277
  18.6 14.1 %collective-permute-start.2 = (bf16[128,2048]{1,0:T(8,128)(2,1)S(1)}, bf16[128,2048]{1,0:T(8,128)(2,1)S(1)}, u32[]{:S(2)}, u32[]{:S(2)}) collective-permute-start(bf16[128,2048]{1,0:T(8,128)(2,1)S(1)} %get-tuple-element.522), channel_id=1, source_target_pairs={{0,2},{2,4},{4,6},{6,0},{8,10},{10,12},{12,14},{14,8},{16,18},{18,... | collective-permute-start | bytes 1572872 | tf_op jit(solution)/shard_map/ppermute | solution.py:281
  20.0 12.8 %collective-permute-start.3 = (bf16[128,2048]{1,0:T(8,128)(2,1)S(1)}, bf16[128,2048]{1,0:T(8,128)(2,1)S(1)}, u32[]{:S(2)}, u32[]{:S(2)}) collective-permute-start(bf16[128,2048]{1,0:T(8,128)(2,1)S(1)} %get-tuple-element.532), channel_id=1, source_target_pairs={{0,6},{2,0},{4,2},{6,4},{8,14},{10,8},{12,10},{14,12},{16,22},{18,... | collective-permute-start | bytes 1572872 | tf_op jit(solution)/shard_map/ppermute | solution.py:282
  21.6 19.8 %collective-permute-start.4 = (bf16[128,2048]{1,0:T(8,128)(2,1)S(1)}, bf16[128,2048]{1,0:T(8,128)(2,1)S(1)}, u32[]{:S(2)}, u32[]{:S(2)}) collective-permute-start(bf16[128,2048]{1,0:T(8,128)(2,1)S(1)} %shard_map.29.mine_ref), channel_id=1, source_target_pairs={{0,120},{2,122},{4,124},{6,126},{8,0},{10,2},{12,4},{14,6},{16,8},... | collective-permute-start | bytes 1572872 | tf_op jit(solution)/shard_map/ppermute | solution.py:277
  29.9 14.4 %collective-permute-start.5 = (bf16[128,2048]{1,0:T(8,128)(2,1)S(1)}, bf16[128,2048]{1,0:T(8,128)(2,1)S(1)}, u32[]{:S(2)}, u32[]{:S(2)}) collective-permute-start(bf16[128,2048]{1,0:T(8,128)(2,1)S(1)} %get-tuple-element.557), channel_id=1, source_target_pairs={{0,2},{2,4},{4,6},{6,0},{8,10},{10,12},{12,14},{14,8},{16,18},{18,... | collective-permute-start | bytes 1572872 | tf_op jit(solution)/shard_map/ppermute | solution.py:281
  31.2 13.0 %collective-permute-start.6 = (bf16[128,2048]{1,0:T(8,128)(2,1)S(1)}, bf16[128,2048]{1,0:T(8,128)(2,1)S(1)}, u32[]{:S(2)}, u32[]{:S(2)}) collective-permute-start(bf16[128,2048]{1,0:T(8,128)(2,1)S(1)} %get-tuple-element.571), channel_id=1, source_target_pairs={{0,6},{2,0},{4,2},{6,4},{8,14},{10,8},{12,10},{14,12},{16,22},{18,... | collective-permute-start | bytes 1572872 | tf_op jit(solution)/shard_map/ppermute | solution.py:282
  32.8 19.4 %collective-permute-start.7 = (bf16[128,2048]{1,0:T(8,128)(2,1)S(1)}, bf16[128,2048]{1,0:T(8,128)(2,1)S(1)}, u32[]{:S(2)}, u32[]{:S(2)}) collective-permute-start(bf16[128,2048]{1,0:T(8,128)(2,1)S(1)} %shard_map.31.mine_ref), channel_id=1, source_target_pairs={{0,120},{2,122},{4,124},{6,126},{8,0},{10,2},{12,4},{14,6},{16,8},... | collective-permute-start | bytes 1572872 | tf_op jit(solution)/shard_map/ppermute | solution.py:277
  41.5 13.7 %collective-permute-start.8 = (bf16[128,2048]{1,0:T(8,128)(2,1)S(1)}, bf16[128,2048]{1,0:T(8,128)(2,1)S(1)}, u32[]{:S(2)}, u32[]{:S(2)}) collective-permute-start(bf16[128,2048]{1,0:T(8,128)(2,1)S(1)} %get-tuple-element.607), channel_id=1, source_target_pairs={{0,2},{2,4},{4,6},{6,0},{8,10},{10,12},{12,14},{14,8},{16,18},{18,... | collective-permute-start | bytes 1572872 | tf_op jit(solution)/shard_map/ppermute | solution.py:281
  42.5 12.8 %collective-permute-start.9 = (bf16[128,2048]{1,0:T(8,128)(2,1)S(1)}, bf16[128,2048]{1,0:T(8,128)(2,1)S(1)}, u32[]{:S(2)}, u32[]{:S(2)}) collective-permute-start(bf16[128,2048]{1,0:T(8,128)(2,1)S(1)} %get-tuple-element.624), channel_id=1, source_target_pairs={{0,6},{2,0},{4,2},{6,4},{8,14},{10,8},{12,10},{14,12},{16,22},{18,... | collective-permute-start | bytes 1572872 | tf_op jit(solution)/shard_map/ppermute | solution.py:282
  44.3 19.1 %collective-permute-start.10 = (bf16[128,2048]{1,0:T(8,128)(2,1)S(1)}, bf16[128,2048]{1,0:T(8,128)(2,1)S(1)}, u32[]{:S(2)}, u32[]{:S(2)}) collective-permute-start(bf16[128,2048]{1,0:T(8,128)(2,1)S(1)} %shard_map.34.mine_ref), channel_id=1, source_target_pairs={{0,120},{2,122},{4,124},{6,126},{8,0},{10,2},{12,4},{14,6},{16,8},... | collective-permute-start | bytes 1572872 | tf_op jit(solution)/shard_map/ppermute | solution.py:277
  52.3 14.1 %collective-permute-start.11 = (bf16[128,2048]{1,0:T(8,128)(2,1)S(1)}, bf16[128,2048]{1,0:T(8,128)(2,1)S(1)}, u32[]{:S(2)}, u32[]{:S(2)}) collective-permute-start(bf16[128,2048]{1,0:T(8,128)(2,1)S(1)} %get-tuple-element.665), channel_id=1, source_target_pairs={{0,2},{2,4},{4,6},{6,0},{8,10},{10,12},{12,14},{14,8},{16,18},{18,... | collective-permute-start | bytes 1572872 | tf_op jit(solution)/shard_map/ppermute | solution.py:281
  53.7 12.8 %collective-permute-start.12 = (bf16[128,2048]{1,0:T(8,128)(2,1)S(1)}, bf16[128,2048]{1,0:T(8,128)(2,1)S(1)}, u32[]{:S(2)}, u32[]{:S(2)}) collective-permute-start(bf16[128,2048]{1,0:T(8,128)(2,1)S(1)} %get-tuple-element.680), channel_id=1, source_target_pairs={{0,6},{2,0},{4,2},{6,4},{8,14},{10,8},{12,10},{14,12},{16,22},{18,... | collective-permute-start | bytes 1572872 | tf_op jit(solution)/shard_map/ppermute | solution.py:282
  55.3 19.4 %collective-permute-start.13 = (bf16[128,2048]{1,0:T(8,128)(2,1)S(1)}, bf16[128,2048]{1,0:T(8,128)(2,1)S(1)}, u32[]{:S(2)}, u32[]{:S(2)}) collective-permute-start(bf16[128,2048]{1,0:T(8,128)(2,1)S(1)} %shard_map.36.mine_ref), channel_id=1, source_target_pairs={{0,120},{2,122},{4,124},{6,126},{8,0},{10,2},{12,4},{14,6},{16,8},... | collective-permute-start | bytes 1572872 | tf_op jit(solution)/shard_map/ppermute | solution.py:277
  63.6 12.6 %collective-permute-start.14 = (bf16[128,2048]{1,0:T(8,128)(2,1)S(1)}, bf16[128,2048]{1,0:T(8,128)(2,1)S(1)}, u32[]{:S(2)}, u32[]{:S(2)}) collective-permute-start(bf16[128,2048]{1,0:T(8,128)(2,1)S(1)} %get-tuple-element.724), channel_id=1, source_target_pairs={{0,2},{2,4},{4,6},{6,0},{8,10},{10,12},{12,14},{14,8},{16,18},{18,... | collective-permute-start | bytes 1572872 | tf_op jit(solution)/shard_map/ppermute | solution.py:281
  64.9 12.8 %collective-permute-start.15 = (bf16[128,2048]{1,0:T(8,128)(2,1)S(1)}, bf16[128,2048]{1,0:T(8,128)(2,1)S(1)}, u32[]{:S(2)}, u32[]{:S(2)}) collective-permute-start(bf16[128,2048]{1,0:T(8,128)(2,1)S(1)} %get-tuple-element.741), channel_id=1, source_target_pairs={{0,6},{2,0},{4,2},{6,4},{8,14},{10,8},{12,10},{14,12},{16,22},{18,... | collective-permute-start | bytes 1572872 | tf_op jit(solution)/shard_map/ppermute | solution.py:282
  66.5 19.4 %collective-permute-start.16 = (bf16[128,2048]{1,0:T(8,128)(2,1)S(1)}, bf16[128,2048]{1,0:T(8,128)(2,1)S(1)}, u32[]{:S(2)}, u32[]{:S(2)}) collective-permute-start(bf16[128,2048]{1,0:T(8,128)(2,1)S(1)} %shard_map.39.mine_ref), channel_id=1, source_target_pairs={{0,120},{2,122},{4,124},{6,126},{8,0},{10,2},{12,4},{14,6},{16,8},... | collective-permute-start | bytes 1572872 | tf_op jit(solution)/shard_map/ppermute | solution.py:277
  74.8 14.1 %collective-permute-start.17 = (bf16[128,2048]{1,0:T(8,128)(2,1)S(1)}, bf16[128,2048]{1,0:T(8,128)(2,1)S(1)}, u32[]{:S(2)}, u32[]{:S(2)}) collective-permute-start(bf16[128,2048]{1,0:T(8,128)(2,1)S(1)} %get-tuple-element.792), channel_id=1, source_target_pairs={{0,2},{2,4},{4,6},{6,0},{8,10},{10,12},{12,14},{14,8},{16,18},{18,... | collective-permute-start | bytes 1572872 | tf_op jit(solution)/shard_map/ppermute | solution.py:281
  76.2 12.8 %collective-permute-start.18 = (bf16[128,2048]{1,0:T(8,128)(2,1)S(1)}, bf16[128,2048]{1,0:T(8,128)(2,1)S(1)}, u32[]{:S(2)}, u32[]{:S(2)}) collective-permute-start(bf16[128,2048]{1,0:T(8,128)(2,1)S(1)} %get-tuple-element.811), channel_id=1, source_target_pairs={{0,6},{2,0},{4,2},{6,4},{8,14},{10,8},{12,10},{14,12},{16,22},{18,... | collective-permute-start | bytes 1572872 | tf_op jit(solution)/shard_map/ppermute | solution.py:282
  77.8 19.4 %collective-permute-start.19 = (bf16[128,2048]{1,0:T(8,128)(2,1)S(1)}, bf16[128,2048]{1,0:T(8,128)(2,1)S(1)}, u32[]{:S(2)}, u32[]{:S(2)}) collective-permute-start(bf16[128,2048]{1,0:T(8,128)(2,1)S(1)} %shard_map.41.mine_ref), channel_id=1, source_target_pairs={{0,120},{2,122},{4,124},{6,126},{8,0},{10,2},{12,4},{14,6},{16,8},... | collective-permute-start | bytes 1572872 | tf_op jit(solution)/shard_map/ppermute | solution.py:277
  86.1 14.1 %collective-permute-start.20 = (bf16[128,2048]{1,0:T(8,128)(2,1)S(1)}, bf16[128,2048]{1,0:T(8,128)(2,1)S(1)}, u32[]{:S(2)}, u32[]{:S(2)}) collective-permute-start(bf16[128,2048]{1,0:T(8,128)(2,1)S(1)} %get-tuple-element.868), channel_id=1, source_target_pairs={{0,2},{2,4},{4,6},{6,0},{8,10},{10,12},{12,14},{14,8},{16,18},{18,... | collective-permute-start | bytes 1572872 | tf_op jit(solution)/shard_map/ppermute | solution.py:281
  87.4 12.8 %collective-permute-start.21 = (bf16[128,2048]{1,0:T(8,128)(2,1)S(1)}, bf16[128,2048]{1,0:T(8,128)(2,1)S(1)}, u32[]{:S(2)}, u32[]{:S(2)}) collective-permute-start(bf16[128,2048]{1,0:T(8,128)(2,1)S(1)} %get-tuple-element.888), channel_id=1, source_target_pairs={{0,6},{2,0},{4,2},{6,4},{8,14},{10,8},{12,10},{14,12},{16,22},{18,... | collective-permute-start | bytes 1572872 | tf_op jit(solution)/shard_map/ppermute | solution.py:282
  97.3 14.0 %collective-permute-start.24 = (bf16[128,2048]{1,0:T(8,128)(2,1)S(1)}, bf16[128,2048]{1,0:T(8,128)(2,1)S(1)}, u32[]{:S(2)}, u32[]{:S(2)}) collective-permute-start(bf16[128,2048]{1,0:T(8,128)(2,1)S(1)} %get-tuple-element.925), channel_id=1, source_target_pairs={{0,2},{2,4},{4,6},{6,0},{8,10},{10,12},{12,14},{14,8},{16,18},{18,... | collective-permute-start | bytes 1572872 | tf_op jit(solution)/shard_map/ppermute | solution.py:281
  98.6 12.6 %collective-permute-start.25 = (bf16[128,2048]{1,0:T(8,128)(2,1)S(1)}, bf16[128,2048]{1,0:T(8,128)(2,1)S(1)}, u32[]{:S(2)}, u32[]{:S(2)}) collective-permute-start(bf16[128,2048]{1,0:T(8,128)(2,1)S(1)} %get-tuple-element.945), channel_id=1, source_target_pairs={{0,6},{2,0},{4,2},{6,4},{8,14},{10,8},{12,10},{14,12},{16,22},{18,... | collective-permute-start | bytes 1572872 | tf_op jit(solution)/shard_map/ppermute | solution.py:282
  101.3 4.2 %collective-permute-start.22 = (f32[384,256]{1,0:T(8,128)S(1)}, f32[384,256]{1,0:T(8,128)S(1)}, u32[]{:S(2)}, u32[]{:S(2)}) collective-permute-start(f32[384,256]{1,0:T(8,128)S(1)} %get-tuple-element.918), channel_id=1, source_target_pairs={{0,1},{1,0},{2,3},{3,2},{4,5},{5,4},{6,7},{7,6},{8,9},{9,8},{10,11... | collective-permute-start | bytes 1179656 | tf_op jit(solution)/shard_map/ppermute | solution.py:263
  111.3 18.2 %collective-permute-start.29 = (f32[512,3584]{1,0:T(8,128)S(1)}, f32[512,3584]{1,0:T(8,128)S(1)}, u32[]{:S(2)}, u32[]{:S(2)}) collective-permute-start(f32[512,3584]{1,0:T(8,128)S(1)} %shard_map.48), channel_id=1, source_target_pairs={{0,1},{1,0},{2,3},{3,2},{4,5},{5,4},{6,7},{7,6},{8,9},{9,8},{10,11... | collective-permute-start | bytes 22020104 | tf_op jit(solution)/shard_map/ppermute | solution.py:263
  113.4 32.0 %collective-permute-start.30 = (bf16[256,2048]{1,0:T(8,128)(2,1)S(1)}, bf16[256,2048]{1,0:T(8,128)(2,1)S(1)}, u32[]{:S(2)}, u32[]{:S(2)}) collective-permute-start(bf16[256,2048]{1,0:T(8,128)(2,1)S(1)} %pad_maximum_fusion), channel_id=1, source_target_pairs={{0,126},{2,0},{4,2},{6,4},{8,6},{10,8},{12,10},{14,12},{16,14},{18... | collective-permute-start | bytes 3145736 | tf_op jit(solution)/shard_map/ppermute | solution.py:358
  121.1 24.3 %collective-permute-start.31 = (f32[384,512]{1,0:T(8,128)S(1)}, f32[384,512]{1,0:T(8,128)S(1)}, u32[]{:S(2)}, u32[]{:S(2)}) collective-permute-start(f32[384,512]{1,0:T(8,128)S(1)} %shard_map.46), channel_id=1, source_target_pairs={{0,2},{2,4},{4,6},{6,8},{8,10},{10,12},{12,14},{14,16},{16,18},{18... | collective-permute-start | bytes 2359304 | tf_op jit(solution)/shard_map/ppermute | solution.py:357
  128.5 33.8 %collective-permute-start.28 = (f32[256,768]{1,0:T(8,128)S(1)}, f32[256,768]{1,0:T(8,128)S(1)}, u32[]{:S(2)}, u32[]{:S(2)}) collective-permute-start(f32[256,768]{1,0:T(8,128)S(1)} %shard_map.52), channel_id=1, source_target_pairs={{0,2},{2,4},{4,6},{6,8},{8,10},{10,12},{12,14},{14,16},{16,18},{18... | collective-permute-start | bytes 2359304 | tf_op jit(solution)/shard_map/ppermute | solution.py:360
  146.2 3.9 %collective-permute-start.34 = (f32[512,256]{1,0:T(8,128)S(1)}, f32[512,256]{1,0:T(8,128)S(1)}, u32[]{:S(2)}, u32[]{:S(2)}) collective-permute-start(f32[512,256]{1,0:T(8,128)S(1)} %shard_map.55), channel_id=1, source_target_pairs={{0,1},{1,0},{2,3},{3,2},{4,5},{5,4},{6,7},{7,6},{8,9},{9,8},{10,11... | collective-permute-start | bytes 1572872 | tf_op jit(solution)/shard_map/ppermute | solution.py:263
  148.1 2.3 %collective-permute-start.32 = (f32[512,256]{1,0:T(8,128)S(1)}, f32[512,256]{1,0:T(8,128)S(1)}, u32[]{:S(2)}, u32[]{:S(2)}) collective-permute-start(f32[512,256]{1,0:T(8,128)S(1)} %shard_map.50), channel_id=1, source_target_pairs={{0,1},{1,0},{2,3},{3,2},{4,5},{5,4},{6,7},{7,6},{8,9},{9,8},{10,11... | collective-permute-start | bytes 1572872 | tf_op jit(solution)/shard_map/ppermute | solution.py:263
  148.2 2.9 %collective-permute-start.33 = (f32[512,256]{1,0:T(8,128)S(1)}, f32[512,256]{1,0:T(8,128)S(1)}, u32[]{:S(2)}, u32[]{:S(2)}) collective-permute-start(f32[512,256]{1,0:T(8,128)S(1)} %shard_map.51), channel_id=1, source_target_pairs={{0,1},{1,0},{2,3},{3,2},{4,5},{5,4},{6,7},{7,6},{8,9},{9,8},{10,11... | collective-permute-start | bytes 1572872 | tf_op jit(solution)/shard_map/ppermute | solution.py:263
  (6 other events, 24.4 us)

commit v5 on v4

--- a/solution.py
+++ b/solution.py
@@ -217,17 +217,16 @@
 
 def scaled_write(out, weights, made, k, regions):
     def kernel(weights_ref, summed_ref, _, out_ref, made_ref, sems):
-        made_ref[...] = summed_ref[...] * weights_ref[k]
-        copies = [
-            pltpu.make_async_copy(
-                made_ref.at[pl.ds(row, height), pl.ds(column, size)],
+        copies = []
+        for n, (row, column, height, size, to_row, to_column) in enumerate(regions):
+            at = pl.ds(row, height), pl.ds(column, size)
+            made_ref[at] = summed_ref[at] * weights_ref[k]
+            copies.append(pltpu.make_async_copy(
+                made_ref.at[at],
                 out_ref.at[k, pl.ds(to_row, height), pl.ds(to_column, size)],
                 sems.at[n],
-            )
-            for n, (row, column, height, size, to_row, to_column) in enumerate(regions)
-        ]
-        for copy in copies:
-            copy.start()
+            ))
+            copies[-1].start()
         for copy in copies:
             copy.wait()
 

time: 164 us -> 164 us (level)
  no operation moved by 1% of the time
where the time goes in v5:
time: 164 us
  starting transfers between devices  79.8 us (49%)
  waiting for transfers between devices  39.1 us (24%)
  Pallas kernels  38.2 us (23%)
  local copies, waits for them, and re-layouts  6.15 us (4%)
    ppermute x8, starting transfers between devices, fetch4(): return ((4, p), lax.ppermute(s['held'][0, p], 'blk', below(4)))  40.9 us
    ppermute x8, waiting for transfers between devices, fetch4(): return ((4, p), lax.ppermute(s['held'][0, p], 'blk', below(4)))  21.7 us
    pallas_call x3, Pallas kernels, kept_products(): pl.pallas_call(kernel, out_shape=jax.ShapeDtypeStruct((5, half, 2 * half)...  15.6 us
    ppermute x8, starting transfers between devices, fetch13(): d.append(((1, p), lax.ppermute(down, 'blk', around(-1))))  12.5 us
    pallas_call x7, Pallas kernels, handed_products(): pl.pallas_call(kernel, out_shape=jax.ShapeDtypeStruct((half, room), jnp.f...  11.2 us
    ppermute x8, starting transfers between devices, fetch13(): u.append(((3, p), lax.ppermute(up, 'blk', around(1))))  10.5 us
    ppermute x1, waiting for transfers between devices, body(): last_sums = lax.ppermute(ahead(late, third, fourth), 'blk', below(-1))  7.79 us
    ppermute x1, starting transfers between devices, body(): relayed = lax.ppermute(jnp.concatenate(part(1, 3)), 'blk', below(1))  7.71 us
  transfers between devices with their start and end apart: 35, of which 13 were waited for; matrix products, arithmetic and copies ran while one was open for 2% of the time, Pallas kernels for 22%

profile of v5, /device:TPU:1, one launch (start us, length us, event | category | flops | bytes accessed | tf_op | source)
XLA Modules:
  0.0 163.9 jit_solution(4994200926374029216)
XLA Ops:
  1.1 6.8 %collective-permute-start = (bf16[128,2048]{1,0:T(8,128)(2,1)S(1)}, bf16[128,2048]{1,0:T(8,128)(2,1)S(1)}, u32[]{:S(2)}, u32[]{:S(2)}) collective-permute-start(bf16[128,2048]{1,0:T(8,128)(2,1)S(1)} %slice.3.mine_ref), channel_id=1, source_target_pairs={{0,120},{2,122},{4,124},{6,126},{8,0},{10,2},{12,4},{14,6},{16,8},... | collective-permute-start | bytes 1572872 | tf_op jit(solution)/shard_map/ppermute | solution.py:276
  7.9 2.2 %copy-done = bf16[1024,2048]{1,0:T(8,128)(2,1)S(1)} copy-done((bf16[1024,2048]{1,0:T(8,128)(2,1)S(1)}, bf16[1024,2048]{1,0:T(8,128)(2,1)}, u32[]{:S(2)}) %copy-start) | copy-done | bytes 4194328
  10.8 2.9 %constant_dynamic-slice_fusion = (bf16[512,2048]{1,0:T(8,128)(2,1)S(1)}, bf16[512,2048]{1,0:T(8,128)(2,1)S(1)}) fusion(bf16[1024,2048]{1,0:T(8,128)(2,1)} %refs_1_.1, s32[]{:T(128)S(6)} %select_n.15, s32[]{:T(128)S(6)} %select_n.13), kind=kLoop, calls=%fused_computation.2 | loop fusion | bytes 8388616 | tf_op jit(solution)/shard_map/dynamic_slice | solution.py:313
  13.7 4.8 %collective-permute-done.received_ref.refs_0_.refs_2_ = bf16[128,2048]{1,0:T(8,128)(2,1)S(1)} collective-permute-done((bf16[128,2048]{1,0:T(8,128)(2,1)S(1)}, bf16[128,2048]{1,0:T(8,128)(2,1)S(1)}, u32[]{:S(2)}, u32[]{:S(2)}) %collective-permute-start) | collective-permute-done | bytes 524320 | tf_op jit(solution)/shard_map/ppermute | solution.py:276
  21.6 5.6 %collective-permute-start.4 = (bf16[128,2048]{1,0:T(8,128)(2,1)S(1)}, bf16[128,2048]{1,0:T(8,128)(2,1)S(1)}, u32[]{:S(2)}, u32[]{:S(2)}) collective-permute-start(bf16[128,2048]{1,0:T(8,128)(2,1)S(1)} %shard_map.29.mine_ref), channel_id=1, source_target_pairs={{0,120},{2,122},{4,124},{6,126},{8,0},{10,2},{12,4},{14,6},{16,8},... | collective-permute-start | bytes 1572872 | tf_op jit(solution)/shard_map/ppermute | solution.py:276
  27.2 2.6 %collective-permute-done.1.received_ref.refs_1_.refs_3_ = bf16[128,2048]{1,0:T(8,128)(2,1)S(1)} collective-permute-done((bf16[128,2048]{1,0:T(8,128)(2,1)S(1)}, bf16[128,2048]{1,0:T(8,128)(2,1)S(1)}, u32[]{:S(2)}, u32[]{:S(2)}) %collective-permute-start.1) | collective-permute-done | bytes 524320 | tf_op jit(solution)/shard_map/ppermute | solution.py:276
  32.8 5.6 %collective-permute-start.7 = (bf16[128,2048]{1,0:T(8,128)(2,1)S(1)}, bf16[128,2048]{1,0:T(8,128)(2,1)S(1)}, u32[]{:S(2)}, u32[]{:S(2)}) collective-permute-start(bf16[128,2048]{1,0:T(8,128)(2,1)S(1)} %shard_map.31.mine_ref), channel_id=1, source_target_pairs={{0,120},{2,122},{4,124},{6,126},{8,0},{10,2},{12,4},{14,6},{16,8},... | collective-permute-start | bytes 1572872 | tf_op jit(solution)/shard_map/ppermute | solution.py:276
  38.4 3.0 %shard_map.32.refs_8_ = f32[512,3584]{1,0:T(8,128)S(1)} custom-call(bf16[512,2048]{1,0:T(8,128)(2,1)S(1)} %get-tuple-element.1003.handed_ref, bf16[1024,2048]{1,0:T(8,128)(2,1)S(1)} %copy-done.1), custom_call_target="tpu_custom_call" | custom-call | flops 1 | bytes 1 | tf_op jit(solution)/shard_map/pallas_call | solution.py:118
  42.5 1.8 %collective-permute-start.9 = (bf16[128,2048]{1,0:T(8,128)(2,1)S(1)}, bf16[128,2048]{1,0:T(8,128)(2,1)S(1)}, u32[]{:S(2)}, u32[]{:S(2)}) collective-permute-start(bf16[128,2048]{1,0:T(8,128)(2,1)S(1)} %get-tuple-element.624), channel_id=1, source_target_pairs={{0,6},{2,0},{4,2},{6,4},{8,14},{10,8},{12,10},{14,12},{16,22},{18,... | collective-permute-start | bytes 1572872 | tf_op jit(solution)/shard_map/ppermute | solution.py:281
  44.3 5.3 %collective-permute-start.10 = (bf16[128,2048]{1,0:T(8,128)(2,1)S(1)}, bf16[128,2048]{1,0:T(8,128)(2,1)S(1)}, u32[]{:S(2)}, u32[]{:S(2)}) collective-permute-start(bf16[128,2048]{1,0:T(8,128)(2,1)S(1)} %shard_map.34.mine_ref), channel_id=1, source_target_pairs={{0,120},{2,122},{4,124},{6,126},{8,0},{10,2},{12,4},{14,6},{16,8},... | collective-permute-start | bytes 1572872 | tf_op jit(solution)/shard_map/ppermute | solution.py:276
  49.6 2.6 %collective-permute-done.7.refs_3_.received_ref.refs_5_ = bf16[128,2048]{1,0:T(8,128)(2,1)S(1)} collective-permute-done((bf16[128,2048]{1,0:T(8,128)(2,1)S(1)}, bf16[128,2048]{1,0:T(8,128)(2,1)S(1)}, u32[]{:S(2)}, u32[]{:S(2)}) %collective-permute-start.7) | collective-permute-done | bytes 524320 | tf_op jit(solution)/shard_map/ppermute | solution.py:276
  55.3 5.6 %collective-permute-start.13 = (bf16[128,2048]{1,0:T(8,128)(2,1)S(1)}, bf16[128,2048]{1,0:T(8,128)(2,1)S(1)}, u32[]{:S(2)}, u32[]{:S(2)}) collective-permute-start(bf16[128,2048]{1,0:T(8,128)(2,1)S(1)} %shard_map.36.mine_ref), channel_id=1, source_target_pairs={{0,120},{2,122},{4,124},{6,126},{8,0},{10,2},{12,4},{14,6},{16,8},... | collective-permute-start | bytes 1572872 | tf_op jit(solution)/shard_map/ppermute | solution.py:276
  60.9 2.4 %shard_map.37.refs_6_ = f32[512,3584]{1,0:T(8,128)S(1)} custom-call(bf16[512,2048]{1,0:T(8,128)(2,1)S(1)} %get-tuple-element.1003.handed_ref, bf16[128,2048]{1,0:T(8,128)(2,1)S(1)} %collective-permute-done.received_ref.refs_0_.refs_2_, bf16[128,2048]{1,0:T(8,128)(2,1)S(1)} %collective-permute-done.1.received_ref.refs_1_.refs_3_, ...), custom_call_target="tpu_custom_call", output_to_operand_aliasing={{}: (9, {})} | custom-call | flops 1 | bytes 1 | tf_op jit(solution)/shard_map/pallas_call | solution.py:118
  66.5 5.6 %collective-permute-start.16 = (bf16[128,2048]{1,0:T(8,128)(2,1)S(1)}, bf16[128,2048]{1,0:T(8,128)(2,1)S(1)}, u32[]{:S(2)}, u32[]{:S(2)}) collective-permute-start(bf16[128,2048]{1,0:T(8,128)(2,1)S(1)} %shard_map.39.mine_ref), channel_id=1, source_target_pairs={{0,120},{2,122},{4,124},{6,126},{8,0},{10,2},{12,4},{14,6},{16,8},... | collective-permute-start | bytes 1572872 | tf_op jit(solution)/shard_map/ppermute | solution.py:276
  72.1 2.6 %collective-permute-done.13.refs_1_.received_ref.refs_2_ = bf16[128,2048]{1,0:T(8,128)(2,1)S(1)} collective-permute-done((bf16[128,2048]{1,0:T(8,128)(2,1)S(1)}, bf16[128,2048]{1,0:T(8,128)(2,1)S(1)}, u32[]{:S(2)}, u32[]{:S(2)}) %collective-permute-start.13) | collective-permute-done | bytes 524320 | tf_op jit(solution)/shard_map/ppermute | solution.py:276
  76.2 1.5 collective-permute-start.18
  77.8 5.8 %collective-permute-start.19 = (bf16[128,2048]{1,0:T(8,128)(2,1)S(1)}, bf16[128,2048]{1,0:T(8,128)(2,1)S(1)}, u32[]{:S(2)}, u32[]{:S(2)}) collective-permute-start(bf16[128,2048]{1,0:T(8,128)(2,1)S(1)} %shard_map.41.mine_ref), channel_id=1, source_target_pairs={{0,120},{2,122},{4,124},{6,126},{8,0},{10,2},{12,4},{14,6},{16,8},... | collective-permute-start | bytes 1572872 | tf_op jit(solution)/shard_map/ppermute | solution.py:276
  83.5 1.8 %shard_map.42.refs_6_ = f32[512,3584]{1,0:T(8,128)S(1)} custom-call(bf16[512,2048]{1,0:T(8,128)(2,1)S(1)} %get-tuple-element.1003.handed_ref, bf16[128,2048]{1,0:T(8,128)(2,1)S(1)} %collective-permute-done.10.received_ref.refs_0_.refs_1_, bf16[128,2048]{1,0:T(8,128)(2,1)S(1)} %collective-permute-done.13.refs_1_.received_ref.refs_2_, ...), custom_call_target="tpu_custom_call", output_to_operand_aliasing={{}: (7, {})} | custom-call | flops 1 | bytes 1 | tf_op jit(solution)/shard_map/pallas_call | solution.py:118
  88.9 8.2 %collective-permute-done.19.received_ref.refs_1_.refs_8_ = bf16[128,2048]{1,0:T(8,128)(2,1)S(1)} collective-permute-done((bf16[128,2048]{1,0:T(8,128)(2,1)S(1)}, bf16[128,2048]{1,0:T(8,128)(2,1)S(1)}, u32[]{:S(2)}, u32[]{:S(2)}) %collective-permute-start.19) | collective-permute-done | bytes 524320 | tf_op jit(solution)/shard_map/ppermute | solution.py:276
  101.3 2.3 %collective-permute-start.22 = (f32[384,256]{1,0:T(8,128)S(1)}, f32[384,256]{1,0:T(8,128)S(1)}, u32[]{:S(2)}, u32[]{:S(2)}) collective-permute-start(f32[384,256]{1,0:T(8,128)S(1)} %get-tuple-element.918), channel_id=1, source_target_pairs={{0,1},{1,0},{2,3},{3,2},{4,5},{5,4},{6,7},{7,6},{8,9},{9,8},{10,11... | collective-permute-start | bytes 1179656 | tf_op jit(solution)/shard_map/ppermute | solution.py:262
  103.7 1.8 %shard_map.48 = f32[512,3584]{1,0:T(8,128)S(1)} custom-call(bf16[512,2048]{1,0:T(8,128)(2,1)S(1)} %get-tuple-element.1003.handed_ref, bf16[128,2048]{1,0:T(8,128)(2,1)S(1)} %collective-permute-done.16.received_ref.refs_0_.refs_7_, bf16[128,2048]{1,0:T(8,128)(2,1)S(1)} %collective-permute-done.19.received_ref.refs_1_.refs_8_, ...), custom_call_target="tpu_custom_call", output_to_operand_aliasing={{}: (7, {})} | custom-call | flops 1 | bytes 1 | tf_op jit(solution)/shard_map/pallas_call | solution.py:118
  106.7 4.6 %collective-permute-done.24.refs_1_.refs_6_ = bf16[128,2048]{1,0:T(8,128)(2,1)S(1)} collective-permute-done((bf16[128,2048]{1,0:T(8,128)(2,1)S(1)}, bf16[128,2048]{1,0:T(8,128)(2,1)S(1)}, u32[]{:S(2)}, u32[]{:S(2)}) %collective-permute-start.24) | collective-permute-done | bytes 524320 | tf_op jit(solution)/shard_map/ppermute | solution.py:280
  111.3 2.1 %collective-permute-start.29 = (f32[512,3584]{1,0:T(8,128)S(1)}, f32[512,3584]{1,0:T(8,128)S(1)}, u32[]{:S(2)}, u32[]{:S(2)}) collective-permute-start(f32[512,3584]{1,0:T(8,128)S(1)} %shard_map.48), channel_id=1, source_target_pairs={{0,1},{1,0},{2,3},{3,2},{4,5},{5,4},{6,7},{7,6},{8,9},{9,8},{10,11... | collective-permute-start | bytes 22020104 | tf_op jit(solution)/shard_map/ppermute | solution.py:262
  113.4 7.7 %collective-permute-start.30 = (bf16[256,2048]{1,0:T(8,128)(2,1)S(1)}, bf16[256,2048]{1,0:T(8,128)(2,1)S(1)}, u32[]{:S(2)}, u32[]{:S(2)}) collective-permute-start(bf16[256,2048]{1,0:T(8,128)(2,1)S(1)} %pad_maximum_fusion), channel_id=1, source_target_pairs={{0,126},{2,0},{4,2},{6,4},{8,6},{10,8},{12,10},{14,12},{16,14},{18... | collective-permute-start | bytes 3145736 | tf_op jit(solution)/shard_map/ppermute | solution.py:357
  121.1 2.4 %shard_map.49 = (f32[128,768]{1,0:T(8,128)S(1)}, f32[128,768]{1,0:T(8,128)S(1)}) custom-call(s32[1]{0:T(128)} %bitcast.2._.where_ref, bf16[128,2048]{1,0:T(8,128)(2,1)S(1)} %collective-permute-done.3.refs_4_.refs_0_.refs_6_, bf16[128,2048]{1,0:T(8,128)(2,1)S(1)} %collective-permute-done.6.refs_5_.refs_1_.refs_7_, ...), custom_call_target="tpu_custom_call" | custom-call | flops 1 | bytes 1 | tf_op jit(solution)/shard_map/pallas_call | solution.py:207
  125.9 2.6 %shard_map.52 = f32[256,768]{1,0:T(8,128)S(1)} custom-call(s32[1]{0:T(128)} %bitcast.2._.where_ref, bf16[128,2048]{1,0:T(8,128)(2,1)S(1)} %collective-permute-done.3.refs_4_.refs_0_.refs_6_, bf16[128,2048]{1,0:T(8,128)(2,1)S(1)} %collective-permute-done.6.refs_5_.refs_1_.refs_7_, bf16[128,2048]{1,0:T(8,128)(2,1)S(1)} %collective-permute-done.9.refs_2_.refs_3_, ...), custom_call_target="tpu_custom_call" | custom-call | flops 1 | bytes 1 | tf_op jit(solution)/shard_map/pallas_call | solution.py:207
  129.5 7.0 %shard_map.53.refs_13_ = f32[5,512,1024]{2,1,0:T(8,128)} custom-call(f32[5]{0:T(128)S(1)} %pad_maximum_fusion.1.weights_ref, bf16[512,2048]{1,0:T(8,128)(2,1)S(1)} %get-tuple-element.1000.kept_ref, f32[512,3584]{1,0:T(8,128)S(1)} %collective-permute-done.29.refs_0_, bf16[1024,2048]{1,0:T(8,128)(2,1)S(1)} %copy-done.1, ...), custom_call_target="tpu_custom_call" | custom-call | flops 1 | bytes 1 | tf_op jit(solution)/shard_map/pallas_call | solution.py:161
  136.5 5.2 %shard_map.54._ = f32[5,512,1024]{2,1,0:T(8,128)} custom-call(f32[5]{0:T(128)S(1)} %pad_maximum_fusion.1.weights_ref, bf16[512,2048]{1,0:T(8,128)(2,1)S(1)} %get-tuple-element.1000.kept_ref, f32[512,3584]{1,0:T(8,128)S(1)} %collective-permute-done.29.refs_0_, ...), custom_call_target="tpu_custom_call", output_to_operand_aliasing={{}: (15, {})} | custom-call | flops 1 | bytes 1 | tf_op jit(solution)/shard_map/pallas_call | solution.py:161
  141.7 3.7 %collective-permute-done.31.summed_ref = f32[384,512]{1,0:T(8,128)S(1)} collective-permute-done((f32[384,512]{1,0:T(8,128)S(1)}, f32[384,512]{1,0:T(8,128)S(1)}, u32[]{:S(2)}, u32[]{:S(2)}) %collective-permute-start.31) | collective-permute-done | bytes 786464 | tf_op jit(solution)/shard_map/ppermute | solution.py:356
  146.2 1.9 %collective-permute-start.34 = (f32[512,256]{1,0:T(8,128)S(1)}, f32[512,256]{1,0:T(8,128)S(1)}, u32[]{:S(2)}, u32[]{:S(2)}) collective-permute-start(f32[512,256]{1,0:T(8,128)S(1)} %shard_map.55), channel_id=1, source_target_pairs={{0,1},{1,0},{2,3},{3,2},{4,5},{5,4},{6,7},{7,6},{8,9},{9,8},{10,11... | collective-permute-start | bytes 1572872 | tf_op jit(solution)/shard_map/ppermute | solution.py:262
  151.1 3.4 %shard_map.57._ = f32[5,512,1024]{2,1,0:T(8,128)} custom-call(f32[5]{0:T(128)S(1)} %pad_maximum_fusion.1.weights_ref, bf16[512,2048]{1,0:T(8,128)(2,1)S(1)} %get-tuple-element.1000.kept_ref, f32[512,256]{1,0:T(8,128)S(1)} %collective-permute-done.32.refs_0_, f32[512,256]{1,0:T(8,128)S(1)} %collective-permute-done.33.refs_1_, ...), custom_call_target="tpu_custom_call", output_to_operand_aliasing={{}: (10, {})} | custom-call | flops 1 | bytes 1 | tf_op jit(solution)/shard_map/pallas_call | solution.py:161
  154.5 7.8 %collective-permute-done.28.summed_ref = f32[256,768]{1,0:T(8,128)S(1)} collective-permute-done((f32[256,768]{1,0:T(8,128)S(1)}, f32[256,768]{1,0:T(8,128)S(1)}, u32[]{:S(2)}, u32[]{:S(2)}) %collective-permute-start.28) | collective-permute-done | bytes 786464 | tf_op jit(solution)/shard_map/ppermute | solution.py:359
  (80 shorter events, 34.3 us)
Async XLA Ops:
  1.1 17.4 %collective-permute-start = (bf16[128,2048]{1,0:T(8,128)(2,1)S(1)}, bf16[128,2048]{1,0:T(8,128)(2,1)S(1)}, u32[]{:S(2)}, u32[]{:S(2)}) collective-permute-start(bf16[128,2048]{1,0:T(8,128)(2,1)S(1)} %slice.3.mine_ref), channel_id=1, source_target_pairs={{0,120},{2,122},{4,124},{6,126},{8,0},{10,2},{12,4},{14,6},{16,8},... | collective-permute-start | bytes 1572872 | tf_op jit(solution)/shard_map/ppermute | solution.py:276
  10.2 19.6 %collective-permute-start.1 = (bf16[128,2048]{1,0:T(8,128)(2,1)S(1)}, bf16[128,2048]{1,0:T(8,128)(2,1)S(1)}, u32[]{:S(2)}, u32[]{:S(2)}) collective-permute-start(bf16[128,2048]{1,0:T(8,128)(2,1)S(1)} %shard_map.28.mine_ref), channel_id=1, source_target_pairs={{0,120},{2,122},{4,124},{6,126},{8,0},{10,2},{12,4},{14,6},{16,8},... | collective-permute-start | bytes 1572872 | tf_op jit(solution)/shard_map/ppermute | solution.py:276
  18.6 14.1 %collective-permute-start.2 = (bf16[128,2048]{1,0:T(8,128)(2,1)S(1)}, bf16[128,2048]{1,0:T(8,128)(2,1)S(1)}, u32[]{:S(2)}, u32[]{:S(2)}) collective-permute-start(bf16[128,2048]{1,0:T(8,128)(2,1)S(1)} %get-tuple-element.522), channel_id=1, source_target_pairs={{0,2},{2,4},{4,6},{6,0},{8,10},{10,12},{12,14},{14,8},{16,18},{18,... | collective-permute-start | bytes 1572872 | tf_op jit(solution)/shard_map/ppermute | solution.py:280
  20.0 12.8 %collective-permute-start.3 = (bf16[128,2048]{1,0:T(8,128)(2,1)S(1)}, bf16[128,2048]{1,0:T(8,128)(2,1)S(1)}, u32[]{:S(2)}, u32[]{:S(2)}) collective-permute-start(bf16[128,2048]{1,0:T(8,128)(2,1)S(1)} %get-tuple-element.532), channel_id=1, source_target_pairs={{0,6},{2,0},{4,2},{6,4},{8,14},{10,8},{12,10},{14,12},{16,22},{18,... | collective-permute-start | bytes 1572872 | tf_op jit(solution)/shard_map/ppermute | solution.py:281
  21.6 19.8 %collective-permute-start.4 = (bf16[128,2048]{1,0:T(8,128)(2,1)S(1)}, bf16[128,2048]{1,0:T(8,128)(2,1)S(1)}, u32[]{:S(2)}, u32[]{:S(2)}) collective-permute-start(bf16[128,2048]{1,0:T(8,128)(2,1)S(1)} %shard_map.29.mine_ref), channel_id=1, source_target_pairs={{0,120},{2,122},{4,124},{6,126},{8,0},{10,2},{12,4},{14,6},{16,8},... | collective-permute-start | bytes 1572872 | tf_op jit(solution)/shard_map/ppermute | solution.py:276
  29.9 14.4 %collective-permute-start.5 = (bf16[128,2048]{1,0:T(8,128)(2,1)S(1)}, bf16[128,2048]{1,0:T(8,128)(2,1)S(1)}, u32[]{:S(2)}, u32[]{:S(2)}) collective-permute-start(bf16[128,2048]{1,0:T(8,128)(2,1)S(1)} %get-tuple-element.557), channel_id=1, source_target_pairs={{0,2},{2,4},{4,6},{6,0},{8,10},{10,12},{12,14},{14,8},{16,18},{18,... | collective-permute-start | bytes 1572872 | tf_op jit(solution)/shard_map/ppermute | solution.py:280
  31.2 13.0 %collective-permute-start.6 = (bf16[128,2048]{1,0:T(8,128)(2,1)S(1)}, bf16[128,2048]{1,0:T(8,128)(2,1)S(1)}, u32[]{:S(2)}, u32[]{:S(2)}) collective-permute-start(bf16[128,2048]{1,0:T(8,128)(2,1)S(1)} %get-tuple-element.571), channel_id=1, source_target_pairs={{0,6},{2,0},{4,2},{6,4},{8,14},{10,8},{12,10},{14,12},{16,22},{18,... | collective-permute-start | bytes 1572872 | tf_op jit(solution)/shard_map/ppermute | solution.py:281
  32.8 19.4 %collective-permute-start.7 = (bf16[128,2048]{1,0:T(8,128)(2,1)S(1)}, bf16[128,2048]{1,0:T(8,128)(2,1)S(1)}, u32[]{:S(2)}, u32[]{:S(2)}) collective-permute-start(bf16[128,2048]{1,0:T(8,128)(2,1)S(1)} %shard_map.31.mine_ref), channel_id=1, source_target_pairs={{0,120},{2,122},{4,124},{6,126},{8,0},{10,2},{12,4},{14,6},{16,8},... | collective-permute-start | bytes 1572872 | tf_op jit(solution)/shard_map/ppermute | solution.py:276
  41.5 13.7 %collective-permute-start.8 = (bf16[128,2048]{1,0:T(8,128)(2,1)S(1)}, bf16[128,2048]{1,0:T(8,128)(2,1)S(1)}, u32[]{:S(2)}, u32[]{:S(2)}) collective-permute-start(bf16[128,2048]{1,0:T(8,128)(2,1)S(1)} %get-tuple-element.607), channel_id=1, source_target_pairs={{0,2},{2,4},{4,6},{6,0},{8,10},{10,12},{12,14},{14,8},{16,18},{18,... | collective-permute-start | bytes 1572872 | tf_op jit(solution)/shard_map/ppermute | solution.py:280
  42.5 12.8 %collective-permute-start.9 = (bf16[128,2048]{1,0:T(8,128)(2,1)S(1)}, bf16[128,2048]{1,0:T(8,128)(2,1)S(1)}, u32[]{:S(2)}, u32[]{:S(2)}) collective-permute-start(bf16[128,2048]{1,0:T(8,128)(2,1)S(1)} %get-tuple-element.624), channel_id=1, source_target_pairs={{0,6},{2,0},{4,2},{6,4},{8,14},{10,8},{12,10},{14,12},{16,22},{18,... | collective-permute-start | bytes 1572872 | tf_op jit(solution)/shard_map/ppermute | solution.py:281
  44.3 19.1 %collective-permute-start.10 = (bf16[128,2048]{1,0:T(8,128)(2,1)S(1)}, bf16[128,2048]{1,0:T(8,128)(2,1)S(1)}, u32[]{:S(2)}, u32[]{:S(2)}) collective-permute-start(bf16[128,2048]{1,0:T(8,128)(2,1)S(1)} %shard_map.34.mine_ref), channel_id=1, source_target_pairs={{0,120},{2,122},{4,124},{6,126},{8,0},{10,2},{12,4},{14,6},{16,8},... | collective-permute-start | bytes 1572872 | tf_op jit(solution)/shard_map/ppermute | solution.py:276
  52.3 14.1 %collective-permute-start.11 = (bf16[128,2048]{1,0:T(8,128)(2,1)S(1)}, bf16[128,2048]{1,0:T(8,128)(2,1)S(1)}, u32[]{:S(2)}, u32[]{:S(2)}) collective-permute-start(bf16[128,2048]{1,0:T(8,128)(2,1)S(1)} %get-tuple-element.665), channel_id=1, source_target_pairs={{0,2},{2,4},{4,6},{6,0},{8,10},{10,12},{12,14},{14,8},{16,18},{18,... | collective-permute-start | bytes 1572872 | tf_op jit(solution)/shard_map/ppermute | solution.py:280
  53.7 12.8 %collective-permute-start.12 = (bf16[128,2048]{1,0:T(8,128)(2,1)S(1)}, bf16[128,2048]{1,0:T(8,128)(2,1)S(1)}, u32[]{:S(2)}, u32[]{:S(2)}) collective-permute-start(bf16[128,2048]{1,0:T(8,128)(2,1)S(1)} %get-tuple-element.680), channel_id=1, source_target_pairs={{0,6},{2,0},{4,2},{6,4},{8,14},{10,8},{12,10},{14,12},{16,22},{18,... | collective-permute-start | bytes 1572872 | tf_op jit(solution)/shard_map/ppermute | solution.py:281
  55.3 19.4 %collective-permute-start.13 = (bf16[128,2048]{1,0:T(8,128)(2,1)S(1)}, bf16[128,2048]{1,0:T(8,128)(2,1)S(1)}, u32[]{:S(2)}, u32[]{:S(2)}) collective-permute-start(bf16[128,2048]{1,0:T(8,128)(2,1)S(1)} %shard_map.36.mine_ref), channel_id=1, source_target_pairs={{0,120},{2,122},{4,124},{6,126},{8,0},{10,2},{12,4},{14,6},{16,8},... | collective-permute-start | bytes 1572872 | tf_op jit(solution)/shard_map/ppermute | solution.py:276
  63.6 12.6 %collective-permute-start.14 = (bf16[128,2048]{1,0:T(8,128)(2,1)S(1)}, bf16[128,2048]{1,0:T(8,128)(2,1)S(1)}, u32[]{:S(2)}, u32[]{:S(2)}) collective-permute-start(bf16[128,2048]{1,0:T(8,128)(2,1)S(1)} %get-tuple-element.724), channel_id=1, source_target_pairs={{0,2},{2,4},{4,6},{6,0},{8,10},{10,12},{12,14},{14,8},{16,18},{18,... | collective-permute-start | bytes 1572872 | tf_op jit(solution)/shard_map/ppermute | solution.py:280
  64.9 12.8 %collective-permute-start.15 = (bf16[128,2048]{1,0:T(8,128)(2,1)S(1)}, bf16[128,2048]{1,0:T(8,128)(2,1)S(1)}, u32[]{:S(2)}, u32[]{:S(2)}) collective-permute-start(bf16[128,2048]{1,0:T(8,128)(2,1)S(1)} %get-tuple-element.741), channel_id=1, source_target_pairs={{0,6},{2,0},{4,2},{6,4},{8,14},{10,8},{12,10},{14,12},{16,22},{18,... | collective-permute-start | bytes 1572872 | tf_op jit(solution)/shard_map/ppermute | solution.py:281
  66.5 19.4 %collective-permute-start.16 = (bf16[128,2048]{1,0:T(8,128)(2,1)S(1)}, bf16[128,2048]{1,0:T(8,128)(2,1)S(1)}, u32[]{:S(2)}, u32[]{:S(2)}) collective-permute-start(bf16[128,2048]{1,0:T(8,128)(2,1)S(1)} %shard_map.39.mine_ref), channel_id=1, source_target_pairs={{0,120},{2,122},{4,124},{6,126},{8,0},{10,2},{12,4},{14,6},{16,8},... | collective-permute-start | bytes 1572872 | tf_op jit(solution)/shard_map/ppermute | solution.py:276
  74.8 14.1 %collective-permute-start.17 = (bf16[128,2048]{1,0:T(8,128)(2,1)S(1)}, bf16[128,2048]{1,0:T(8,128)(2,1)S(1)}, u32[]{:S(2)}, u32[]{:S(2)}) collective-permute-start(bf16[128,2048]{1,0:T(8,128)(2,1)S(1)} %get-tuple-element.792), channel_id=1, source_target_pairs={{0,2},{2,4},{4,6},{6,0},{8,10},{10,12},{12,14},{14,8},{16,18},{18,... | collective-permute-start | bytes 1572872 | tf_op jit(solution)/shard_map/ppermute | solution.py:280
  76.2 12.8 %collective-permute-start.18 = (bf16[128,2048]{1,0:T(8,128)(2,1)S(1)}, bf16[128,2048]{1,0:T(8,128)(2,1)S(1)}, u32[]{:S(2)}, u32[]{:S(2)}) collective-permute-start(bf16[128,2048]{1,0:T(8,128)(2,1)S(1)} %get-tuple-element.811), channel_id=1, source_target_pairs={{0,6},{2,0},{4,2},{6,4},{8,14},{10,8},{12,10},{14,12},{16,22},{18,... | collective-permute-start | bytes 1572872 | tf_op jit(solution)/shard_map/ppermute | solution.py:281
  77.8 19.4 %collective-permute-start.19 = (bf16[128,2048]{1,0:T(8,128)(2,1)S(1)}, bf16[128,2048]{1,0:T(8,128)(2,1)S(1)}, u32[]{:S(2)}, u32[]{:S(2)}) collective-permute-start(bf16[128,2048]{1,0:T(8,128)(2,1)S(1)} %shard_map.41.mine_ref), channel_id=1, source_target_pairs={{0,120},{2,122},{4,124},{6,126},{8,0},{10,2},{12,4},{14,6},{16,8},... | collective-permute-start | bytes 1572872 | tf_op jit(solution)/shard_map/ppermute | solution.py:276
  86.1 14.1 %collective-permute-start.20 = (bf16[128,2048]{1,0:T(8,128)(2,1)S(1)}, bf16[128,2048]{1,0:T(8,128)(2,1)S(1)}, u32[]{:S(2)}, u32[]{:S(2)}) collective-permute-start(bf16[128,2048]{1,0:T(8,128)(2,1)S(1)} %get-tuple-element.868), channel_id=1, source_target_pairs={{0,2},{2,4},{4,6},{6,0},{8,10},{10,12},{12,14},{14,8},{16,18},{18,... | collective-permute-start | bytes 1572872 | tf_op jit(solution)/shard_map/ppermute | solution.py:280
  87.4 12.8 %collective-permute-start.21 = (bf16[128,2048]{1,0:T(8,128)(2,1)S(1)}, bf16[128,2048]{1,0:T(8,128)(2,1)S(1)}, u32[]{:S(2)}, u32[]{:S(2)}) collective-permute-start(bf16[128,2048]{1,0:T(8,128)(2,1)S(1)} %get-tuple-element.888), channel_id=1, source_target_pairs={{0,6},{2,0},{4,2},{6,4},{8,14},{10,8},{12,10},{14,12},{16,22},{18,... | collective-permute-start | bytes 1572872 | tf_op jit(solution)/shard_map/ppermute | solution.py:281
  97.3 14.0 %collective-permute-start.24 = (bf16[128,2048]{1,0:T(8,128)(2,1)S(1)}, bf16[128,2048]{1,0:T(8,128)(2,1)S(1)}, u32[]{:S(2)}, u32[]{:S(2)}) collective-permute-start(bf16[128,2048]{1,0:T(8,128)(2,1)S(1)} %get-tuple-element.925), channel_id=1, source_target_pairs={{0,2},{2,4},{4,6},{6,0},{8,10},{10,12},{12,14},{14,8},{16,18},{18,... | collective-permute-start | bytes 1572872 | tf_op jit(solution)/shard_map/ppermute | solution.py:280
  98.6 12.6 %collective-permute-start.25 = (bf16[128,2048]{1,0:T(8,128)(2,1)S(1)}, bf16[128,2048]{1,0:T(8,128)(2,1)S(1)}, u32[]{:S(2)}, u32[]{:S(2)}) collective-permute-start(bf16[128,2048]{1,0:T(8,128)(2,1)S(1)} %get-tuple-element.945), channel_id=1, source_target_pairs={{0,6},{2,0},{4,2},{6,4},{8,14},{10,8},{12,10},{14,12},{16,22},{18,... | collective-permute-start | bytes 1572872 | tf_op jit(solution)/shard_map/ppermute | solution.py:281
  101.3 4.2 %collective-permute-start.22 = (f32[384,256]{1,0:T(8,128)S(1)}, f32[384,256]{1,0:T(8,128)S(1)}, u32[]{:S(2)}, u32[]{:S(2)}) collective-permute-start(f32[384,256]{1,0:T(8,128)S(1)} %get-tuple-element.918), channel_id=1, source_target_pairs={{0,1},{1,0},{2,3},{3,2},{4,5},{5,4},{6,7},{7,6},{8,9},{9,8},{10,11... | collective-permute-start | bytes 1179656 | tf_op jit(solution)/shard_map/ppermute | solution.py:262
  111.3 18.2 %collective-permute-start.29 = (f32[512,3584]{1,0:T(8,128)S(1)}, f32[512,3584]{1,0:T(8,128)S(1)}, u32[]{:S(2)}, u32[]{:S(2)}) collective-permute-start(f32[512,3584]{1,0:T(8,128)S(1)} %shard_map.48), channel_id=1, source_target_pairs={{0,1},{1,0},{2,3},{3,2},{4,5},{5,4},{6,7},{7,6},{8,9},{9,8},{10,11... | collective-permute-start | bytes 22020104 | tf_op jit(solution)/shard_map/ppermute | solution.py:262
  113.4 32.0 %collective-permute-start.30 = (bf16[256,2048]{1,0:T(8,128)(2,1)S(1)}, bf16[256,2048]{1,0:T(8,128)(2,1)S(1)}, u32[]{:S(2)}, u32[]{:S(2)}) collective-permute-start(bf16[256,2048]{1,0:T(8,128)(2,1)S(1)} %pad_maximum_fusion), channel_id=1, source_target_pairs={{0,126},{2,0},{4,2},{6,4},{8,6},{10,8},{12,10},{14,12},{16,14},{18... | collective-permute-start | bytes 3145736 | tf_op jit(solution)/shard_map/ppermute | solution.py:357
  121.1 24.3 %collective-permute-start.31 = (f32[384,512]{1,0:T(8,128)S(1)}, f32[384,512]{1,0:T(8,128)S(1)}, u32[]{:S(2)}, u32[]{:S(2)}) collective-permute-start(f32[384,512]{1,0:T(8,128)S(1)} %shard_map.46), channel_id=1, source_target_pairs={{0,2},{2,4},{4,6},{6,8},{8,10},{10,12},{12,14},{14,16},{16,18},{18... | collective-permute-start | bytes 2359304 | tf_op jit(solution)/shard_map/ppermute | solution.py:356
  128.5 33.8 %collective-permute-start.28 = (f32[256,768]{1,0:T(8,128)S(1)}, f32[256,768]{1,0:T(8,128)S(1)}, u32[]{:S(2)}, u32[]{:S(2)}) collective-permute-start(f32[256,768]{1,0:T(8,128)S(1)} %shard_map.52), channel_id=1, source_target_pairs={{0,2},{2,4},{4,6},{6,8},{8,10},{10,12},{12,14},{14,16},{16,18},{18... | collective-permute-start | bytes 2359304 | tf_op jit(solution)/shard_map/ppermute | solution.py:359
  146.2 3.9 %collective-permute-start.34 = (f32[512,256]{1,0:T(8,128)S(1)}, f32[512,256]{1,0:T(8,128)S(1)}, u32[]{:S(2)}, u32[]{:S(2)}) collective-permute-start(f32[512,256]{1,0:T(8,128)S(1)} %shard_map.55), channel_id=1, source_target_pairs={{0,1},{1,0},{2,3},{3,2},{4,5},{5,4},{6,7},{7,6},{8,9},{9,8},{10,11... | collective-permute-start | bytes 1572872 | tf_op jit(solution)/shard_map/ppermute | solution.py:262
  148.1 2.3 %collective-permute-start.32 = (f32[512,256]{1,0:T(8,128)S(1)}, f32[512,256]{1,0:T(8,128)S(1)}, u32[]{:S(2)}, u32[]{:S(2)}) collective-permute-start(f32[512,256]{1,0:T(8,128)S(1)} %shard_map.50), channel_id=1, source_target_pairs={{0,1},{1,0},{2,3},{3,2},{4,5},{5,4},{6,7},{7,6},{8,9},{9,8},{10,11... | collective-permute-start | bytes 1572872 | tf_op jit(solution)/shard_map/ppermute | solution.py:262
  148.2 2.9 %collective-permute-start.33 = (f32[512,256]{1,0:T(8,128)S(1)}, f32[512,256]{1,0:T(8,128)S(1)}, u32[]{:S(2)}, u32[]{:S(2)}) collective-permute-start(f32[512,256]{1,0:T(8,128)S(1)} %shard_map.51), channel_id=1, source_target_pairs={{0,1},{1,0},{2,3},{3,2},{4,5},{5,4},{6,7},{7,6},{8,9},{9,8},{10,11... | collective-permute-start | bytes 1572872 | tf_op jit(solution)/shard_map/ppermute | solution.py:262
  (6 other events, 24.4 us)
